TPU v7x, 128 devices: a whole 4x4x4 slice. The times are simulated.
128 devices in a mesh: lat: 8 (over y, core), lon: 16 (over x, z).
Axes of the slice: x: 4, y: 4, z: 4, core: 2. Of those that a mesh axis runs over, the one named last changes fastest.
Arguments:
- probes: float32 [128, 256, 4096], P(None, 'lat', 'lon'), may hold values from -6 to 6
- kappa: float32 [256, 4096], P('lat', 'lon'), may hold values from 0.12 to 0.24
- sweep_counts: int32 [256], P('lat'), may hold values from 1 to 4
- obs_cell: int32 [49152], P(('lat', 'lon')), may hold values from 0 to 8191
- obs_owner: int32 [49152, 1], P(('lat', 'lon')), may hold values from 0 to 15; in each aligned block of 384 rows (0 to 383, 384 to 767, ...) at most 48 rows name the same one
- obs_count: int32 [8, 16], P('lat', 'lon'), may hold values from 288 to 384
- r_inv: float32 [8, 16, 768, 768], P('lat', 'lon'), may hold values from -8 to 32
Outputs:
- sketch: float32 [128, 256, 4096], P(None, 'lat', 'lon')
- r_factor: float32 [128, 128], replicated
All inputs are finite; a program needn't handle non-finite values.
Results may differ from a plain program's by a relative error of at most 0.00013.
Values sent between devices are 32-bit elements; how exact they have to be, the bound alone decides.
No kernel may reach another device: no remote copies, remote signals or barrier semaphores. Data moves between devices by JAX's collectives and lax.ppermute only.
A program may use at most 64 MiB of HBM per device.

v0:
```python
import jax
import jax.numpy as jnp
from jax import lax
from jax.sharding import PartitionSpec as P

SWEEPS = 4
CAP = 48


def extended(array, sides, width):
    for axis, dim in sides:
        size, length = (lax.axis_size(axis), array.shape[dim])
        up = [(i, (i + 1) % size) for i in range(size - 1)]
        down = [(j, i) for i, j in up]
        last = lax.slice_in_dim(array, length - width, length, axis=dim)
        initial = lax.slice_in_dim(array, 0, width, axis=dim)
        before = lax.ppermute(last, axis, up)
        after = lax.ppermute(initial, axis, down)
        array = jnp.concatenate([before, array, after], axis=dim)
    return array


def relax_once(padded, kappa_part, count_part, sweep_step):
    center = padded[:, 1:-1, 1:-1]
    laplace_sum = (
        padded[:, :-2, 1:-1]
        + padded[:, 2:, 1:-1]
        + padded[:, 1:-1, :-2]
        + padded[:, 1:-1, 2:]
        - 4.0 * center
    )
    active = (count_part > sweep_step)[:, None]
    return center + jnp.where(active, kappa_part * laplace_sum, 0.0)


def plain_sweeps(state_field, kappa, sweep_counts):
    for sweep_step in range(SWEEPS):
        padded = extended(state_field, (("lat", 1), ("lon", 2)), 1)
        state_field = relax_once(padded, kappa, sweep_counts, sweep_step)
    return state_field


def observe_term(state_field, obs_cell, obs_owner, obs_count, r_inv):
    k_probes, lat_rows, lon_cols = state_field.shape
    n_lon = lax.axis_size("lon")
    slot_ids = jnp.arange(obs_cell.shape[0], dtype=jnp.int32)
    is_live = slot_ids < obs_count[0, 0]
    owner_ids = obs_owner[:, 0]
    owner_hit = (
        (owner_ids[:, None] == jnp.arange(n_lon, dtype=jnp.int32)[None, :]) & is_live[:, None]
    ).astype(jnp.int32)
    slot_rank = jnp.sum(jnp.cumsum(owner_hit, axis=0) * owner_hit, axis=1) - 1
    send_slot = jnp.where(is_live, owner_ids * CAP + slot_rank, 0)
    flat_field = state_field.reshape(k_probes, lat_rows * lon_cols)
    picked = jnp.where(is_live[None, :], flat_field[:, obs_cell], 0.0)
    outgoing = jnp.zeros((k_probes, n_lon * CAP), jnp.float32).at[:, send_slot].add(picked)
    weights = r_inv[0, 0]
    mixed = jnp.dot(
        lax.all_to_all(outgoing, "lon", split_axis=1, concat_axis=1, tiled=True),
        weights,
        precision=lax.Precision.HIGHEST,
        preferred_element_type=jnp.float32,
    )
    returned = lax.all_to_all(mixed, "lon", split_axis=1, concat_axis=1, tiled=True)
    answered = jnp.where(is_live[None, :], returned[:, send_slot], 0.0)
    spread = jnp.zeros_like(flat_field).at[:, obs_cell].add(answered)
    return spread.reshape(state_field.shape)


def shards(probes, kappa, sweep_counts, obs_cell, obs_owner, obs_count, r_inv):
    k_probes, lat_rows, lon_cols = probes.shape
    smoothed = plain_sweeps(probes, kappa, sweep_counts)
    adjoint = observe_term(smoothed, obs_cell, obs_owner, obs_count, r_inv)
    sketch = probes + plain_sweeps(adjoint, kappa, sweep_counts)
    flat_sketch = sketch.reshape(k_probes, lat_rows * lon_cols)
    gram_local = jnp.dot(
        flat_sketch,
        flat_sketch.T,
        precision=lax.Precision.HIGHEST,
        preferred_element_type=jnp.float32,
    )
    gram_total = lax.psum(gram_local, ("lat", "lon"))
    cells_all = lat_rows * lon_cols * lax.axis_size("lat") * lax.axis_size("lon")
    r_factor = jnp.linalg.cholesky(gram_total / cells_all).T
    return (sketch, r_factor)


def solution(mesh):
    return jax.shard_map(
        shards,
        mesh=mesh,
        in_specs=(
            P(None, "lat", "lon"),
            P("lat", "lon"),
            P("lat"),
            P(("lat", "lon")),
            P(("lat", "lon"), None),
            P("lat", "lon"),
            P("lat", "lon", None, None),
        ),
        out_specs=(P(None, "lat", "lon"), P()),
        check_vma=False,
    )
```

profile of v0, /device:TPU:1, one launch (start us, length us, event | category | flops | bytes accessed | tf_op | source)
XLA Modules:
  0.0 465.6 jit_solution(6277622947983621271)
XLA Ops:
  8.9 4.6 collective-permute-start
  15.5 5.9 %copy.103 = f32[128,32,256]{0,1,2:T(8,128)} copy(f32[128,32,256]{2,1,0:T(8,128)} %param.7) | data formatting | bytes 8388608 | tf_op args[0]
  31.3 13.0 %fusion.54 = f32[128,32,256]{0,1,2:T(8,128)S(1)} fusion(f32[128,32,256]{0,1,2:T(8,128)} %copy.103, f32[128,34,1]{0,1,2:T(8,128)S(1)} %collective-permute-done.3, f32[128,1,256]{0,1,2:T(1,128)S(1)} %copy.47, f32[128,1,256]{0,1,2:T(1,128)S(1)} %copy.43, f32[128,34,1]{0,1,2:T(8,128)S(1)} %collective-permute-done.2, f32[32,256]{0,1:T(8,128)S(1)} %copy.41, ...), kind=kLoop, calls=%fused_computation.115 | loop fusion | flops 16777216 | bytes 8718368 | tf_op jit(solution)/shard_map/add | solution.py:33
  46.6 4.9 %collective-permute-start.4 = (f32[128,1,256]{2,0,1:T(8,128)S(1)}, f32[128,1,256]{2,0,1:T(8,128)S(1)}, u32[]{:S(2)}, u32[]{:S(2)}) collective-permute-start(f32[128,1,256]{2,0,1:T(8,128)S(1)} %copy.53), channel_id=1, source_target_pairs={{0,16},{16,32},{32,48},{48,64},{64,80},{80,96},{96,112},{1,17},{17... | collective-permute-start | bytes 393224 | tf_op jit(solution)/shard_map/ppermute | solution.py:17
  67.0 5.7 %fusion.47 = f32[128,32,256]{0,1,2:T(8,128)S(1)} fusion(f32[128,32,256]{0,1,2:T(8,128)S(1)} %copy-done.8, f32[128,34,1]{0,1,2:T(8,128)S(1)} %collective-permute-done.7, f32[128,1,256]{0,1,2:T(1,128)S(1)} %copy.56, f32[128,1,256]{0,1,2:T(1,128)S(1)} %copy.54, f32[128,34,1]{0,1,2:T(8,128)S(1)} %collective-permute-done.6, f32[32,256]{0,1:T(8,128)S(1)} %copy.41, ...), kind=kLoop, calls=%fused_computation.100 | loop fusion | flops 16777216 | bytes 8718368 | tf_op jit(solution)/shard_map/add | solution.py:33
  94.0 5.7 %fusion.40 = f32[128,32,256]{0,1,2:T(8,128)S(1)} fusion(f32[128,32,256]{0,1,2:T(8,128)S(1)} %copy-done.4, f32[128,34,1]{0,1,2:T(8,128)S(1)} %collective-permute-done.11, f32[128,1,256]{0,1,2:T(1,128)S(1)} %copy.62, f32[128,1,256]{0,1,2:T(1,128)S(1)} %copy.60, f32[128,34,1]{0,1,2:T(8,128)S(1)} %collective-permute-done.10, f32[32,256]{0,1:T(8,128)S(1)} %copy.41, ...), kind=kLoop, calls=%fused_computation.85 | loop fusion | flops 16777216 | bytes 8718368 | tf_op jit(solution)/shard_map/add | solution.py:33
  120.9 5.7 %fusion.33 = f32[128,32,256]{0,1,2:T(8,128)S(1)} fusion(f32[128,32,256]{0,1,2:T(8,128)S(1)} %copy-done.6, f32[128,34,1]{0,1,2:T(8,128)S(1)} %collective-permute-done.15, f32[128,1,256]{0,1,2:T(1,128)S(1)} %copy.68, f32[128,1,256]{0,1,2:T(1,128)S(1)} %copy.66, f32[128,34,1]{0,1,2:T(8,128)S(1)} %collective-permute-done.14, f32[32,256]{0,1:T(8,128)S(1)} %copy.41, ...), kind=kLoop, calls=%fused_computation.70 | loop fusion | flops 16777216 | bytes 8718368 | tf_op jit(solution)/shard_map/add | solution.py:33
  131.0 5.3 %scatter_custom_fusion = f32[128,768]{0,1:T(8,128)} fusion(s32[384]{0:T(512)S(1)} %fusion.73, f32[]{:T(128)} %constant.55.clone.1, pred[384]{0:T(512)(128)(4,1)S(1)} %iota_compare_fusion.4, f32[128,8192]{0,1:T(8,128)} %bitcast.47, s32[1024]{0:T(1024)S(1)} %pad_clamp_fusion.1), kind=kCustom, calls=%fused_computation.129 | custom fusion | flops 98304 | bytes 4593152 | tf_op jit(solution)/shard_map/scatter-add | solution.py:56
  136.3 8.3 %all-to-all-start = ((f32[128,16,48]{0,2,1:T(8,128)}), f32[128,16,48]{0,2,1:T(8,128)S(1)}, u32[]{:S(2)}, u32[]{:S(2)}) async-start(f32[128,16,48]{0,2,1:T(8,128)} %bitcast.3), calls=%async_computation | async-start | bytes 786432 | tf_op jit(solution)/shard_map/all_to_all | solution.py:59
  146.7 6.7 %all-to-all-done = f32[128,16,48]{0,2,1:T(8,128)S(1)} async-done(((f32[128,16,48]{0,2,1:T(8,128)}), f32[128,16,48]{0,2,1:T(8,128)S(1)}, u32[]{:S(2)}, u32[]{:S(2)}) %all-to-all-start) | async-done | bytes 393248 | tf_op jit(solution)/shard_map/all_to_all | solution.py:59
  159.8 9.5 %all-to-all-done.1 = f32[128,16,48]{0,2,1:T(8,128)S(1)} async-done(((f32[128,16,48]{0,2,1:T(8,128)}), f32[128,16,48]{0,2,1:T(8,128)S(1)}, u32[]{:S(2)}, u32[]{:S(2)}) %all-to-all-start.1) | async-done | bytes 393248 | tf_op jit(solution)/shard_map/all_to_all | solution.py:64
  169.3 5.5 %scatter_custom_fusion.1 = f32[128,8192]{0,1:T(8,128)} fusion(s32[384]{0:T(512)S(1)} %compare_select_fusion.2, f32[]{:T(128)} %constant.55.clone.1, pred[384]{0:T(512)(128)(4,1)S(1)} %iota_compare_fusion.4, f32[128,768]{0,1:T(8,128)S(1)} %bitcast.49, s32[1024]{0:T(1024)S(1)} %pad_clamp_fusion), kind=kCustom, calls=%fused_computation.125 | custom fusion | flops 98304 | bytes 4593152 | tf_op jit(solution)/shard_map/scatter-add | solution.py:66
  175.8 4.8 %collective-permute-start.16 = (f32[128,1,256]{2,0,1:T(8,128)S(1)}, f32[128,1,256]{2,0,1:T(8,128)S(1)}, u32[]{:S(2)}, u32[]{:S(2)}) collective-permute-start(f32[128,1,256]{2,0,1:T(8,128)S(1)} %copy.118), channel_id=1, source_target_pairs={{0,16},{16,32},{32,48},{48,64},{64,80},{80,96},{96,112},{1,17},{17... | collective-permute-start | bytes 393224 | tf_op jit(solution)/shard_map/ppermute | solution.py:17
  182.8 6.7 %copy.84 = f32[128,32,256]{0,1,2:T(8,128)} copy(f32[128,32,256]{0,2,1:T(8,128)} %bitcast.46) | data formatting | bytes 8388608 | tf_op jit(solution)/shard_map/reshape | solution.py:67
  197.2 5.7 %fusion.26 = f32[128,32,256]{0,1,2:T(8,128)S(1)} fusion(f32[128,32,256]{0,1,2:T(8,128)S(1)} %copy-done.13, f32[128,34,1]{0,1,2:T(8,128)S(1)} %collective-permute-done.19, f32[128,1,256]{0,1,2:T(1,128)S(1)} %copy.79, f32[128,1,256]{0,1,2:T(1,128)S(1)} %copy.75, f32[128,34,1]{0,1,2:T(8,128)S(1)} %collective-permute-done.18, f32[32,256]{0,1:T(8,128)S(1)} %copy.41, ...), kind=kLoop, calls=%fused_computation.55 | loop fusion | flops 16777216 | bytes 8718368 | tf_op jit(solution)/shard_map/add | solution.py:33
  205.1 5.1 %collective-permute-start.20 = (f32[128,1,256]{2,0,1:T(8,128)S(1)}, f32[128,1,256]{2,0,1:T(8,128)S(1)}, u32[]{:S(2)}, u32[]{:S(2)}) collective-permute-start(f32[128,1,256]{2,0,1:T(8,128)S(1)} %copy.85), channel_id=1, source_target_pairs={{0,16},{16,32},{32,48},{48,64},{64,80},{80,96},{96,112},{1,17},{17... | collective-permute-start | bytes 393224 | tf_op jit(solution)/shard_map/ppermute | solution.py:17
  225.0 5.7 %fusion.19 = f32[128,32,256]{0,1,2:T(8,128)S(1)} fusion(f32[128,32,256]{0,1,2:T(8,128)S(1)} %copy-done.10, f32[128,34,1]{0,1,2:T(8,128)S(1)} %collective-permute-done.23, f32[128,1,256]{0,1,2:T(1,128)S(1)} %copy.88, f32[128,1,256]{0,1,2:T(1,128)S(1)} %copy.86, f32[128,34,1]{0,1,2:T(8,128)S(1)} %collective-permute-done.22, f32[32,256]{0,1:T(8,128)S(1)} %copy.41, ...), kind=kLoop, calls=%fused_computation.40 | loop fusion | flops 16777216 | bytes 8718368 | tf_op jit(solution)/shard_map/add | solution.py:33
  243.5 4.6 collective-permute-start.26
  253.0 5.7 %fusion.12 = f32[128,32,256]{0,1,2:T(8,128)S(1)} fusion(f32[128,32,256]{0,1,2:T(8,128)S(1)} %copy-done.12, f32[128,34,1]{0,1,2:T(8,128)S(1)} %collective-permute-done.27, f32[128,1,256]{0,1,2:T(1,128)S(1)} %copy.94, f32[128,1,256]{0,1,2:T(1,128)S(1)} %copy.92, f32[128,34,1]{0,1,2:T(8,128)S(1)} %collective-permute-done.26, f32[32,256]{0,1:T(8,128)S(1)} %copy.41, ...), kind=kLoop, calls=%fused_computation.25 | loop fusion | flops 16777216 | bytes 8718368 | tf_op jit(solution)/shard_map/add | solution.py:33
  277.9 13.0 %fusion.5 = f32[128,32,256]{0,1,2:T(8,128)S(1)} fusion(f32[128,32,256]{0,1,2:T(8,128)S(1)} %copy-done.1, f32[128,32,256]{0,1,2:T(8,128)} %copy-done.2, f32[128,34,1]{0,1,2:T(8,128)S(1)} %collective-permute-done.31, f32[128,1,256]{0,1,2:T(1,128)S(1)} %copy.100, f32[128,1,256]{0,1,2:T(1,128)S(1)} %copy.98, f32[128,34,1]{0,1,2:T(8,128)S(1)} %collective-permute-done.30, ...), kind=kLoop, calls=%fused_computation.10 | loop fusion | flops 17825792 | bytes 12912672 | tf_op jit(solution)/shard_map/add | solution.py:74
  292.9 7.6 %convolution_bitcast_fusion = f32[128,128]{0,1:T(8,128)} fusion(f32[128,32,256]{0,1,2:T(8,128)S(1)} %fusion.5), kind=kOutput, calls=%fused_computation.127 | convolution fusion | flops 1610612736 | bytes 4259840 | tf_op jit(solution)/shard_map/dot_general | solution.py:76
  300.5 5.8 %copy.108 = f32[128,32,256]{2,1,0:T(8,128)} copy(f32[128,32,256]{0,1,2:T(8,128)} %copy-done) | data formatting | bytes 8388608
  306.3 136.6 %all-reduce.2.cloned.1.call-done = f32[128,128]{0,1:T(8,128)} async-done(((f32[128,128]{0,1:T(8,128)}), f32[128,128]{0,1:T(8,128)}) %all-reduce.2.cloned.1.call-update) | async-done | bytes 65552 | tf_op jit(solution)/shard_map/psum | solution.py:82
  444.7 11.7 %cholesky.18 = f32[128,128]{1,0:T(8,128)S(1)} custom-call(f32[128,128]{1,0:T(8,128)S(1)} %fusion.67), custom_call_target="Cholesky" | custom-call | tf_op jit(solution)/shard_map/jit(cholesky)/cholesky | solution.py:84
  (171 shorter events, 156.2 us)
Async XLA Ops:
  8.9 13.2 %collective-permute-start = (f32[128,1,256]{2,0,1:T(8,128)S(1)}, f32[128,1,256]{2,0,1:T(8,128)S(1)}, u32[]{:S(2)}, u32[]{:S(2)}) collective-permute-start(f32[128,1,256]{2,0,1:T(8,128)S(1)} %copy.116), channel_id=1, source_target_pairs={{0,16},{16,32},{32,48},{48,64},{64,80},{80,96},{96,112},{1,17},{17... | collective-permute-start | bytes 393224 | tf_op jit(solution)/shard_map/ppermute | solution.py:17
  13.6 8.6 %collective-permute-start.1 = (f32[128,1,256]{2,0,1:T(8,128)S(1)}, f32[128,1,256]{2,0,1:T(8,128)S(1)}, u32[]{:S(2)}, u32[]{:S(2)}) collective-permute-start(f32[128,1,256]{2,0,1:T(8,128)S(1)} %copy.117), channel_id=1, source_target_pairs={{16,0},{32,16},{48,32},{64,48},{80,64},{96,80},{112,96},{17,1},{33... | collective-permute-start | bytes 393224 | tf_op jit(solution)/shard_map/ppermute | solution.py:18
  23.0 5.0 %collective-permute-start.2 = (f32[128,34,1]{0,1,2:T(8,128)S(1)}, f32[128,34,1]{0,1,2:T(8,128)S(1)}, u32[]{:S(2)}, u32[]{:S(2)}) collective-permute-start(f32[128,34,1]{0,1,2:T(8,128)S(1)} %get-tuple-element.22), channel_id=1, source_target_pairs={{0,1},{1,2},{2,3},{3,4},{4,5},{5,6},{6,7},{7,8},{8,9},{9,10},{10,1... | collective-permute-start | bytes 52232 | tf_op jit(solution)/shard_map/ppermute | solution.py:17
  46.6 7.8 %collective-permute-start.4 = (f32[128,1,256]{2,0,1:T(8,128)S(1)}, f32[128,1,256]{2,0,1:T(8,128)S(1)}, u32[]{:S(2)}, u32[]{:S(2)}) collective-permute-start(f32[128,1,256]{2,0,1:T(8,128)S(1)} %copy.53), channel_id=1, source_target_pairs={{0,16},{16,32},{32,48},{48,64},{64,80},{80,96},{96,112},{1,17},{17... | collective-permute-start | bytes 393224 | tf_op jit(solution)/shard_map/ppermute | solution.py:17
  51.5 6.3 %collective-permute-start.5 = (f32[128,1,256]{2,0,1:T(8,128)S(1)}, f32[128,1,256]{2,0,1:T(8,128)S(1)}, u32[]{:S(2)}, u32[]{:S(2)}) collective-permute-start(f32[128,1,256]{2,0,1:T(8,128)S(1)} %copy.55), channel_id=1, source_target_pairs={{16,0},{32,16},{48,32},{64,48},{80,64},{96,80},{112,96},{17,1},{33... | collective-permute-start | bytes 393224 | tf_op jit(solution)/shard_map/ppermute | solution.py:18
  58.8 5.2 %collective-permute-start.6 = (f32[128,34,1]{0,1,2:T(8,128)S(1)}, f32[128,34,1]{0,1,2:T(8,128)S(1)}, u32[]{:S(2)}, u32[]{:S(2)}) collective-permute-start(f32[128,34,1]{0,1,2:T(8,128)S(1)} %get-tuple-element.20), channel_id=1, source_target_pairs={{0,1},{1,2},{2,3},{3,4},{4,5},{5,6},{6,7},{7,8},{8,9},{9,10},{10,1... | collective-permute-start | bytes 52232 | tf_op jit(solution)/shard_map/ppermute | solution.py:17
  75.0 5.4 %collective-permute-start.8 = (f32[128,1,256]{2,0,1:T(8,128)S(1)}, f32[128,1,256]{2,0,1:T(8,128)S(1)}, u32[]{:S(2)}, u32[]{:S(2)}) collective-permute-start(f32[128,1,256]{2,0,1:T(8,128)S(1)} %copy.59), channel_id=1, source_target_pairs={{0,16},{16,32},{32,48},{48,64},{64,80},{80,96},{96,112},{1,17},{17... | collective-permute-start | bytes 393224 | tf_op jit(solution)/shard_map/ppermute | solution.py:17
  78.3 6.3 %collective-permute-start.9 = (f32[128,1,256]{2,0,1:T(8,128)S(1)}, f32[128,1,256]{2,0,1:T(8,128)S(1)}, u32[]{:S(2)}, u32[]{:S(2)}) collective-permute-start(f32[128,1,256]{2,0,1:T(8,128)S(1)} %copy.61), channel_id=1, source_target_pairs={{16,0},{32,16},{48,32},{64,48},{80,64},{96,80},{112,96},{17,1},{33... | collective-permute-start | bytes 393224 | tf_op jit(solution)/shard_map/ppermute | solution.py:18
  101.9 5.0 %collective-permute-start.12 = (f32[128,1,256]{2,0,1:T(8,128)S(1)}, f32[128,1,256]{2,0,1:T(8,128)S(1)}, u32[]{:S(2)}, u32[]{:S(2)}) collective-permute-start(f32[128,1,256]{2,0,1:T(8,128)S(1)} %copy.65), channel_id=1, source_target_pairs={{0,16},{16,32},{32,48},{48,64},{64,80},{80,96},{96,112},{1,17},{17... | collective-permute-start | bytes 393224 | tf_op jit(solution)/shard_map/ppermute | solution.py:17
  105.0 6.3 %collective-permute-start.13 = (f32[128,1,256]{2,0,1:T(8,128)S(1)}, f32[128,1,256]{2,0,1:T(8,128)S(1)}, u32[]{:S(2)}, u32[]{:S(2)}) collective-permute-start(f32[128,1,256]{2,0,1:T(8,128)S(1)} %copy.67), channel_id=1, source_target_pairs={{16,0},{32,16},{48,32},{64,48},{80,64},{96,80},{112,96},{17,1},{33... | collective-permute-start | bytes 393224 | tf_op jit(solution)/shard_map/ppermute | solution.py:18
  112.3 5.7 %collective-permute-start.14 = (f32[128,34,1]{0,1,2:T(8,128)S(1)}, f32[128,34,1]{0,1,2:T(8,128)S(1)}, u32[]{:S(2)}, u32[]{:S(2)}) collective-permute-start(f32[128,34,1]{0,1,2:T(8,128)S(1)} %get-tuple-element.16), channel_id=1, source_target_pairs={{0,1},{1,2},{2,3},{3,4},{4,5},{5,6},{6,7},{7,8},{8,9},{9,10},{10,1... | collective-permute-start | bytes 52232 | tf_op jit(solution)/shard_map/ppermute | solution.py:17
  136.3 17.1 %all-to-all-start = ((f32[128,16,48]{0,2,1:T(8,128)}), f32[128,16,48]{0,2,1:T(8,128)S(1)}, u32[]{:S(2)}, u32[]{:S(2)}) async-start(f32[128,16,48]{0,2,1:T(8,128)} %bitcast.3), calls=%async_computation | async-start | bytes 786432 | tf_op jit(solution)/shard_map/all_to_all | solution.py:59
  156.2 13.1 %all-to-all-start.1 = ((f32[128,16,48]{0,2,1:T(8,128)}), f32[128,16,48]{0,2,1:T(8,128)S(1)}, u32[]{:S(2)}, u32[]{:S(2)}) async-start(f32[128,16,48]{0,2,1:T(8,128)} %fusion.84), calls=%async_computation.1 | async-start | bytes 786432 | tf_op jit(solution)/shard_map/all_to_all | solution.py:64
  159.7 283.2 %all-reduce.2.cloned.1.call-start = ((), (), s32[]{:S(2)}) async-start(), calls=%async_computation.2 | async-start | bytes 131072 | tf_op jit(solution)/shard_map/psum | solution.py:82
  175.8 13.7 %collective-permute-start.16 = (f32[128,1,256]{2,0,1:T(8,128)S(1)}, f32[128,1,256]{2,0,1:T(8,128)S(1)}, u32[]{:S(2)}, u32[]{:S(2)}) collective-permute-start(f32[128,1,256]{2,0,1:T(8,128)S(1)} %copy.118), channel_id=1, source_target_pairs={{0,16},{16,32},{32,48},{48,64},{64,80},{80,96},{96,112},{1,17},{17... | collective-permute-start | bytes 393224 | tf_op jit(solution)/shard_map/ppermute | solution.py:17
  180.7 8.9 %collective-permute-start.17 = (f32[128,1,256]{2,0,1:T(8,128)S(1)}, f32[128,1,256]{2,0,1:T(8,128)S(1)}, u32[]{:S(2)}, u32[]{:S(2)}) collective-permute-start(f32[128,1,256]{2,0,1:T(8,128)S(1)} %copy.119), channel_id=1, source_target_pairs={{16,0},{32,16},{48,32},{64,48},{80,64},{96,80},{112,96},{17,1},{33... | collective-permute-start | bytes 393224 | tf_op jit(solution)/shard_map/ppermute | solution.py:18
  205.1 7.1 %collective-permute-start.20 = (f32[128,1,256]{2,0,1:T(8,128)S(1)}, f32[128,1,256]{2,0,1:T(8,128)S(1)}, u32[]{:S(2)}, u32[]{:S(2)}) collective-permute-start(f32[128,1,256]{2,0,1:T(8,128)S(1)} %copy.85), channel_id=1, source_target_pairs={{0,16},{16,32},{32,48},{48,64},{64,80},{80,96},{96,112},{1,17},{17... | collective-permute-start | bytes 393224 | tf_op jit(solution)/shard_map/ppermute | solution.py:17
  210.3 6.3 %collective-permute-start.21 = (f32[128,1,256]{2,0,1:T(8,128)S(1)}, f32[128,1,256]{2,0,1:T(8,128)S(1)}, u32[]{:S(2)}, u32[]{:S(2)}) collective-permute-start(f32[128,1,256]{2,0,1:T(8,128)S(1)} %copy.87), channel_id=1, source_target_pairs={{16,0},{32,16},{48,32},{64,48},{80,64},{96,80},{112,96},{17,1},{33... | collective-permute-start | bytes 393224 | tf_op jit(solution)/shard_map/ppermute | solution.py:18
  232.9 5.3 %collective-permute-start.24 = (f32[128,1,256]{2,0,1:T(8,128)S(1)}, f32[128,1,256]{2,0,1:T(8,128)S(1)}, u32[]{:S(2)}, u32[]{:S(2)}) collective-permute-start(f32[128,1,256]{2,0,1:T(8,128)S(1)} %copy.91), channel_id=1, source_target_pairs={{0,16},{16,32},{32,48},{48,64},{64,80},{80,96},{96,112},{1,17},{17... | collective-permute-start | bytes 393224 | tf_op jit(solution)/shard_map/ppermute | solution.py:17
  236.2 6.3 %collective-permute-start.25 = (f32[128,1,256]{2,0,1:T(8,128)S(1)}, f32[128,1,256]{2,0,1:T(8,128)S(1)}, u32[]{:S(2)}, u32[]{:S(2)}) collective-permute-start(f32[128,1,256]{2,0,1:T(8,128)S(1)} %copy.93), channel_id=1, source_target_pairs={{16,0},{32,16},{48,32},{64,48},{80,64},{96,80},{112,96},{17,1},{33... | collective-permute-start | bytes 393224 | tf_op jit(solution)/shard_map/ppermute | solution.py:18
  243.5 5.9 %collective-permute-start.26 = (f32[128,34,1]{0,1,2:T(8,128)S(1)}, f32[128,34,1]{0,1,2:T(8,128)S(1)}, u32[]{:S(2)}, u32[]{:S(2)}) collective-permute-start(f32[128,34,1]{0,1,2:T(8,128)S(1)} %get-tuple-element.10), channel_id=1, source_target_pairs={{0,1},{1,2},{2,3},{3,4},{4,5},{5,6},{6,7},{7,8},{8,9},{9,10},{10,1... | collective-permute-start | bytes 52232 | tf_op jit(solution)/shard_map/ppermute | solution.py:17
  260.9 6.3 %collective-permute-start.29 = (f32[128,1,256]{2,0,1:T(8,128)S(1)}, f32[128,1,256]{2,0,1:T(8,128)S(1)}, u32[]{:S(2)}, u32[]{:S(2)}) collective-permute-start(f32[128,1,256]{2,0,1:T(8,128)S(1)} %copy.99), channel_id=1, source_target_pairs={{16,0},{32,16},{48,32},{64,48},{80,64},{96,80},{112,96},{17,1},{33... | collective-permute-start | bytes 393224 | tf_op jit(solution)/shard_map/ppermute | solution.py:18
  263.0 5.6 %collective-permute-start.28 = (f32[128,1,256]{2,0,1:T(8,128)S(1)}, f32[128,1,256]{2,0,1:T(8,128)S(1)}, u32[]{:S(2)}, u32[]{:S(2)}) collective-permute-start(f32[128,1,256]{2,0,1:T(8,128)S(1)} %copy.97), channel_id=1, source_target_pairs={{0,16},{16,32},{32,48},{48,64},{64,80},{80,96},{96,112},{1,17},{17... | collective-permute-start | bytes 393224 | tf_op jit(solution)/shard_map/ppermute | solution.py:17
  269.5 5.4 %collective-permute-start.30 = (f32[128,34,1]{0,1,2:T(8,128)S(1)}, f32[128,34,1]{0,1,2:T(8,128)S(1)}, u32[]{:S(2)}, u32[]{:S(2)}) collective-permute-start(f32[128,34,1]{0,1,2:T(8,128)S(1)} %get-tuple-element.8), channel_id=1, source_target_pairs={{0,1},{1,2},{2,3},{3,4},{4,5},{5,6},{6,7},{7,8},{8,9},{9,10},{10,1... | collective-permute-start | bytes 52232 | tf_op jit(solution)/shard_map/ppermute | solution.py:17
  (29 other events, 161.6 us)
Sparse Core Ops, SparseCore 0:
  300.6 142.2 all-reduce.1
where the time goes:
time: 473 us; the launch traced here: 466 us
  waiting for transfers between devices  201 us (42%)
  starting transfers between devices  98.9 us (21%)
  other arithmetic  93.5 us (20%)
  local copies, waits for them, and re-layouts  46.3 us (10%)
  between operations  15.9 us (3%)
  matrix products  10.3 us (2%)
    psum x1, waiting for transfers between devices, shards(): gram_total = lax.psum(gram_local, ('lat', 'lon'))  137 us
    ppermute x16, starting transfers between devices, extended(): before = lax.ppermute(last, axis, up)  60.4 us
    add x7, other arithmetic, relax_once(): return center + jnp.where(active, kappa_part * laplace_sum, 0.0)  46.9 us
    ppermute x16, waiting for transfers between devices, extended(): after = lax.ppermute(initial, axis, down)  46.5 us
    unnamed x45, local copies, waits for them, and re-layouts  28.6 us
    ppermute x16, starting transfers between devices, extended(): after = lax.ppermute(initial, axis, down)  26.6 us
    add x1, other arithmetic, shards(): sketch = probes + plain_sweeps(adjoint, kappa, sweep_counts)  13 us
    another operation x3, other arithmetic, shards(): r_factor = jnp.linalg.cholesky(gram_total / cells_all).T  12.4 us
  transfers between devices with their start and end apart: 35, of which 18 were waited for; matrix products, arithmetic and copies ran while one was open for 5% of the time, Pallas kernels for 0%

commit v1 on v0

v1 whole, which is shorter than its diff:
```python
import functools

import jax
import jax.numpy as jnp
from jax import lax
from jax.experimental import pallas as pl
from jax.experimental.pallas import tpu as pltpu
from jax.sharding import PartitionSpec as P

SWEEPS = 4
CAP = 48
K = 128
R = 32
C = 256
H = 4
RE = R + 2 * H
CB = C + 16
NROW = RE * CB
OFF = 8
SLOTS = 384
PLACES = 768
LANES = 128
VMEM_LIMIT = 30 * 1024 * 1024
LAT_ROWS = H * C + 16
OWN_ROWS = R * H + R


def vmem_spec():
    return pl.BlockSpec(memory_space=pltpu.VMEM)


def smem_spec():
    return pl.BlockSpec(memory_space=pltpu.SMEM)


def hbm_spec():
    return pl.BlockSpec(memory_space=pltpu.HBM)


def params():
    return pltpu.CompilerParams(vmem_limit_bytes=VMEM_LIMIT)


def f32(*shape):
    return jax.ShapeDtypeStruct(shape, jnp.float32)


def at(r, c):
    return OFF + r * CB + c


def edge_pack_kernel(flags, counts, kappa_ref, p_hbm, pay_a, pay_b, chunk, sems):
    odd = flags[0]
    first = (jnp.where(odd == 1, 0, R - H), jnp.where(odd == 1, R - H, 0))
    copies = []
    for side in range(2):
        block = pl.multiple_of(jnp.where(first[side] == 0, 0, R - 8), 8)
        for half in range(2):
            n = side * 2 + half
            copies.append(pltpu.make_async_copy(
                p_hbm.at[:, pl.ds(block, 8), pl.ds(half * LANES, LANES)], chunk.at[n], sems.at[n]))
            copies[-1].start()
    flat = chunk.reshape(4 * K * 8, LANES)
    for side, pay in ((0, pay_a), (1, pay_b)):
        within = jnp.where(first[side] == 0, 0, 8 - H)
        for r in range(H):
            for half in range(2):
                lanes = slice(half * LANES, (half + 1) * LANES)
                pay[H * C + 2 * r + half:H * C + 2 * r + half + 1, :] = jnp.where(
                    first[side] == 0, kappa_ref[r:r + 1, lanes], kappa_ref[R - H + r:R - H + r + 1, lanes])
            value = counts[first[side] + r].astype(jnp.float32)
            pay[H * C + 8 + r:H * C + 9 + r, :] = jnp.full((1, K), value, jnp.float32)
        pay[H * C + 8 + H:, :] = jnp.zeros((4, K), jnp.float32)
        for half in range(2):
            n = side * 2 + half
            copies[n].wait()
            for r in range(H):
                pay[r * C + half * LANES:r * C + (half + 1) * LANES, :] = flat[
                    pl.ds(n * K * 8 + within + r, K, stride=8), :].T


def edge_pack(flags, counts, kappa, probes):
    return pl.pallas_call(
        edge_pack_kernel,
        in_specs=[smem_spec(), smem_spec(), vmem_spec(), hbm_spec()],
        out_specs=[vmem_spec()] * 2,
        out_shape=[f32(LAT_ROWS, K)] * 2,
        scratch_shapes=[pltpu.VMEM((4, K, 8, LANES), jnp.float32), pltpu.SemaphoreType.DMA((4,))],
        compiler_params=pltpu.CompilerParams(vmem_limit_bytes=8 * 1024 * 1024),
        name="edge_pack",
    )(flags, counts, kappa, probes)


def turn_kernel(flags, kappa_ref, p_hbm, y_ref, own_a, own_b, chunk, sems):
    def copy(n):
        half, block = n // 4, n % 4
        return pltpu.make_async_copy(
            p_hbm.at[:, pl.ds(block * 8, 8), pl.ds(half * LANES, LANES)], chunk.at[n], sems.at[n])

    for n in range(8):
        copy(n).start()
    flat = chunk.reshape(8 * K * 8, LANES)
    for n in range(8):
        copy(n).wait()
        half, block = n // 4, n % 4
        for i in range(8):
            r = block * 8 + i
            y_ref[r, half * LANES:(half + 1) * LANES, :] = flat[pl.ds(n * K * 8 + i, K, stride=8), :].T
    odd = flags[2]
    for own, low in ((own_a, odd), (own_b, 1 - odd)):
        col = jnp.where(low == 1, 0, C - H)
        lane = pl.multiple_of(jnp.where(low == 1, 0, LANES), LANES)
        for r in range(R):
            own[r * H:(r + 1) * H, :] = y_ref[r, pl.ds(col, H), :]
        own[R * H:, :] = kappa_ref[:, pl.ds(lane, LANES)]


def turn(flags, kappa, probes):
    return pl.pallas_call(
        turn_kernel,
        in_specs=[smem_spec(), vmem_spec(), hbm_spec()],
        out_specs=[vmem_spec()] * 3,
        out_shape=[f32(R, C, K), f32(OWN_ROWS, K), f32(OWN_ROWS, K)],
        scratch_shapes=[pltpu.VMEM((8, K, 8, LANES), jnp.float32), pltpu.SemaphoreType.DMA((8,))],
        compiler_params=pltpu.CompilerParams(vmem_limit_bytes=12 * 1024 * 1024),
        cost_estimate=pl.CostEstimate(flops=0, bytes_accessed=12 * 1024 * 1024, transcendentals=0),
        name="turn",
    )(flags, kappa, probes)


def corner_kernel(flags, own_a, own_b, lat_a, lat_b, pay_a, pay_b):
    odd = flags[2]
    own_rows = own_a.shape[0]
    for own, pay, low in ((own_a, pay_a, odd), (own_b, pay_b, 1 - odd)):
        col = jnp.where(low == 1, 0, C - H)
        pay[:own_rows, :] = own[...]
        base = own_rows
        for lat in (lat_a, lat_b):
            for r in range(H):
                pay[base:base + H, :] = lat[pl.ds(r * C + col, H), :]
                base += H
        if own_rows > R * H:
            for lat in (lat_a, lat_b):
                for r in range(H):
                    pay[base:base + 1, :] = lat[pl.ds(H * C + 2 * r + 1 - low, 1), :]
                    base += 1


def corner(flags, own_a, own_b, lat_a, lat_b):
    rows = own_a.shape[0] + 2 * H * H + (2 * H if own_a.shape[0] > R * H else 0)
    return pl.pallas_call(
        corner_kernel,
        in_specs=[smem_spec()] + [vmem_spec()] * 4,
        out_specs=[vmem_spec()] * 2,
        out_shape=[f32(rows, K)] * 2,
        compiler_params=pltpu.CompilerParams(vmem_limit_bytes=8 * 1024 * 1024),
        name="corner",
    )(flags, own_a, own_b, lat_a, lat_b)


def put_halos(buf, flags, lat_a, lat_b, lon_a, lon_b):
    odd = flags[0]
    lon_odd = flags[2]
    lat_ok = (None, flags[1] == 1)
    lon_ok = (None, flags[3] == 1)
    lat_row = (jnp.where(odd == 1, 0, R + H), jnp.where(odd == 1, R + H, 0))
    lon_col = (jnp.where(lon_odd == 1, 0, C + H), jnp.where(lon_odd == 1, C + H, 0))

    def keep(ok, x):
        return x if ok is None else jnp.where(ok, x, 0.0)

    own_rows = lon_a.shape[0] - 2 * H * H
    own_rows = R * H if own_rows == R * H else OWN_ROWS
    for n, lat in ((0, lat_a), (1, lat_b)):
        for r in range(H):
            start = pl.multiple_of(OFF + (lat_row[n] + r) * CB + 8, 8)
            buf[pl.ds(start, C), :] = keep(lat_ok[n], lat[r * C:(r + 1) * C, :])
    for m, lon in ((0, lon_a), (1, lon_b)):
        for r in range(R):
            start = at(r + H, 4) + lon_col[m]
            buf[pl.ds(start, H), :] = keep(lon_ok[m], lon[r * H:(r + 1) * H, :])
        for n in range(2):
            for r in range(H):
                part = own_rows + (n * H + r) * H
                start = OFF + (lat_row[n] + r) * CB + 4 + lon_col[m]
                buf[pl.ds(start, H), :] = keep(lat_ok[n], keep(lon_ok[m], lon[part:part + H, :]))


def put_kappa(kap, act, flags, counts, kappa_ref, lat_a, lat_b, lon_a, lon_b):
    odd = flags[0]
    lon_odd = flags[2]
    lat_ok = (None, flags[1] == 1)
    lat_row = (jnp.where(odd == 1, 0, R + H), jnp.where(odd == 1, R + H, 0))
    lon_col = (jnp.where(lon_odd == 1, 0, C + H), jnp.where(lon_odd == 1, C + H, 0))
    kap_t = kappa_ref[...].T
    for r in range(R):
        kap[pl.ds(at(r + H, 8), C), :] = jnp.broadcast_to(kap_t[:, r:r + 1], (C, K))
    for n, lat in ((0, lat_a), (1, lat_b)):
        turned = lat[H * C:H * C + 8, :].T
        if n == 1:
            turned = jnp.where(lat_ok[1], turned, 0.0)
        for r in range(H):
            for h in range(2):
                start = pl.multiple_of(OFF + (lat_row[n] + r) * CB + 8 + h * LANES, 8)
                kap[pl.ds(start, LANES), :] = jnp.broadcast_to(turned[:, 2 * r + h:2 * r + h + 1], (LANES, K))
        for r in range(H):
            wide = jnp.broadcast_to(lat[H * C + 8 + r:H * C + 9 + r, :], (8, K))
            for s in range(SWEEPS):
                act[s, lat_row[n] + r] = jnp.where(wide > s, 1.0, 0.0)
    for r in range(R):
        for s in range(SWEEPS):
            act[s, r + H] = jnp.full((8, K), jnp.where(counts[r] > s, 1.0, 0.0), jnp.float32)
    for m, lon in ((0, lon_a), (1, lon_b)):
        src = (jnp.where(lon_odd == 1, LANES - H, 0), jnp.where(lon_odd == 1, 0, LANES - H))[m]
        own = lon[R * H:R * H + R, :].T
        tail = lon[OWN_ROWS + 2 * H * H:, :].T
        low, high = own[:H, :], own[LANES - H:, :]
        edge = jnp.where(src == 0, low, high)
        tail = jnp.where(src == 0, tail[:H, :], tail[LANES - H:, :])
        if m == 1:
            edge = jnp.where(flags[3] == 1, edge, 0.0)
            tail = jnp.where(flags[3] == 1, tail, 0.0)
        for r in range(R):
            kap[pl.ds(at(r + H, 4) + lon_col[m], H), :] = jnp.broadcast_to(edge[:, r:r + 1], (H, K))
        for n in range(2):
            for r in range(H):
                part = jnp.broadcast_to(tail[:, n * H + r:n * H + r + 1], (H, K))
                if n == 1:
                    part = jnp.where(lat_ok[1], part, 0.0)
                kap[pl.ds(OFF + (lat_row[n] + r) * CB + 4 + lon_col[m], H), :] = part


def sweep(src, dst, kap, act, s):
    first = s + 1
    count = RE - 2 * first

    def body(i, _):
        r = first + 2 * i
        base = pl.multiple_of(r * CB, 8)
        a0 = act[s, r]
        a1 = act[s, r + 1]
        for t in range(CB // 8):
            o = base + OFF + t * 8
            up = src[pl.ds(o - CB, 8), :]
            c0 = src[pl.ds(o, 8), :]
            c1 = src[pl.ds(o + CB, 8), :]
            dn = src[pl.ds(o + 2 * CB, 8), :]
            l0 = src[pl.ds(o - 1, 8), :]
            r0 = src[pl.ds(o + 1, 8), :]
            l1 = src[pl.ds(o + CB - 1, 8), :]
            r1 = src[pl.ds(o + CB + 1, 8), :]
            lap0 = (up + c1) + (l0 + r0) - 4.0 * c0
            lap1 = (c0 + dn) + (l1 + r1) - 4.0 * c1
            dst[pl.ds(o, 8), :] = c0 + (a0 * kap[pl.ds(o, 8), :]) * lap0
            dst[pl.ds(o + CB, 8), :] = c1 + (a1 * kap[pl.ds(o + CB, 8), :]) * lap1
        return 0

    lax.fori_loop(0, count // 2, body, 0)


def smooth_kernel(flags, counts, cell_ref, place_ref, y_ref, kap_ref, lat_a, lat_b, lon_a, lon_b,
                  out_ref, kap, act, buf_a, buf_b, rows_ref):
    for r in range(R):
        buf_a[pl.ds(at(r + H, 8), C), :] = y_ref[r]
    put_halos(buf_a, flags, lat_a, lat_b, lon_a, lon_b)
    put_kappa(kap, act, flags, counts, kap_ref, lat_a, lat_b, lon_a, lon_b)
    bufs = (buf_a, buf_b)
    for s in range(SWEEPS):
        sweep(bufs[s % 2], bufs[(s + 1) % 2], kap, act, s)
    rows_ref[...] = jnp.zeros_like(rows_ref)

    def copy(i, _):
        for j in range(8):
            t = i * 8 + j
            rows_ref[pl.ds(place_ref[t], 1), :] = buf_a[pl.ds(cell_ref[t], 1), :]
        return 0

    lax.fori_loop(0, SLOTS // 8, copy, 0)
    out_ref[...] = rows_ref[:PLACES]


def smooth(flags, counts, cell, place, y, kappa, halos):
    return pl.pallas_call(
        smooth_kernel,
        in_specs=[smem_spec()] * 4 + [vmem_spec()] * 6,
        out_specs=[vmem_spec()] * 3,
        out_shape=[f32(PLACES, K), f32(NROW + 16, K), f32(SWEEPS, RE, 8, K)],
        scratch_shapes=[
            pltpu.VMEM((NROW + 16, K), jnp.float32),
            pltpu.VMEM((NROW + 16, K), jnp.float32),
            pltpu.VMEM((PLACES + 8, K), jnp.float32),
        ],
        compiler_params=params(),
        name="smooth",
    )(flags, counts, cell, place, y, kappa, *halos)


def split_kernel(r_ref, high_ref, low_ref):
    for i in range(PLACES // LANES):
        part = r_ref[:, i * LANES:(i + 1) * LANES].T
        high = part.astype(jnp.bfloat16)
        high_ref[i * LANES:(i + 1) * LANES, :] = high
        low_ref[i * LANES:(i + 1) * LANES, :] = (part - high.astype(jnp.float32)).astype(jnp.bfloat16)


def split(r):
    return pl.pallas_call(
        split_kernel,
        in_specs=[vmem_spec()],
        out_specs=[vmem_spec()] * 2,
        out_shape=[jax.ShapeDtypeStruct((PLACES, PLACES), jnp.bfloat16)] * 2,
        compiler_params=pltpu.CompilerParams(vmem_limit_bytes=8 * 1024 * 1024),
        cost_estimate=pl.CostEstimate(flops=0, bytes_accessed=6 * 1024 * 1024, transcendentals=0),
        name="split",
    )(r)


def weigh_kernel(high_ref, low_ref, b_ref, out_ref):
    b = b_ref[...]
    high = b.astype(jnp.bfloat16)
    low = (b - high.astype(jnp.float32)).astype(jnp.bfloat16)
    both = jnp.concatenate([high, low], axis=1)
    one = jnp.dot(high_ref[...], both, preferred_element_type=jnp.float32)
    two = jnp.dot(low_ref[...], high, preferred_element_type=jnp.float32)
    out_ref[...] = one[:, :K] + (one[:, K:] + two)


def weigh(high, low, buffer):
    return pl.pallas_call(
        weigh_kernel,
        in_specs=[vmem_spec()] * 3,
        out_specs=vmem_spec(),
        out_shape=f32(PLACES, K),
        compiler_params=pltpu.CompilerParams(vmem_limit_bytes=12 * 1024 * 1024),
        name="weigh",
    )(high, low, buffer)


def spread_kernel(flags, cell_ref, place_ref, count_ref, ret_ref, field, pay_a, pay_b, own_a, own_b):
    field[...] = jnp.zeros_like(field)

    def add(t, _):
        i = pl.ds(cell_ref[t], 1)
        field[i, :] = field[i, :] + ret_ref[pl.ds(place_ref[t], 1), :]
        return 0

    lax.fori_loop(0, count_ref[0], add, 0)
    odd = flags[0]
    lon_odd = flags[2]
    for pay, low in ((pay_a, odd), (pay_b, 1 - odd)):
        first = jnp.where(low == 1, H, R)
        for r in range(H):
            start = pl.multiple_of(OFF + (first + r) * CB + 8, 8)
            pay[r * C:(r + 1) * C, :] = field[pl.ds(start, C), :]
    for own, low in ((own_a, lon_odd), (own_b, 1 - lon_odd)):
        col = jnp.where(low == 1, 8, 4 + C)
        for r in range(R):
            own[r * H:(r + 1) * H, :] = field[pl.ds(at(r + H, 0) + col, H), :]


def spread(flags, cell, place, count, returned):
    return pl.pallas_call(
        spread_kernel,
        in_specs=[smem_spec()] * 4 + [vmem_spec()],
        out_specs=[vmem_spec()] * 5,
        out_shape=[f32(NROW + 16, K), f32(H * C, K), f32(H * C, K), f32(R * H, K), f32(R * H, K)],
        compiler_params=pltpu.CompilerParams(vmem_limit_bytes=10 * 1024 * 1024),
        name="spread",
    )(flags, cell, place, count, returned)


def finish_kernel(flags, field, kap, act, lat_a, lat_b, lon_a, lon_b, p_hbm, out_hbm, gram_ref,
                  buf_a, buf_b, chunk, in_sems, out_sems):
    def part(ref, n):
        half, block = n // 4, n % 4
        return ref.at[:, pl.ds(block * 8, 8), pl.ds(half * LANES, LANES)]

    def copy_in(n):
        return pltpu.make_async_copy(part(p_hbm, n), chunk.at[n], in_sems.at[n])

    def copy_out(n):
        return pltpu.make_async_copy(chunk.at[n], part(out_hbm, n), out_sems.at[n])

    for n in range(8):
        copy_in(n).start()
    buf_a[...] = field[...]
    put_halos(buf_a, flags, lat_a, lat_b, lon_a, lon_b)
    bufs = (buf_a, buf_b)
    for s in range(SWEEPS):
        sweep(bufs[s % 2], bufs[(s + 1) % 2], kap, act, s)
    flat = chunk.reshape(8 * K * 8, LANES)
    contract = (((1,), (1,)), ((), ()))
    hh = jnp.zeros((K, K), jnp.float32)
    hl = jnp.zeros((K, K), jnp.float32)
    for n in range(8):
        half, block = n // 4, n % 4
        copy_in(n).wait()
        for i in range(0, 8, 2):
            parts = []
            for j in range(2):
                where = pl.ds(n * K * 8 + i + j, K, stride=8)
                start = at(block * 8 + i + j + H, 8) + half * LANES
                sk = flat[where, :] + buf_a[pl.ds(start, LANES), :].T
                flat[where, :] = sk
                parts.append(sk)
            sk = jnp.concatenate(parts, axis=1)
            high = sk.astype(jnp.bfloat16)
            low = (sk - high.astype(jnp.float32)).astype(jnp.bfloat16)
            hh = hh + lax.dot_general(high, high, contract, preferred_element_type=jnp.float32)
            hl = hl + lax.dot_general(high, low, contract, preferred_element_type=jnp.float32)
        copy_out(n).start()
    gram_ref[...] = hh + (hl + hl.T)
    for n in range(8):
        copy_out(n).wait()


def finish(flags, field, kap, act, halos, probes):
    return pl.pallas_call(
        finish_kernel,
        in_specs=[smem_spec()] + [vmem_spec()] * 7 + [hbm_spec()],
        out_specs=[hbm_spec(), vmem_spec()],
        out_shape=[f32(K, R, C), f32(K, K)],
        scratch_shapes=[
            pltpu.VMEM((NROW + 16, K), jnp.float32),
            pltpu.VMEM((NROW + 16, K), jnp.float32),
            pltpu.VMEM((8, K, 8, LANES), jnp.float32),
            pltpu.SemaphoreType.DMA((8,)),
            pltpu.SemaphoreType.DMA((8,)),
        ],
        compiler_params=params(),
        name="finish",
    )(flags, field, kap, act, *halos, probes)


def pairs(size, first):
    return [(i, (i + 1) % size if (i - first) % 2 == 0 else (i - 1) % size) for i in range(size)]


def swap(a, b, axis):
    size = lax.axis_size(axis)
    return lax.ppermute(a, axis, pairs(size, 0)), lax.ppermute(b, axis, pairs(size, 1))


def sum_everywhere(x):
    n_lat, n_lon = lax.axis_size("lat"), lax.axis_size("lon")

    def stage(x, axis, perms):
        got = [lax.ppermute(x, axis, p) for p in perms]
        for g in got:
            x = x + g
        return x

    x = stage(x, "lat", [[(i, i ^ 1) for i in range(n_lat)]])
    x = stage(x, "lat", [[(i, i ^ (2 * d)) for i in range(n_lat)] for d in (1, 2, 3)])
    x = stage(x, "lon", [[(i, i ^ d) for i in range(n_lon)] for d in (1, 2, 3)])
    return stage(x, "lon", [[(i, i ^ (4 * d)) for i in range(n_lon)] for d in (1, 2, 3)])


def shards(probes, kappa, sweep_counts, obs_cell, obs_owner, obs_count, r_inv):
    n_lat, n_lon = lax.axis_size("lat"), lax.axis_size("lon")
    lat, lon = lax.axis_index("lat"), lax.axis_index("lon")
    flags = jnp.stack([
        lat % 2, ((lat > 0) & (lat < n_lat - 1)).astype(jnp.int32),
        lon % 2, ((lon > 0) & (lon < n_lon - 1)).astype(jnp.int32),
    ]).astype(jnp.int32)
    lat_a, lat_b = swap(*edge_pack(flags, sweep_counts, kappa, probes), "lat")
    y, own_a, own_b = turn(flags, kappa, probes)
    high, low = split(r_inv[0, 0])
    halos = (lat_a, lat_b) + swap(*corner(flags, own_a, own_b, lat_a, lat_b), "lon")

    count = obs_count.reshape(1)
    slot_ids = jnp.arange(SLOTS, dtype=jnp.int32)
    is_live = slot_ids < count
    owner_ids = obs_owner[:, 0]
    owner_hit = (
        (owner_ids[:, None] == jnp.arange(n_lon, dtype=jnp.int32)[None, :]) & is_live[:, None]
    ).astype(jnp.int32)
    slot_rank = jnp.sum(jnp.cumsum(owner_hit, axis=0) * owner_hit, axis=1) - 1
    place = jnp.where(is_live, owner_ids * CAP + slot_rank, PLACES)
    cell = OFF + (obs_cell // C + H) * CB + 8 + obs_cell % C

    outgoing, kap, act = smooth(flags, sweep_counts, cell, place, y, kappa, halos)
    buffer = lax.all_to_all(outgoing, "lon", split_axis=0, concat_axis=0, tiled=True)
    mixed = weigh(high, low, buffer)
    returned = lax.all_to_all(mixed, "lon", split_axis=0, concat_axis=0, tiled=True)
    field, pay_a, pay_b, own_a, own_b = spread(flags, cell, place, count, returned)
    lat_a, lat_b = swap(pay_a, pay_b, "lat")
    back = (lat_a, lat_b) + swap(*corner(flags, own_a, own_b, lat_a, lat_b), "lon")
    sketch, gram = finish(flags, field, kap, act, back, probes)
    cells_all = R * C * n_lat * n_lon
    r_factor = jnp.linalg.cholesky(sum_everywhere(gram) / cells_all, symmetrize_input=False).T
    return (sketch, r_factor)


def solution(mesh):
    return jax.shard_map(
        shards,
        mesh=mesh,
        in_specs=(
            P(None, "lat", "lon"),
            P("lat", "lon"),
            P("lat"),
            P(("lat", "lon")),
            P(("lat", "lon"), None),
            P("lat", "lon"),
            P("lat", "lon", None, None),
        ),
        out_specs=(P(None, "lat", "lon"), P()),
        check_vma=False,
    )
```

time: 473 us -> 156 us (0.33)
  the two profiles are of different devices: /device:TPU:1 before, /device:TPU:0 now
where the time goes in v1:
time: 156 us
  waiting for transfers between devices  34.1 us (22%)
  Pallas kernels  32.7 us (21%)
  starting transfers between devices  32.5 us (21%)
  local copies, waits for them, and re-layouts  22.5 us (14%)
  other arithmetic  19.7 us (13%)
  blocking collectives  12.6 us (8%)
    unnamed x45, local copies, waits for them, and re-layouts  21.6 us
    ppermute x4, waiting for transfers between devices, swap(): lax.ppermute(b, axis, pairs(size, 1))  14.4 us
    all_to_all x1, blocking collectives, shards(): lax.all_to_all(mixed, 'lon', split_axis=0, concat_axis=0, tiled=True)  12.6 us
    ppermute x10, starting transfers between devices, stage(): got = [lax.ppermute(x, axis, p) for p in perms]  12.6 us
    another operation x3, other arithmetic, shards(): jnp.linalg.cholesky(sum_everywhere(gram) / cells_all, symmetrize_input=Fa...  12.4 us
    pallas_call x1, Pallas kernels, finish(): pl.pallas_call(finish_kernel, in_specs=[smem_spec()] + [vmem_spec()] * 7...  11.8 us
    ppermute x4, starting transfers between devices, swap(): lax.ppermute(b, axis, pairs(size, 1))  10.9 us
    ppermute x10, waiting for transfers between devices, stage(): got = [lax.ppermute(x, axis, p) for p in perms]  10.6 us
  transfers between devices with their start and end apart: 19, of which 14 were waited for; matrix products, arithmetic and copies ran while one was open for 5% of the time, Pallas kernels for 2%

profile of v1, /device:TPU:0, one launch (start us, length us, event | category | flops | bytes accessed | tf_op | source)
XLA Modules:
  0.0 155.7 jit_solution(11780782960024854165)
XLA Ops:
  0.7 2.2 %copy-done = f32[128,32,256]{2,1,0:T(8,128)S(1)} copy-done((f32[128,32,256]{2,1,0:T(8,128)S(1)}, f32[128,32,256]{2,1,0:T(8,128)}, u32[]{:S(2)}) %copy-start) | copy-done | bytes 4194328
  4.4 2.3 %edge_pack.1 = (f32[1040,128]{1,0:T(8,128)}, f32[1040,128]{1,0:T(8,128)}) custom-call(s32[4]{0:T(128)S(1)} %pad_add_fusion.flags, s32[32]{0:T(128)S(1)} %copy-done.19, f32[32,256]{1,0:T(8,128)S(1)} %copy-done.15, f32[128,32,256]{2,1,0:T(8,128)S(1)} %copy-done), custom_call_target="tpu_custom_call" | custom-call | tf_op jit(solution)/shard_map/edge_pack/pallas_call | solution.py:83
  6.8 3.2 %collective-permute-start.1 = (f32[1040,128]{1,0:T(8,128)}, f32[1040,128]{1,0:T(8,128)S(1)}, u32[]{:S(2)}, u32[]{:S(2)}) collective-permute-start(f32[1040,128]{1,0:T(8,128)} %get-tuple-element.27), channel_id=1, source_target_pairs={{0,112},{16,32},{32,16},{48,64},{64,48},{80,96},{96,80},{112,0},{1... | collective-permute-start | bytes 1597448 | tf_op jit(solution)/shard_map/ppermute | solution.py:441
  10.0 2.9 %turn.1 = (f32[32,256,128]{2,1,0:T(8,128)S(1)}, f32[160,128]{1,0:T(8,128)S(1)}, f32[160,128]{1,0:T(8,128)S(1)}) custom-call(s32[4]{0:T(128)S(1)} %pad_add_fusion.flags, f32[32,256]{1,0:T(8,128)S(1)} %copy-done.16, f32[128,32,256]{2,1,0:T(8,128)S(1)} %copy-done.1), custom_call_target="tpu_custom_call" | custom-call | bytes 12582912 | tf_op jit(solution)/shard_map/turn/pallas_call | solution.py:119
  18.0 2.6 %reduce-window.6 = s32[16,3,128]{2,0,1:T(8,128)} reduce-window(s32[16,3,128]{2,0,1:T(8,128)} %fusion.4, s32[]{:T(128)} %constant.92.clone.1), window={size=1x1x128 pad=0_0x0_0x127_0}, to_apply=%region_0.1 | reduce-window | flops 780288 | bytes 49156 | tf_op jit(solution)/shard_map/reduce-window
  26.4 4.7 %collective-permute-start.3 = (f32[200,128]{1,0:T(8,128)S(1)}, f32[200,128]{1,0:T(8,128)S(1)}, u32[]{:S(2)}, u32[]{:S(2)}) collective-permute-start(f32[200,128]{1,0:T(8,128)S(1)} %get-tuple-element.31), channel_id=1, source_target_pairs={{0,15},{1,2},{2,1},{3,4},{4,3},{5,6},{6,5},{7,8},{8,7},{9,10},{10,... | collective-permute-start | bytes 307208 | tf_op jit(solution)/shard_map/ppermute | solution.py:441
  31.8 2.6 %collective-permute-done.3.lon_b = f32[200,128]{1,0:T(8,128)S(1)} collective-permute-done((f32[200,128]{1,0:T(8,128)S(1)}, f32[200,128]{1,0:T(8,128)S(1)}, u32[]{:S(2)}, u32[]{:S(2)}) %collective-permute-start.3) | collective-permute-done | bytes 102432 | tf_op jit(solution)/shard_map/ppermute | solution.py:441
  34.4 2.2 %copy-done.6 = f32[32,256,128]{2,1,0:T(8,128)S(1)} copy-done((f32[32,256,128]{2,1,0:T(8,128)S(1)}, f32[32,256,128]{2,1,0:T(8,128)}, u32[]{:S(2)}) %copy-start.6) | copy-done | bytes 4194328
  36.6 9.8 %smooth.1 = (f32[768,128]{1,0:T(8,128)S(1)}, f32[10896,128]{1,0:T(8,128)S(1)}, f32[4,40,8,128]{3,2,1,0:T(8,128)S(1)}) custom-call(s32[4]{0:T(128)S(1)} %pad_add_fusion.flags, s32[32]{0:T(128)S(1)} %copy-done.20, s32[384]{0:T(512)S(1)} %get-tuple-element.48.cell_ref, s32[384]{0:T(512)S(1)} %get-tuple-element.49.place_ref, f32[32,256,128]{2,1,0:T(8,128)S(1)} %copy-done.6, ...), custom_call_target="tpu_custom_call" | custom-call | tf_op jit(solution)/shard_map/smooth/pallas_call | solution.py:283
  46.4 2.4 %copy-done.3 = f32[10896,128]{1,0:T(8,128)} copy-done((f32[10896,128]{1,0:T(8,128)}, f32[10896,128]{1,0:T(8,128)S(1)}, u32[]{:S(2)}) %copy-start.3) | copy-done | bytes 5578776
  50.4 6.2 %all-to-all-start = ((f32[16,48,128]{2,1,0:T(8,128)}), f32[16,48,128]{2,1,0:T(8,128)S(1)}, u32[]{:S(2)}, u32[]{:S(2)}) async-start(f32[16,48,128]{2,1,0:T(8,128)} %bitcast.38), calls=%async_computation | async-start | bytes 786432 | tf_op jit(solution)/shard_map/all_to_all | solution.py:483
  59.4 6.4 %all-to-all-done = f32[16,48,128]{2,1,0:T(8,128)S(1)} async-done(((f32[16,48,128]{2,1,0:T(8,128)}), f32[16,48,128]{2,1,0:T(8,128)S(1)}, u32[]{:S(2)}, u32[]{:S(2)}) %all-to-all-start) | async-done | bytes 393248 | tf_op jit(solution)/shard_map/all_to_all | solution.py:483
  69.4 12.6 %all_to_all.22 = f32[16,48,128]{2,1,0:T(8,128)S(1)} all-to-all(f32[16,48,128]{2,1,0:T(8,128)S(1)} %bitcast.37), channel_id=1, replica_groups=mesh['lat'=8,'lon'=16] {'lon'}, dimensions={0} | all-to-all | bytes 786432 | tf_op jit(solution)/shard_map/all_to_all | solution.py:485
  82.1 3.3 %spread.1 = (f32[10896,128]{1,0:T(8,128)S(1)}, f32[1024,128]{1,0:T(8,128)S(1)}, f32[1024,128]{1,0:T(8,128)S(1)}, f32[128,128]{1,0:T(8,128)S(1)}, f32[128,128]{1,0:T(8,128)S(1)}) custom-call(s32[4]{0:T(128)S(1)} %pad_add_fusion.flags, s32[384]{0:T(512)S(1)} %get-tuple-element.48.cell_ref, s32[384]{0:T(512)S(1)} %get-tuple-element.49.place_ref, ...), custom_call_target="tpu_custom_call" | custom-call | tf_op jit(solution)/shard_map/spread/pallas_call | solution.py:362
  87.4 8.0 %collective-permute-done.5.lat_b = f32[1024,128]{1,0:T(8,128)S(1)} collective-permute-done((f32[1024,128]{1,0:T(8,128)S(1)}, f32[1024,128]{1,0:T(8,128)S(1)}, u32[]{:S(2)}, u32[]{:S(2)}) %collective-permute-start.5) | collective-permute-done | bytes 524320 | tf_op jit(solution)/shard_map/ppermute | solution.py:441
  96.5 2.1 %collective-permute-start.7 = (f32[160,128]{1,0:T(8,128)S(1)}, f32[160,128]{1,0:T(8,128)S(1)}, u32[]{:S(2)}, u32[]{:S(2)}) collective-permute-start(f32[160,128]{1,0:T(8,128)S(1)} %get-tuple-element.41), channel_id=1, source_target_pairs={{0,15},{1,2},{2,1},{3,4},{4,3},{5,6},{6,5},{7,8},{8,7},{9,10},{10,... | collective-permute-start | bytes 245768 | tf_op jit(solution)/shard_map/ppermute | solution.py:441
  100.5 3.8 %collective-permute-done.7.lon_b = f32[160,128]{1,0:T(8,128)S(1)} collective-permute-done((f32[160,128]{1,0:T(8,128)S(1)}, f32[160,128]{1,0:T(8,128)S(1)}, u32[]{:S(2)}, u32[]{:S(2)}) %collective-permute-start.7) | collective-permute-done | bytes 81952 | tf_op jit(solution)/shard_map/ppermute | solution.py:441
  104.3 2.6 %copy-done.4 = f32[10896,128]{1,0:T(8,128)S(1)} copy-done((f32[10896,128]{1,0:T(8,128)S(1)}, f32[10896,128]{1,0:T(8,128)}, u32[]{:S(2)}) %copy-start.4) | copy-done | bytes 5578776
  106.9 11.8 %finish.1 = (f32[128,32,256]{2,1,0:T(8,128)}, f32[128,128]{1,0:T(8,128)S(1)}) custom-call(s32[4]{0:T(128)S(1)} %pad_add_fusion.flags, f32[10896,128]{1,0:T(8,128)S(1)} %get-tuple-element.33.field, f32[10896,128]{1,0:T(8,128)S(1)} %copy-done.4, f32[4,40,8,128]{3,2,1,0:T(8,128)S(1)} %copy-done.13, f32[1024,128]{1,0:T(8,128)S(1)} %collective-permute-done.4.lat_a, ...), custom_call_target="tpu_custom_call" | custom-call | tf_op jit(solution)/shard_map/finish/pallas_call | solution.py:418
  121.8 2.4 %collective-permute-start.9 = (f32[128,128]{1,0:T(8,128)S(1)}, f32[128,128]{1,0:T(8,128)S(1)}, u32[]{:S(2)}, u32[]{:S(2)}) collective-permute-start(f32[128,128]{1,0:T(8,128)S(1)} %add.80), channel_id=1, source_target_pairs={{0,32},{16,48},{32,0},{48,16},{64,96},{80,112},{96,64},{112,80},{1... | collective-permute-start | bytes 196616 | tf_op jit(solution)/shard_map/ppermute | solution.py:448
  124.2 2.7 %collective-permute-done.11 = f32[128,128]{1,0:T(8,128)S(1)} collective-permute-done((f32[128,128]{1,0:T(8,128)S(1)}, f32[128,128]{1,0:T(8,128)S(1)}, u32[]{:S(2)}, u32[]{:S(2)}) %collective-permute-start.11) | collective-permute-done | bytes 65568 | tf_op jit(solution)/shard_map/ppermute | solution.py:448
  127.9 3.7 %collective-permute-start.12 = (f32[128,128]{1,0:T(8,128)S(1)}, f32[128,128]{1,0:T(8,128)S(1)}, u32[]{:S(2)}, u32[]{:S(2)}) collective-permute-start(f32[128,128]{1,0:T(8,128)S(1)} %add_add_fusion.1), channel_id=1, source_target_pairs={{0,1},{1,0},{2,3},{3,2},{4,5},{5,4},{6,7},{7,6},{8,9},{9,8},{10,11... | collective-permute-start | bytes 196616 | tf_op jit(solution)/shard_map/ppermute | solution.py:448
  136.1 2.6 %collective-permute-start.15 = (f32[128,128]{1,0:T(8,128)S(1)}, f32[128,128]{1,0:T(8,128)S(1)}, u32[]{:S(2)}, u32[]{:S(2)}) collective-permute-start(f32[128,128]{1,0:T(8,128)S(1)} %add_add_fusion), channel_id=1, source_target_pairs={{0,4},{1,5},{2,6},{3,7},{4,0},{5,1},{6,2},{7,3},{8,12},{9,13},{10,... | collective-permute-start | bytes 196616 | tf_op jit(solution)/shard_map/ppermute | solution.py:448
  141.9 11.7 %cholesky.18 = f32[128,128]{1,0:T(8,128)S(1)} custom-call(f32[128,128]{1,0:T(8,128)S(1)} %add_multiply_fusion), custom_call_target="Cholesky" | custom-call | tf_op jit(solution)/shard_map/jit(cholesky)/cholesky | solution.py:491
  (87 shorter events, 39.3 us)
Async XLA Ops:
  4.4 12.4 %copy-start.21 = (s32[384,1]{0,1:T(1,128)S(1)}, s32[384,1]{0,1:T(1,128)}, u32[]{:S(2)}) copy-start(s32[384,1]{0,1:T(1,128)} %param.11) | copy-start | bytes 4612
  4.4 30.0 %copy-start.20 = (s32[32]{0:T(128)S(1)}, s32[32]{0:T(128)}, u32[]{:S(2)}) copy-start(s32[32]{0:T(128)} %counts.3) | copy-start | bytes 388
  6.7 16.2 %collective-permute-start = (f32[1040,128]{1,0:T(8,128)}, f32[1040,128]{1,0:T(8,128)S(1)}, u32[]{:S(2)}, u32[]{:S(2)}) collective-permute-start(f32[1040,128]{1,0:T(8,128)} %get-tuple-element.26), channel_id=1, source_target_pairs={{0,16},{16,0},{32,48},{48,32},{64,80},{80,64},{96,112},{112,96},{1... | collective-permute-start | bytes 1597448 | tf_op jit(solution)/shard_map/ppermute | solution.py:441
  6.8 16.1 %collective-permute-start.1 = (f32[1040,128]{1,0:T(8,128)}, f32[1040,128]{1,0:T(8,128)S(1)}, u32[]{:S(2)}, u32[]{:S(2)}) collective-permute-start(f32[1040,128]{1,0:T(8,128)} %get-tuple-element.27), channel_id=1, source_target_pairs={{0,112},{16,32},{32,16},{48,64},{64,48},{80,96},{96,80},{112,0},{1... | collective-permute-start | bytes 1597448 | tf_op jit(solution)/shard_map/ppermute | solution.py:441
  10.0 46.6 %copy-start.7 = (f32[1,1,768,768]{3,2,1,0:T(8,128)S(1)}, f32[1,1,768,768]{3,2,1,0:T(8,128)}, u32[]{:S(2)}) copy-start(f32[1,1,768,768]{3,2,1,0:T(8,128)} %param.13) | copy-start | bytes 7077892
  24.4 7.4 %collective-permute-start.2 = (f32[200,128]{1,0:T(8,128)S(1)}, f32[200,128]{1,0:T(8,128)S(1)}, u32[]{:S(2)}, u32[]{:S(2)}) collective-permute-start(f32[200,128]{1,0:T(8,128)S(1)} %get-tuple-element.30), channel_id=1, source_target_pairs={{0,1},{1,0},{2,3},{3,2},{4,5},{5,4},{6,7},{7,6},{8,9},{9,8},{10,11... | collective-permute-start | bytes 307208 | tf_op jit(solution)/shard_map/ppermute | solution.py:441
  26.4 8.0 %collective-permute-start.3 = (f32[200,128]{1,0:T(8,128)S(1)}, f32[200,128]{1,0:T(8,128)S(1)}, u32[]{:S(2)}, u32[]{:S(2)}) collective-permute-start(f32[200,128]{1,0:T(8,128)S(1)} %get-tuple-element.31), channel_id=1, source_target_pairs={{0,15},{1,2},{2,1},{3,4},{4,3},{5,6},{6,5},{7,8},{8,7},{9,10},{10,... | collective-permute-start | bytes 307208 | tf_op jit(solution)/shard_map/ppermute | solution.py:441
  50.4 53.9 %copy-start.13 = (f32[4,40,8,128]{3,2,1,0:T(8,128)S(1)}, f32[4,40,8,128]{3,2,1,0:T(8,128)}, u32[]{:S(2)}) copy-start(f32[4,40,8,128]{3,2,1,0:T(8,128)} %copy-done.12) | copy-start | bytes 1966084
  50.4 15.4 %all-to-all-start = ((f32[16,48,128]{2,1,0:T(8,128)}), f32[16,48,128]{2,1,0:T(8,128)S(1)}, u32[]{:S(2)}, u32[]{:S(2)}) async-start(f32[16,48,128]{2,1,0:T(8,128)} %bitcast.38), calls=%async_computation | async-start | bytes 786432 | tf_op jit(solution)/shard_map/all_to_all | solution.py:483
  65.8 38.5 %copy-start.2 = (f32[128,32,256]{2,1,0:T(8,128)S(1)}, f32[128,32,256]{2,1,0:T(8,128)}, u32[]{:S(2)}) copy-start(f32[128,32,256]{2,1,0:T(8,128)} %p_hbm.5) | copy-start | bytes 12582916
  85.4 2.0 %collective-permute-start.4 = (f32[1024,128]{1,0:T(8,128)S(1)}, f32[1024,128]{1,0:T(8,128)S(1)}, u32[]{:S(2)}, u32[]{:S(2)}) collective-permute-start(f32[1024,128]{1,0:T(8,128)S(1)} %get-tuple-element.36), channel_id=1, source_target_pairs={{0,16},{16,0},{32,48},{48,32},{64,80},{80,64},{96,112},{112,96},{1... | collective-permute-start | bytes 1572872 | tf_op jit(solution)/shard_map/ppermute | solution.py:441
  85.5 9.9 %collective-permute-start.5 = (f32[1024,128]{1,0:T(8,128)S(1)}, f32[1024,128]{1,0:T(8,128)S(1)}, u32[]{:S(2)}, u32[]{:S(2)}) collective-permute-start(f32[1024,128]{1,0:T(8,128)S(1)} %get-tuple-element.37), channel_id=1, source_target_pairs={{0,112},{16,32},{32,16},{48,64},{64,48},{80,96},{96,80},{112,0},{1... | collective-permute-start | bytes 1572872 | tf_op jit(solution)/shard_map/ppermute | solution.py:441
  95.9 4.5 %collective-permute-start.6 = (f32[160,128]{1,0:T(8,128)S(1)}, f32[160,128]{1,0:T(8,128)S(1)}, u32[]{:S(2)}, u32[]{:S(2)}) collective-permute-start(f32[160,128]{1,0:T(8,128)S(1)} %get-tuple-element.40), channel_id=1, source_target_pairs={{0,1},{1,0},{2,3},{3,2},{4,5},{5,4},{6,7},{7,6},{8,9},{9,8},{10,11... | collective-permute-start | bytes 245768 | tf_op jit(solution)/shard_map/ppermute | solution.py:441
  96.5 7.8 %collective-permute-start.7 = (f32[160,128]{1,0:T(8,128)S(1)}, f32[160,128]{1,0:T(8,128)S(1)}, u32[]{:S(2)}, u32[]{:S(2)}) collective-permute-start(f32[160,128]{1,0:T(8,128)S(1)} %get-tuple-element.41), channel_id=1, source_target_pairs={{0,15},{1,2},{2,1},{3,4},{4,3},{5,6},{6,5},{7,8},{8,7},{9,10},{10,... | collective-permute-start | bytes 245768 | tf_op jit(solution)/shard_map/ppermute | solution.py:441
  118.7 1.3 collective-permute-start.8
  120.0 6.8 %collective-permute-start.11 = (f32[128,128]{1,0:T(8,128)S(1)}, f32[128,128]{1,0:T(8,128)S(1)}, u32[]{:S(2)}, u32[]{:S(2)}) collective-permute-start(f32[128,128]{1,0:T(8,128)S(1)} %add.80), channel_id=1, source_target_pairs={{0,96},{16,112},{32,64},{48,80},{64,32},{80,48},{96,0},{112,16},{1... | collective-permute-start | bytes 196616 | tf_op jit(solution)/shard_map/ppermute | solution.py:448
  120.1 6.8 %collective-permute-start.10 = (f32[128,128]{1,0:T(8,128)S(1)}, f32[128,128]{1,0:T(8,128)S(1)}, u32[]{:S(2)}, u32[]{:S(2)}) collective-permute-start(f32[128,128]{1,0:T(8,128)S(1)} %add.80), channel_id=1, source_target_pairs={{0,64},{16,80},{32,96},{48,112},{64,0},{80,16},{96,32},{112,48},{1... | collective-permute-start | bytes 196616 | tf_op jit(solution)/shard_map/ppermute | solution.py:448
  121.8 5.6 %collective-permute-start.9 = (f32[128,128]{1,0:T(8,128)S(1)}, f32[128,128]{1,0:T(8,128)S(1)}, u32[]{:S(2)}, u32[]{:S(2)}) collective-permute-start(f32[128,128]{1,0:T(8,128)S(1)} %add.80), channel_id=1, source_target_pairs={{0,32},{16,48},{32,0},{48,16},{64,96},{80,112},{96,64},{112,80},{1... | collective-permute-start | bytes 196616 | tf_op jit(solution)/shard_map/ppermute | solution.py:448
  127.4 5.6 %collective-permute-start.14 = (f32[128,128]{1,0:T(8,128)S(1)}, f32[128,128]{1,0:T(8,128)S(1)}, u32[]{:S(2)}, u32[]{:S(2)}) collective-permute-start(f32[128,128]{1,0:T(8,128)S(1)} %add_add_fusion.1), channel_id=1, source_target_pairs={{0,3},{1,2},{2,1},{3,0},{4,7},{5,6},{6,5},{7,4},{8,11},{9,10},{10,... | collective-permute-start | bytes 196616 | tf_op jit(solution)/shard_map/ppermute | solution.py:448
  127.9 5.8 %collective-permute-start.13 = (f32[128,128]{1,0:T(8,128)S(1)}, f32[128,128]{1,0:T(8,128)S(1)}, u32[]{:S(2)}, u32[]{:S(2)}) collective-permute-start(f32[128,128]{1,0:T(8,128)S(1)} %add_add_fusion.1), channel_id=1, source_target_pairs={{0,2},{1,3},{2,0},{3,1},{4,6},{5,7},{6,4},{7,5},{8,10},{9,11},{10,... | collective-permute-start | bytes 196616 | tf_op jit(solution)/shard_map/ppermute | solution.py:448
  127.9 6.7 %collective-permute-start.12 = (f32[128,128]{1,0:T(8,128)S(1)}, f32[128,128]{1,0:T(8,128)S(1)}, u32[]{:S(2)}, u32[]{:S(2)}) collective-permute-start(f32[128,128]{1,0:T(8,128)S(1)} %add_add_fusion.1), channel_id=1, source_target_pairs={{0,1},{1,0},{2,3},{3,2},{4,5},{5,4},{6,7},{7,6},{8,9},{9,8},{10,11... | collective-permute-start | bytes 196616 | tf_op jit(solution)/shard_map/ppermute | solution.py:448
  134.6 5.6 %collective-permute-start.17 = (f32[128,128]{1,0:T(8,128)S(1)}, f32[128,128]{1,0:T(8,128)S(1)}, u32[]{:S(2)}, u32[]{:S(2)}) collective-permute-start(f32[128,128]{1,0:T(8,128)S(1)} %add_add_fusion), channel_id=1, source_target_pairs={{0,12},{1,13},{2,14},{3,15},{4,8},{5,9},{6,10},{7,11},{8,4},{9,5},... | collective-permute-start | bytes 196616 | tf_op jit(solution)/shard_map/ppermute | solution.py:448
  136.1 5.8 %collective-permute-start.16 = (f32[128,128]{1,0:T(8,128)S(1)}, f32[128,128]{1,0:T(8,128)S(1)}, u32[]{:S(2)}, u32[]{:S(2)}) collective-permute-start(f32[128,128]{1,0:T(8,128)S(1)} %add_add_fusion), channel_id=1, source_target_pairs={{0,8},{1,9},{2,10},{3,11},{4,12},{5,13},{6,14},{7,15},{8,0},{9,1},... | collective-permute-start | bytes 196616 | tf_op jit(solution)/shard_map/ppermute | solution.py:448
  136.1 5.8 %collective-permute-start.15 = (f32[128,128]{1,0:T(8,128)S(1)}, f32[128,128]{1,0:T(8,128)S(1)}, u32[]{:S(2)}, u32[]{:S(2)}) collective-permute-start(f32[128,128]{1,0:T(8,128)S(1)} %add_add_fusion), channel_id=1, source_target_pairs={{0,4},{1,5},{2,6},{3,7},{4,0},{5,1},{6,2},{7,3},{8,12},{9,13},{10,... | collective-permute-start | bytes 196616 | tf_op jit(solution)/shard_map/ppermute | solution.py:448
  (17 other events, 35.9 us)

commit v2 on v1

--- a/solution.py
+++ b/solution.py
@@ -23,6 +23,8 @@
 VMEM_LIMIT = 30 * 1024 * 1024
 LAT_ROWS = H * C + 16
 OWN_ROWS = R * H + R
+LON_OWNERS = 16
+WEIGH_PARTS = 3
 
 
 def vmem_spec():
@@ -43,6 +45,18 @@
 
 def f32(*shape):
     return jax.ShapeDtypeStruct(shape, jnp.float32)
+
+
+def held(*shape):
+    return pltpu.VMEM(shape, jnp.float32)
+
+
+def in_vmem(*arrays):
+    return tuple(pltpu.with_memory_space_constraint(a, pltpu.VMEM) for a in arrays)
+
+
+def in_hbm(array):
+    return pltpu.with_memory_space_constraint(array, pltpu.HBM)
 
 
 def at(r, c):
@@ -88,7 +102,7 @@
         scratch_shapes=[pltpu.VMEM((4, K, 8, LANES), jnp.float32), pltpu.SemaphoreType.DMA((4,))],
         compiler_params=pltpu.CompilerParams(vmem_limit_bytes=8 * 1024 * 1024),
         name="edge_pack",
-    )(flags, counts, kappa, probes)
+    )(flags, counts, kappa, in_hbm(probes))
 
 
 def turn_kernel(flags, kappa_ref, p_hbm, y_ref, own_a, own_b, chunk, sems):
@@ -120,12 +134,12 @@
         turn_kernel,
         in_specs=[smem_spec(), vmem_spec(), hbm_spec()],
         out_specs=[vmem_spec()] * 3,
-        out_shape=[f32(R, C, K), f32(OWN_ROWS, K), f32(OWN_ROWS, K)],
+        out_shape=[held(R, C, K), held(OWN_ROWS, K), held(OWN_ROWS, K)],
         scratch_shapes=[pltpu.VMEM((8, K, 8, LANES), jnp.float32), pltpu.SemaphoreType.DMA((8,))],
         compiler_params=pltpu.CompilerParams(vmem_limit_bytes=12 * 1024 * 1024),
         cost_estimate=pl.CostEstimate(flops=0, bytes_accessed=12 * 1024 * 1024, transcendentals=0),
         name="turn",
-    )(flags, kappa, probes)
+    )(flags, kappa, in_hbm(probes))
 
 
 def corner_kernel(flags, own_a, own_b, lat_a, lat_b, pay_a, pay_b):
@@ -155,7 +169,7 @@
         out_shape=[f32(rows, K)] * 2,
         compiler_params=pltpu.CompilerParams(vmem_limit_bytes=8 * 1024 * 1024),
         name="corner",
-    )(flags, own_a, own_b, lat_a, lat_b)
+    )(flags, *in_vmem(own_a, own_b), lat_a, lat_b)
 
 
 def put_halos(buf, flags, lat_a, lat_b, lon_a, lon_b):
@@ -186,7 +200,7 @@
                 buf[pl.ds(start, H), :] = keep(lat_ok[n], keep(lon_ok[m], lon[part:part + H, :]))
 
 
-def put_kappa(kap, act, flags, counts, kappa_ref, lat_a, lat_b, lon_a, lon_b):
+def coeffs_kernel(flags, counts, kappa_ref, tail_a, tail_b, lon_a, lon_b, after, kap, act):
     odd = flags[0]
     lon_odd = flags[2]
     lat_ok = (None, flags[1] == 1)
@@ -195,8 +209,8 @@
     kap_t = kappa_ref[...].T
     for r in range(R):
         kap[pl.ds(at(r + H, 8), C), :] = jnp.broadcast_to(kap_t[:, r:r + 1], (C, K))
-    for n, lat in ((0, lat_a), (1, lat_b)):
-        turned = lat[H * C:H * C + 8, :].T
+    for n, lat in ((0, tail_a), (1, tail_b)):
+        turned = lat[:8, :].T
         if n == 1:
             turned = jnp.where(lat_ok[1], turned, 0.0)
         for r in range(H):
@@ -204,7 +218,7 @@
                 start = pl.multiple_of(OFF + (lat_row[n] + r) * CB + 8 + h * LANES, 8)
                 kap[pl.ds(start, LANES), :] = jnp.broadcast_to(turned[:, 2 * r + h:2 * r + h + 1], (LANES, K))
         for r in range(H):
-            wide = jnp.broadcast_to(lat[H * C + 8 + r:H * C + 9 + r, :], (8, K))
+            wide = jnp.broadcast_to(lat[8 + r:9 + r, :], (8, K))
             for s in range(SWEEPS):
                 act[s, lat_row[n] + r] = jnp.where(wide > s, 1.0, 0.0)
     for r in range(R):
@@ -258,12 +272,56 @@
     lax.fori_loop(0, count // 2, body, 0)
 
 
-def smooth_kernel(flags, counts, cell_ref, place_ref, y_ref, kap_ref, lat_a, lat_b, lon_a, lon_b,
-                  out_ref, kap, act, buf_a, buf_b, rows_ref):
+def coeffs(flags, counts, kappa, tail_a, tail_b, lon_a, lon_b, after):
+    return pl.pallas_call(
+        coeffs_kernel,
+        in_specs=[smem_spec()] * 2 + [vmem_spec()] * 5 + [pl.BlockSpec(memory_space=pl.ANY)],
+        out_specs=[vmem_spec()] * 2,
+        out_shape=[held(NROW + 16, K), held(SWEEPS, RE, 8, K)],
+        compiler_params=pltpu.CompilerParams(vmem_limit_bytes=8 * 1024 * 1024),
+        cost_estimate=pl.CostEstimate(flops=0, bytes_accessed=4 * 1024 * 1024, transcendentals=0),
+        name="coeffs",
+    )(flags, counts, kappa, tail_a, tail_b, lon_a, lon_b, after)
+
+
+def places_kernel(count_ref, cell_ref, owner_ref, row_ref, place_ref, seen):
+    for i in range(LON_OWNERS):
+        seen[i] = 0
+    count = count_ref[0]
+
+    def one(t, _):
+        owner = owner_ref[0, t]
+        rank = seen[owner]
+        live = t < count
+        seen[owner] = rank + jnp.where(live, 1, 0)
+        place_ref[t] = jnp.where(live, owner * CAP + rank, PLACES)
+        cell = cell_ref[t]
+        row_ref[t] = OFF + 8 + H * CB + (cell >> 8) * CB + (cell & (C - 1))
+        return 0
+
+    lax.fori_loop(0, SLOTS, one, 0, unroll=8)
+
+
+def places(count, cell, owner):
+    return pl.pallas_call(
+        places_kernel,
+        in_specs=[smem_spec()] * 3,
+        out_specs=[smem_spec()] * 2,
+        out_shape=[jax.ShapeDtypeStruct((SLOTS,), jnp.int32)] * 2,
+        scratch_shapes=[pltpu.SMEM((LON_OWNERS,), jnp.int32)],
+        cost_estimate=pl.CostEstimate(flops=0, bytes_accessed=4 * 1024 * 1024, transcendentals=0),
+        compiler_params=pltpu.CompilerParams(vmem_limit_bytes=1024 * 1024),
+        name="places",
+    )(count, cell, owner)
+
+
+def smooth_kernel(flags, cell_ref, place_ref, y_ref, kap, act, lat_a, lat_b, lon_a, lon_b,
+                  out_ref, tail_a, tail_b, buf_a, buf_b, rows_ref):
     for r in range(R):
         buf_a[pl.ds(at(r + H, 8), C), :] = y_ref[r]
     put_halos(buf_a, flags, lat_a, lat_b, lon_a, lon_b)
-    put_kappa(kap, act, flags, counts, kap_ref, lat_a, lat_b, lon_a, lon_b)
+    tail_a[...] = lat_a[H * C:, :]
+    tail_b[...] = lat_b[H * C:, :]
     bufs = (buf_a, buf_b)
     for s in range(SWEEPS):
         sweep(bufs[s % 2], bufs[(s + 1) % 2], kap, act, s)
@@ -279,12 +337,12 @@
     out_ref[...] = rows_ref[:PLACES]
 
 
-def smooth(flags, counts, cell, place, y, kappa, halos):
+def smooth(flags, cell, place, y, kap, act, halos):
     return pl.pallas_call(
         smooth_kernel,
-        in_specs=[smem_spec()] * 4 + [vmem_spec()] * 6,
+        in_specs=[smem_spec()] * 3 + [vmem_spec()] * 7,
         out_specs=[vmem_spec()] * 3,
-        out_shape=[f32(PLACES, K), f32(NROW + 16, K), f32(SWEEPS, RE, 8, K)],
+        out_shape=[f32(PLACES, K), f32(16, K), f32(16, K)],
         scratch_shapes=[
             pltpu.VMEM((NROW + 16, K), jnp.float32),
             pltpu.VMEM((NROW + 16, K), jnp.float32),
@@ -292,48 +350,44 @@
         ],
         compiler_params=params(),
         name="smooth",
-    )(flags, counts, cell, place, y, kappa, *halos)
-
-
-def split_kernel(r_ref, high_ref, low_ref):
-    for i in range(PLACES // LANES):
-        part = r_ref[:, i * LANES:(i + 1) * LANES].T
-        high = part.astype(jnp.bfloat16)
-        high_ref[i * LANES:(i + 1) * LANES, :] = high
-        low_ref[i * LANES:(i + 1) * LANES, :] = (part - high.astype(jnp.float32)).astype(jnp.bfloat16)
-
-
-def split(r):
-    return pl.pallas_call(
-        split_kernel,
-        in_specs=[vmem_spec()],
-        out_specs=[vmem_spec()] * 2,
-        out_shape=[jax.ShapeDtypeStruct((PLACES, PLACES), jnp.bfloat16)] * 2,
-        compiler_params=pltpu.CompilerParams(vmem_limit_bytes=8 * 1024 * 1024),
-        cost_estimate=pl.CostEstimate(flops=0, bytes_accessed=6 * 1024 * 1024, transcendentals=0),
-        name="split",
-    )(r)
-
-
-def weigh_kernel(high_ref, low_ref, b_ref, out_ref):
-    b = b_ref[...]
+    )(flags, cell, place, *in_vmem(y, kap, act), *halos)
+
+
+def weigh_kernel(b_ref, r_hbm, out_ref, r_ref, sems):
+    width = PLACES // WEIGH_PARTS
+
+    def copy(n):
+        return pltpu.make_async_copy(r_hbm.at[:, pl.ds(n * width, width)], r_ref.at[n], sems.at[n])
+
+    for n in range(WEIGH_PARTS):
+        copy(n).start()
+    b = b_ref[...].T
     high = b.astype(jnp.bfloat16)
     low = (b - high.astype(jnp.float32)).astype(jnp.bfloat16)
-    both = jnp.concatenate([high, low], axis=1)
-    one = jnp.dot(high_ref[...], both, preferred_element_type=jnp.float32)
-    two = jnp.dot(low_ref[...], high, preferred_element_type=jnp.float32)
-    out_ref[...] = one[:, :K] + (one[:, K:] + two)
-
-
-def weigh(high, low, buffer):
+    both = jnp.concatenate([high, low], axis=0)
+    for n in range(WEIGH_PARTS):
+        copy(n).wait()
+        r = r_ref[n]
+        r_high = r.astype(jnp.bfloat16)
+        r_low = (r - r_high.astype(jnp.float32)).astype(jnp.bfloat16)
+        one = jnp.dot(both, r_high, preferred_element_type=jnp.float32)
+        two = jnp.dot(high, r_low, preferred_element_type=jnp.float32)
+        out_ref[n * width:(n + 1) * width, :] = (one[:K] + (one[K:] + two)).T
+
+
+def weigh(buffer, r):
     return pl.pallas_call(
         weigh_kernel,
-        in_specs=[vmem_spec()] * 3,
+        in_specs=[vmem_spec(), hbm_spec()],
         out_specs=vmem_spec(),
         out_shape=f32(PLACES, K),
+        scratch_shapes=[
+            pltpu.VMEM((WEIGH_PARTS, PLACES, PLACES // WEIGH_PARTS), jnp.float32),
+            pltpu.SemaphoreType.DMA((WEIGH_PARTS,)),
+        ],
         compiler_params=pltpu.CompilerParams(vmem_limit_bytes=12 * 1024 * 1024),
         name="weigh",
-    )(high, low, buffer)
+    )(buffer, in_hbm(r))
 
 
 def spread_kernel(flags, cell_ref, place_ref, count_ref, ret_ref, field, pay_a, pay_b, own_a, own_b):
@@ -363,7 +417,7 @@
         spread_kernel,
         in_specs=[smem_spec()] * 4 + [vmem_spec()],
         out_specs=[vmem_spec()] * 5,
-        out_shape=[f32(NROW + 16, K), f32(H * C, K), f32(H * C, K), f32(R * H, K), f32(R * H, K)],
+        out_shape=[held(NROW + 16, K), f32(H * C, K), f32(H * C, K), held(R * H, K), held(R * H, K)],
         compiler_params=pltpu.CompilerParams(vmem_limit_bytes=10 * 1024 * 1024),
         name="spread",
     )(flags, cell, place, count, returned)
@@ -429,7 +483,7 @@
         ],
         compiler_params=params(),
         name="finish",
-    )(flags, field, kap, act, *halos, probes)
+    )(flags, *in_vmem(field, kap, act), *halos, in_hbm(probes))
 
 
 def pairs(size, first):
@@ -465,25 +519,16 @@
     ]).astype(jnp.int32)
     lat_a, lat_b = swap(*edge_pack(flags, sweep_counts, kappa, probes), "lat")
     y, own_a, own_b = turn(flags, kappa, probes)
-    high, low = split(r_inv[0, 0])
-    halos = (lat_a, lat_b) + swap(*corner(flags, own_a, own_b, lat_a, lat_b), "lon")
-
     count = obs_count.reshape(1)
-    slot_ids = jnp.arange(SLOTS, dtype=jnp.int32)
-    is_live = slot_ids < count
-    owner_ids = obs_owner[:, 0]
-    owner_hit = (
-        (owner_ids[:, None] == jnp.arange(n_lon, dtype=jnp.int32)[None, :]) & is_live[:, None]
-    ).astype(jnp.int32)
-    slot_rank = jnp.sum(jnp.cumsum(owner_hit, axis=0) * owner_hit, axis=1) - 1
-    place = jnp.where(is_live, owner_ids * CAP + slot_rank, PLACES)
-    cell = OFF + (obs_cell // C + H) * CB + 8 + obs_cell % C
-
-    outgoing, kap, act = smooth(flags, sweep_counts, cell, place, y, kappa, halos)
+    cell, place = places(count, obs_cell, obs_owner.reshape(1, SLOTS))
+    lon_a, lon_b = swap(*corner(flags, own_a, own_b, lat_a, lat_b), "lon")
+    kap, act = coeffs(flags, sweep_counts, kappa, lat_a[H * C:], lat_b[H * C:], lon_a, lon_b, count)
+    outgoing, tail_a, tail_b = smooth(flags, cell, place, y, kap, act, (lat_a, lat_b, lon_a, lon_b))
     buffer = lax.all_to_all(outgoing, "lon", split_axis=0, concat_axis=0, tiled=True)
-    mixed = weigh(high, low, buffer)
+    mixed = weigh(buffer, r_inv[0, 0])
     returned = lax.all_to_all(mixed, "lon", split_axis=0, concat_axis=0, tiled=True)
     field, pay_a, pay_b, own_a, own_b = spread(flags, cell, place, count, returned)
+    kap, act = coeffs(flags, sweep_counts, kappa, tail_a, tail_b, lon_a, lon_b, pay_a)
     lat_a, lat_b = swap(pay_a, pay_b, "lat")
     back = (lat_a, lat_b) + swap(*corner(flags, own_a, own_b, lat_a, lat_b), "lon")
     sketch, gram = finish(flags, field, kap, act, back, probes)

time: 156 us -> 138 us (0.88)
  local copies, waits for them, and re-layouts: 22.5 us -> 2.17 us
  blocking collectives: 12.6 us -> 26.5 us
  Pallas kernels: 32.7 us -> 41.1 us
  waiting for transfers between devices: 34.1 us -> 27 us
  other arithmetic: 19.7 us -> 13.2 us
  starting transfers between devices: 32.5 us -> 26.3 us
    unnamed x45 -> x13, local copies, waits for them, and re-layouts: 21.6 us -> 2.16 us
    all_to_all x0 -> x1, blocking collectives: none -> 13.9 us  [shards(): lax.all_to_all(outgoing, 'lon', split_axis=0, concat_axis=0, tiled=True)]
    pallas_call x3 -> x5, Pallas kernels: 11.3 us -> 19.7 us  [the longest x1 8.43 us: smooth(): pl.pallas_call(smooth_kernel, in_specs=[smem_spec()] * 3 + [vmem_spec()]...]
    all_to_all x1 -> x0, waiting for transfers between devices: 6.36 us -> none  [shards(): lax.all_to_all(outgoing, 'lon', split_axis=0, concat_axis=0, tiled=True)]
    all_to_all x1 -> x0, starting transfers between devices: 6.23 us -> none  [shards(): lax.all_to_all(outgoing, 'lon', split_axis=0, concat_axis=0, tiled=True)]
    another operation x2 -> x0, other arithmetic: 3.17 us -> none
    ppermute x4, waiting for transfers between devices: 2.83 us -> 0.01 us  [swap(): lax.ppermute(a, axis, pairs(size, 0))]
  transfers between devices with their start and end apart: 19 -> 18, of which waited for: 14 -> 11; matrix products, arithmetic and copies ran while one was open for 5% -> 0% of each run, Pallas kernels for 2% -> 7%
where the time goes in v2:
time: 138 us
  Pallas kernels  41.1 us (30%)
  waiting for transfers between devices  27 us (20%)
  blocking collectives  26.5 us (19%)
  starting transfers between devices  26.3 us (19%)
  other arithmetic  13.2 us (10%)
  local copies, waits for them, and re-layouts  2.17 us (2%)
  between operations  1.54 us (1%)
    ppermute x4, waiting for transfers between devices, swap(): lax.ppermute(b, axis, pairs(size, 1))  15.7 us
    all_to_all x1, blocking collectives, shards(): lax.all_to_all(outgoing, 'lon', split_axis=0, concat_axis=0, tiled=True)  13.9 us
    all_to_all x1, blocking collectives, shards(): lax.all_to_all(mixed, 'lon', split_axis=0, concat_axis=0, tiled=True)  12.6 us
    ppermute x10, starting transfers between devices, stage(): got = [lax.ppermute(x, axis, p) for p in perms]  12.6 us
    another operation x3, other arithmetic, shards(): jnp.linalg.cholesky(sum_everywhere(gram) / cells_all, symmetrize_input=Fa...  12.4 us
    pallas_call x1, Pallas kernels, finish(): pl.pallas_call(finish_kernel, in_specs=[smem_spec()] + [vmem_spec()] * 7...  11.6 us
    ppermute x10, waiting for transfers between devices, stage(): got = [lax.ppermute(x, axis, p) for p in perms]  11.2 us
    ppermute x4, starting transfers between devices, swap(): lax.ppermute(b, axis, pairs(size, 1))  11 us
  transfers between devices with their start and end apart: 18, of which 11 were waited for; matrix products, arithmetic and copies ran while one was open for 0% of the time, Pallas kernels for 7%

profile of v2, /device:TPU:0, one launch (start us, length us, event | category | flops | bytes accessed | tf_op | source)
XLA Modules:
  0.0 137.8 jit_solution(185498079999847169)
XLA Ops:
  2.2 2.3 %edge_pack.1 = (f32[1040,128]{1,0:T(8,128)S(1)}, f32[1040,128]{1,0:T(8,128)S(1)}) custom-call(s32[4]{0:T(128)S(1)} %pad_add_fusion.flags, s32[32]{0:T(128)S(1)} %copy-done.2, f32[32,256]{1,0:T(8,128)S(1)} %copy-done, f32[128,32,256]{2,1,0:T(8,128)} %p_hbm.5), custom_call_target="tpu_custom_call" | custom-call | tf_op jit(solution)/shard_map/edge_pack/pallas_call | solution.py:97
  4.5 3.2 %collective-permute-start.1 = (f32[1040,128]{1,0:T(8,128)S(1)}, f32[1040,128]{1,0:T(8,128)S(1)}, u32[]{:S(2)}, u32[]{:S(2)}) collective-permute-start(f32[1040,128]{1,0:T(8,128)S(1)} %get-tuple-element.31), channel_id=1, source_target_pairs={{0,112},{16,32},{32,16},{48,64},{64,48},{80,96},{96,80},{112,0},{1... | collective-permute-start | bytes 1597448 | tf_op jit(solution)/shard_map/ppermute | solution.py:495
  7.7 3.3 %turn.1 = (f32[32,256,128]{2,1,0:T(8,128)S(1)}, f32[160,128]{1,0:T(8,128)S(1)}, f32[160,128]{1,0:T(8,128)S(1)}) custom-call(s32[4]{0:T(128)S(1)} %pad_add_fusion.flags, f32[32,256]{1,0:T(8,128)S(1)} %copy-done.1, f32[128,32,256]{2,1,0:T(8,128)} %p_hbm.5), custom_call_target="tpu_custom_call" | custom-call | bytes 12582912 | tf_op jit(solution)/shard_map/turn/pallas_call | solution.py:133
  11.0 3.6 %collective-permute-done.1.lat_b = f32[1040,128]{1,0:T(8,128)S(1)} collective-permute-done((f32[1040,128]{1,0:T(8,128)S(1)}, f32[1040,128]{1,0:T(8,128)S(1)}, u32[]{:S(2)}, u32[]{:S(2)}) %collective-permute-start.1) | collective-permute-done | bytes 532512 | tf_op jit(solution)/shard_map/ppermute | solution.py:495
  15.2 2.0 %collective-permute-start.2 = (f32[200,128]{1,0:T(8,128)S(1)}, f32[200,128]{1,0:T(8,128)S(1)}, u32[]{:S(2)}, u32[]{:S(2)}) collective-permute-start(f32[200,128]{1,0:T(8,128)S(1)} %get-tuple-element.34), channel_id=1, source_target_pairs={{0,1},{1,0},{2,3},{3,2},{4,5},{5,4},{6,7},{7,6},{8,9},{9,8},{10,11... | collective-permute-start | bytes 307208 | tf_op jit(solution)/shard_map/ppermute | solution.py:495
  17.2 4.7 %collective-permute-start.3 = (f32[200,128]{1,0:T(8,128)S(1)}, f32[200,128]{1,0:T(8,128)S(1)}, u32[]{:S(2)}, u32[]{:S(2)}) collective-permute-start(f32[200,128]{1,0:T(8,128)S(1)} %get-tuple-element.35), channel_id=1, source_target_pairs={{0,15},{1,2},{2,1},{3,4},{4,3},{5,6},{6,5},{7,8},{8,7},{9,10},{10,... | collective-permute-start | bytes 307208 | tf_op jit(solution)/shard_map/ppermute | solution.py:495
  22.6 3.7 %places.1 = (s32[384]{0:T(512)S(1)}, s32[384]{0:T(512)S(1)}) custom-call(s32[1]{0:T(128)} %bitcast.13.count_ref, s32[384]{0:T(512)S(1)} %copy-done.4, s32[1,384]{1,0:T(1,128)S(1)} %bitcast.20), custom_call_target="tpu_custom_call" | custom-call | bytes 4194304 | tf_op jit(solution)/shard_map/places/pallas_call | solution.py:306
  26.4 2.4 %coeffs.2 = (f32[10896,128]{1,0:T(8,128)S(1)}, f32[4,40,8,128]{3,2,1,0:T(8,128)S(1)}) custom-call(s32[4]{0:T(128)S(1)} %pad_add_fusion.flags, s32[32]{0:T(128)S(1)} %copy-done.3, f32[32,256]{1,0:T(8,128)S(1)} %copy-done.1, f32[16,128]{1,0:T(8,128)S(1)} %slice.14.tail_a, f32[16,128]{1,0:T(8,128)S(1)} %slice.15.tail_b, ...), custom_call_target="tpu_custom_call" | custom-call | bytes 4194304 | tf_op jit(solution)/shard_map/coeffs/pallas_call | solution.py:276
  28.8 8.4 %smooth.1 = (f32[768,128]{1,0:T(8,128)S(1)}, f32[16,128]{1,0:T(8,128)S(1)}, f32[16,128]{1,0:T(8,128)S(1)}) custom-call(s32[4]{0:T(128)S(1)} %pad_add_fusion.flags, s32[384]{0:T(512)S(1)} %get-tuple-element.27.cell_ref, s32[384]{0:T(512)S(1)} %get-tuple-element.28.place_ref, f32[32,256,128]{2,1,0:T(8,128)S(1)} %get-tuple-element.29.y_ref, ...), custom_call_target="tpu_custom_call" | custom-call | tf_op jit(solution)/shard_map/smooth/pallas_call | solution.py:341
  37.3 13.9 %all_to_all.22 = f32[16,48,128]{2,1,0:T(8,128)S(1)} all-to-all(f32[16,48,128]{2,1,0:T(8,128)S(1)} %bitcast.19), channel_id=1, replica_groups=mesh['lat'=8,'lon'=16] {'lon'}, dimensions={0} | all-to-all | bytes 786432 | tf_op jit(solution)/shard_map/all_to_all | solution.py:527
  51.1 2.7 %weigh.1 = f32[768,128]{1,0:T(8,128)S(1)} custom-call(f32[768,128]{1,0:T(8,128)S(1)} %bitcast.17, f32[768,768]{1,0:T(8,128)} %bitcast.21), custom_call_target="tpu_custom_call" | custom-call | tf_op jit(solution)/shard_map/weigh/pallas_call | solution.py:379
  53.8 12.6 %all_to_all.23 = f32[16,48,128]{2,1,0:T(8,128)S(1)} all-to-all(f32[16,48,128]{2,1,0:T(8,128)S(1)} %bitcast.18), channel_id=1, replica_groups=mesh['lat'=8,'lon'=16] {'lon'}, dimensions={0} | all-to-all | bytes 786432 | tf_op jit(solution)/shard_map/all_to_all | solution.py:529
  66.5 3.1 %spread.1 = (f32[10896,128]{1,0:T(8,128)S(1)}, f32[1024,128]{1,0:T(8,128)S(1)}, f32[1024,128]{1,0:T(8,128)S(1)}, f32[128,128]{1,0:T(8,128)S(1)}, f32[128,128]{1,0:T(8,128)S(1)}) custom-call(s32[4]{0:T(128)S(1)} %pad_add_fusion.flags, s32[384]{0:T(512)S(1)} %get-tuple-element.27.cell_ref, s32[384]{0:T(512)S(1)} %get-tuple-element.28.place_ref, ...), custom_call_target="tpu_custom_call" | custom-call | tf_op jit(solution)/shard_map/spread/pallas_call | solution.py:416
  70.6 9.0 %collective-permute-done.5.lat_b = f32[1024,128]{1,0:T(8,128)S(1)} collective-permute-done((f32[1024,128]{1,0:T(8,128)S(1)}, f32[1024,128]{1,0:T(8,128)S(1)}, u32[]{:S(2)}, u32[]{:S(2)}) %collective-permute-start.5) | collective-permute-done | bytes 524320 | tf_op jit(solution)/shard_map/ppermute | solution.py:495
  80.7 2.2 %collective-permute-start.7 = (f32[160,128]{1,0:T(8,128)S(1)}, f32[160,128]{1,0:T(8,128)S(1)}, u32[]{:S(2)}, u32[]{:S(2)}) collective-permute-start(f32[160,128]{1,0:T(8,128)S(1)} %get-tuple-element.49), channel_id=1, source_target_pairs={{0,15},{1,2},{2,1},{3,4},{4,3},{5,6},{6,5},{7,8},{8,7},{9,10},{10,... | collective-permute-start | bytes 245768 | tf_op jit(solution)/shard_map/ppermute | solution.py:495
  82.9 2.4 %coeffs.3 = (f32[10896,128]{1,0:T(8,128)S(1)}, f32[4,40,8,128]{3,2,1,0:T(8,128)S(1)}) custom-call(s32[4]{0:T(128)S(1)} %pad_add_fusion.flags, s32[32]{0:T(128)S(1)} %copy-done.3, f32[32,256]{1,0:T(8,128)S(1)} %copy-done.1, f32[16,128]{1,0:T(8,128)S(1)} %get-tuple-element.40.tail_a, f32[16,128]{1,0:T(8,128)S(1)} %get-tuple-element.41.tail_b, ...), custom_call_target="tpu_custom_call" | custom-call | bytes 4194304 | tf_op jit(solution)/shard_map/coeffs/pallas_call | solution.py:276
  85.3 3.2 %collective-permute-done.7.lon_b = f32[160,128]{1,0:T(8,128)S(1)} collective-permute-done((f32[160,128]{1,0:T(8,128)S(1)}, f32[160,128]{1,0:T(8,128)S(1)}, u32[]{:S(2)}, u32[]{:S(2)}) %collective-permute-start.7) | collective-permute-done | bytes 81952 | tf_op jit(solution)/shard_map/ppermute | solution.py:495
  88.5 11.6 %finish.1 = (f32[128,32,256]{2,1,0:T(8,128)}, f32[128,128]{1,0:T(8,128)S(1)}) custom-call(s32[4]{0:T(128)S(1)} %pad_add_fusion.flags, f32[10896,128]{1,0:T(8,128)S(1)} %get-tuple-element.39.field, f32[10896,128]{1,0:T(8,128)S(1)} %get-tuple-element.43.kap, f32[4,40,8,128]{3,2,1,0:T(8,128)S(1)} %get-tuple-element.44.act, ...), custom_call_target="tpu_custom_call" | custom-call | tf_op jit(solution)/shard_map/finish/pallas_call | solution.py:472
  101.5 2.1 %collective-permute-start.11 = (f32[128,128]{1,0:T(8,128)S(1)}, f32[128,128]{1,0:T(8,128)S(1)}, u32[]{:S(2)}, u32[]{:S(2)}) collective-permute-start(f32[128,128]{1,0:T(8,128)S(1)} %add.44), channel_id=1, source_target_pairs={{0,96},{16,112},{32,64},{48,80},{64,32},{80,48},{96,0},{112,16},{1... | collective-permute-start | bytes 196616 | tf_op jit(solution)/shard_map/ppermute | solution.py:502
  103.6 2.1 %collective-permute-start.9 = (f32[128,128]{1,0:T(8,128)S(1)}, f32[128,128]{1,0:T(8,128)S(1)}, u32[]{:S(2)}, u32[]{:S(2)}) collective-permute-start(f32[128,128]{1,0:T(8,128)S(1)} %add.44), channel_id=1, source_target_pairs={{0,32},{16,48},{32,0},{48,16},{64,96},{80,112},{96,64},{112,80},{1... | collective-permute-start | bytes 196616 | tf_op jit(solution)/shard_map/ppermute | solution.py:502
  107.0 2.6 %collective-permute-done.10 = f32[128,128]{1,0:T(8,128)S(1)} collective-permute-done((f32[128,128]{1,0:T(8,128)S(1)}, f32[128,128]{1,0:T(8,128)S(1)}, u32[]{:S(2)}, u32[]{:S(2)}) %collective-permute-start.10) | collective-permute-done | bytes 65568 | tf_op jit(solution)/shard_map/ppermute | solution.py:502
  110.2 3.6 %collective-permute-start.12 = (f32[128,128]{1,0:T(8,128)S(1)}, f32[128,128]{1,0:T(8,128)S(1)}, u32[]{:S(2)}, u32[]{:S(2)}) collective-permute-start(f32[128,128]{1,0:T(8,128)S(1)} %add_add_fusion.1), channel_id=1, source_target_pairs={{0,1},{1,0},{2,3},{3,2},{4,5},{5,4},{6,7},{7,6},{8,9},{9,8},{10,11... | collective-permute-start | bytes 196616 | tf_op jit(solution)/shard_map/ppermute | solution.py:502
  118.8 2.2 %collective-permute-start.15 = (f32[128,128]{1,0:T(8,128)S(1)}, f32[128,128]{1,0:T(8,128)S(1)}, u32[]{:S(2)}, u32[]{:S(2)}) collective-permute-start(f32[128,128]{1,0:T(8,128)S(1)} %add_add_fusion), channel_id=1, source_target_pairs={{0,4},{1,5},{2,6},{3,7},{4,0},{5,1},{6,2},{7,3},{8,12},{9,13},{10,... | collective-permute-start | bytes 196616 | tf_op jit(solution)/shard_map/ppermute | solution.py:502
  124.0 11.7 %cholesky.18 = f32[128,128]{1,0:T(8,128)S(1)} custom-call(f32[128,128]{1,0:T(8,128)S(1)} %add_multiply_fusion), custom_call_target="Cholesky" | custom-call | tf_op jit(solution)/shard_map/jit(cholesky)/cholesky | solution.py:536
  (49 shorter events, 17.7 us)
Async XLA Ops:
  0.6 7.1 %copy-start.1 = (f32[32,256]{1,0:T(8,128)S(1)}, f32[32,256]{1,0:T(8,128)}, u32[]{:S(2)}) copy-start(f32[32,256]{1,0:T(8,128)} %kappa_ref.7) | copy-start | bytes 98308
  0.7 0.8 copy-start
  1.5 0.7 copy-start.2
  2.2 20.5 %copy-start.4 = (s32[384]{0:T(512)S(1)}, s32[384]{0:T(512)}, u32[]{:S(2)}) copy-start(s32[384]{0:T(512)} %cell_ref.1) | copy-start | bytes 4612
  2.2 20.5 %copy-start.5 = (s32[384,1]{0,1:T(1,128)S(1)}, s32[384,1]{0,1:T(1,128)}, u32[]{:S(2)}) copy-start(s32[384,1]{0,1:T(1,128)} %param.11) | copy-start | bytes 4612
  2.2 24.2 %copy-start.3 = (s32[32]{0:T(128)S(1)}, s32[32]{0:T(128)}, u32[]{:S(2)}) copy-start(s32[32]{0:T(128)} %counts.5) | copy-start | bytes 388
  4.4 6.6 %collective-permute-start = (f32[1040,128]{1,0:T(8,128)S(1)}, f32[1040,128]{1,0:T(8,128)S(1)}, u32[]{:S(2)}, u32[]{:S(2)}) collective-permute-start(f32[1040,128]{1,0:T(8,128)S(1)} %get-tuple-element.30), channel_id=1, source_target_pairs={{0,16},{16,0},{32,48},{48,32},{64,80},{80,64},{96,112},{112,96},{1... | collective-permute-start | bytes 1597448 | tf_op jit(solution)/shard_map/ppermute | solution.py:495
  4.5 10.2 %collective-permute-start.1 = (f32[1040,128]{1,0:T(8,128)S(1)}, f32[1040,128]{1,0:T(8,128)S(1)}, u32[]{:S(2)}, u32[]{:S(2)}) collective-permute-start(f32[1040,128]{1,0:T(8,128)S(1)} %get-tuple-element.31), channel_id=1, source_target_pairs={{0,112},{16,32},{32,16},{48,64},{64,48},{80,96},{96,80},{112,0},{1... | collective-permute-start | bytes 1597448 | tf_op jit(solution)/shard_map/ppermute | solution.py:495
  15.2 11.1 %collective-permute-start.2 = (f32[200,128]{1,0:T(8,128)S(1)}, f32[200,128]{1,0:T(8,128)S(1)}, u32[]{:S(2)}, u32[]{:S(2)}) collective-permute-start(f32[200,128]{1,0:T(8,128)S(1)} %get-tuple-element.34), channel_id=1, source_target_pairs={{0,1},{1,0},{2,3},{3,2},{4,5},{5,4},{6,7},{7,6},{8,9},{9,8},{10,11... | collective-permute-start | bytes 307208 | tf_op jit(solution)/shard_map/ppermute | solution.py:495
  17.2 9.1 %collective-permute-start.3 = (f32[200,128]{1,0:T(8,128)S(1)}, f32[200,128]{1,0:T(8,128)S(1)}, u32[]{:S(2)}, u32[]{:S(2)}) collective-permute-start(f32[200,128]{1,0:T(8,128)S(1)} %get-tuple-element.35), channel_id=1, source_target_pairs={{0,15},{1,2},{2,1},{3,4},{4,3},{5,6},{6,5},{7,8},{8,7},{9,10},{10,... | collective-permute-start | bytes 307208 | tf_op jit(solution)/shard_map/ppermute | solution.py:495
  69.6 9.9 %collective-permute-start.5 = (f32[1024,128]{1,0:T(8,128)S(1)}, f32[1024,128]{1,0:T(8,128)S(1)}, u32[]{:S(2)}, u32[]{:S(2)}) collective-permute-start(f32[1024,128]{1,0:T(8,128)S(1)} %get-tuple-element.45), channel_id=1, source_target_pairs={{0,112},{16,32},{32,16},{48,64},{64,48},{80,96},{96,80},{112,0},{1... | collective-permute-start | bytes 1572872 | tf_op jit(solution)/shard_map/ppermute | solution.py:495
  70.5 9.0 %collective-permute-start.4 = (f32[1024,128]{1,0:T(8,128)S(1)}, f32[1024,128]{1,0:T(8,128)S(1)}, u32[]{:S(2)}, u32[]{:S(2)}) collective-permute-start(f32[1024,128]{1,0:T(8,128)S(1)} %get-tuple-element.42.after), channel_id=1, source_target_pairs={{0,16},{16,0},{32,48},{48,32},{64,80},{80,64},{96,112},{112,96},{1... | collective-permute-start | bytes 1572872 | tf_op jit(solution)/shard_map/ppermute | solution.py:495
  80.1 5.2 %collective-permute-start.6 = (f32[160,128]{1,0:T(8,128)S(1)}, f32[160,128]{1,0:T(8,128)S(1)}, u32[]{:S(2)}, u32[]{:S(2)}) collective-permute-start(f32[160,128]{1,0:T(8,128)S(1)} %get-tuple-element.48), channel_id=1, source_target_pairs={{0,1},{1,0},{2,3},{3,2},{4,5},{5,4},{6,7},{7,6},{8,9},{9,8},{10,11... | collective-permute-start | bytes 245768 | tf_op jit(solution)/shard_map/ppermute | solution.py:495
  80.7 7.8 %collective-permute-start.7 = (f32[160,128]{1,0:T(8,128)S(1)}, f32[160,128]{1,0:T(8,128)S(1)}, u32[]{:S(2)}, u32[]{:S(2)}) collective-permute-start(f32[160,128]{1,0:T(8,128)S(1)} %get-tuple-element.49), channel_id=1, source_target_pairs={{0,15},{1,2},{2,1},{3,4},{4,3},{5,6},{6,5},{7,8},{8,7},{9,10},{10,... | collective-permute-start | bytes 245768 | tf_op jit(solution)/shard_map/ppermute | solution.py:495
  100.1 1.3 collective-permute-start.8
  101.5 5.6 %collective-permute-start.11 = (f32[128,128]{1,0:T(8,128)S(1)}, f32[128,128]{1,0:T(8,128)S(1)}, u32[]{:S(2)}, u32[]{:S(2)}) collective-permute-start(f32[128,128]{1,0:T(8,128)S(1)} %add.44), channel_id=1, source_target_pairs={{0,96},{16,112},{32,64},{48,80},{64,32},{80,48},{96,0},{112,16},{1... | collective-permute-start | bytes 196616 | tf_op jit(solution)/shard_map/ppermute | solution.py:502
  103.6 6.1 %collective-permute-start.10 = (f32[128,128]{1,0:T(8,128)S(1)}, f32[128,128]{1,0:T(8,128)S(1)}, u32[]{:S(2)}, u32[]{:S(2)}) collective-permute-start(f32[128,128]{1,0:T(8,128)S(1)} %add.44), channel_id=1, source_target_pairs={{0,64},{16,80},{32,96},{48,112},{64,0},{80,16},{96,32},{112,48},{1... | collective-permute-start | bytes 196616 | tf_op jit(solution)/shard_map/ppermute | solution.py:502
  103.6 6.1 %collective-permute-start.9 = (f32[128,128]{1,0:T(8,128)S(1)}, f32[128,128]{1,0:T(8,128)S(1)}, u32[]{:S(2)}, u32[]{:S(2)}) collective-permute-start(f32[128,128]{1,0:T(8,128)S(1)} %add.44), channel_id=1, source_target_pairs={{0,32},{16,48},{32,0},{48,16},{64,96},{80,112},{96,64},{112,80},{1... | collective-permute-start | bytes 196616 | tf_op jit(solution)/shard_map/ppermute | solution.py:502
  109.7 5.6 %collective-permute-start.14 = (f32[128,128]{1,0:T(8,128)S(1)}, f32[128,128]{1,0:T(8,128)S(1)}, u32[]{:S(2)}, u32[]{:S(2)}) collective-permute-start(f32[128,128]{1,0:T(8,128)S(1)} %add_add_fusion.1), channel_id=1, source_target_pairs={{0,3},{1,2},{2,1},{3,0},{4,7},{5,6},{6,5},{7,4},{8,11},{9,10},{10,... | collective-permute-start | bytes 196616 | tf_op jit(solution)/shard_map/ppermute | solution.py:502
  110.0 5.9 %collective-permute-start.13 = (f32[128,128]{1,0:T(8,128)S(1)}, f32[128,128]{1,0:T(8,128)S(1)}, u32[]{:S(2)}, u32[]{:S(2)}) collective-permute-start(f32[128,128]{1,0:T(8,128)S(1)} %add_add_fusion.1), channel_id=1, source_target_pairs={{0,2},{1,3},{2,0},{3,1},{4,6},{5,7},{6,4},{7,5},{8,10},{9,11},{10,... | collective-permute-start | bytes 196616 | tf_op jit(solution)/shard_map/ppermute | solution.py:502
  110.2 6.6 %collective-permute-start.12 = (f32[128,128]{1,0:T(8,128)S(1)}, f32[128,128]{1,0:T(8,128)S(1)}, u32[]{:S(2)}, u32[]{:S(2)}) collective-permute-start(f32[128,128]{1,0:T(8,128)S(1)} %add_add_fusion.1), channel_id=1, source_target_pairs={{0,1},{1,0},{2,3},{3,2},{4,5},{5,4},{6,7},{7,6},{8,9},{9,8},{10,11... | collective-permute-start | bytes 196616 | tf_op jit(solution)/shard_map/ppermute | solution.py:502
  116.8 5.6 %collective-permute-start.17 = (f32[128,128]{1,0:T(8,128)S(1)}, f32[128,128]{1,0:T(8,128)S(1)}, u32[]{:S(2)}, u32[]{:S(2)}) collective-permute-start(f32[128,128]{1,0:T(8,128)S(1)} %add_add_fusion), channel_id=1, source_target_pairs={{0,12},{1,13},{2,14},{3,15},{4,8},{5,9},{6,10},{7,11},{8,4},{9,5},... | collective-permute-start | bytes 196616 | tf_op jit(solution)/shard_map/ppermute | solution.py:502
  118.3 5.8 %collective-permute-start.16 = (f32[128,128]{1,0:T(8,128)S(1)}, f32[128,128]{1,0:T(8,128)S(1)}, u32[]{:S(2)}, u32[]{:S(2)}) collective-permute-start(f32[128,128]{1,0:T(8,128)S(1)} %add_add_fusion), channel_id=1, source_target_pairs={{0,8},{1,9},{2,10},{3,11},{4,12},{5,13},{6,14},{7,15},{8,0},{9,1},... | collective-permute-start | bytes 196616 | tf_op jit(solution)/shard_map/ppermute | solution.py:502
  118.8 5.2 %collective-permute-start.15 = (f32[128,128]{1,0:T(8,128)S(1)}, f32[128,128]{1,0:T(8,128)S(1)}, u32[]{:S(2)}, u32[]{:S(2)}) collective-permute-start(f32[128,128]{1,0:T(8,128)S(1)} %add_add_fusion), channel_id=1, source_target_pairs={{0,4},{1,5},{2,6},{3,7},{4,0},{5,1},{6,2},{7,3},{8,12},{9,13},{10,... | collective-permute-start | bytes 196616 | tf_op jit(solution)/shard_map/ppermute | solution.py:502

commit v3 on v2

--- a/solution.py
+++ b/solution.py
@@ -25,6 +25,8 @@
 OWN_ROWS = R * H + R
 LON_OWNERS = 16
 WEIGH_PARTS = 3
+HALF = 64
+EXACT = False
 
 
 def vmem_spec():
@@ -63,8 +65,8 @@
     return OFF + r * CB + c
 
 
-def edge_pack_kernel(flags, counts, kappa_ref, p_hbm, pay_a, pay_b, chunk, sems):
-    odd = flags[0]
+def edge_pack_kernel(counts_hbm, kappa_hbm, p_hbm, pay_a, pay_b, chunk, kappa_ref, counts, sems):
+    odd = lax.axis_index("lat") % 2
     first = (jnp.where(odd == 1, 0, R - H), jnp.where(odd == 1, R - H, 0))
     copies = []
     for side in range(2):
@@ -73,7 +75,12 @@
             n = side * 2 + half
             copies.append(pltpu.make_async_copy(
                 p_hbm.at[:, pl.ds(block, 8), pl.ds(half * LANES, LANES)], chunk.at[n], sems.at[n]))
-            copies[-1].start()
+    small = [pltpu.make_async_copy(kappa_hbm, kappa_ref, sems.at[4]),
+             pltpu.make_async_copy(counts_hbm, counts, sems.at[5])]
+    for copy in small + copies:
+        copy.start()
+    for copy in small:
+        copy.wait()
     flat = chunk.reshape(4 * K * 8, LANES)
     for side, pay in ((0, pay_a), (1, pay_b)):
         within = jnp.where(first[side] == 0, 0, 8 - H)
@@ -93,16 +100,21 @@
                     pl.ds(n * K * 8 + within + r, K, stride=8), :].T
 
 
-def edge_pack(flags, counts, kappa, probes):
+def edge_pack(counts, kappa, probes):
     return pl.pallas_call(
         edge_pack_kernel,
-        in_specs=[smem_spec(), smem_spec(), vmem_spec(), hbm_spec()],
+        in_specs=[hbm_spec()] * 3,
         out_specs=[vmem_spec()] * 2,
         out_shape=[f32(LAT_ROWS, K)] * 2,
-        scratch_shapes=[pltpu.VMEM((4, K, 8, LANES), jnp.float32), pltpu.SemaphoreType.DMA((4,))],
+        scratch_shapes=[
+            pltpu.VMEM((4, K, 8, LANES), jnp.float32),
+            pltpu.VMEM((R, C), jnp.float32),
+            pltpu.SMEM((R,), jnp.int32),
+            pltpu.SemaphoreType.DMA((6,)),
+        ],
         compiler_params=pltpu.CompilerParams(vmem_limit_bytes=8 * 1024 * 1024),
         name="edge_pack",
-    )(flags, counts, kappa, in_hbm(probes))
+    )(in_hbm(counts), in_hbm(kappa), in_hbm(probes))
 
 
 def turn_kernel(flags, kappa_ref, p_hbm, y_ref, own_a, own_b, chunk, sems):
@@ -142,7 +154,7 @@
     )(flags, kappa, in_hbm(probes))
 
 
-def corner_kernel(flags, own_a, own_b, lat_a, lat_b, pay_a, pay_b):
+def corner_kernel(flags, own_a, own_b, lat_a, lat_b, after, pay_a, pay_b):
     odd = flags[2]
     own_rows = own_a.shape[0]
     for own, pay, low in ((own_a, pay_a, odd), (own_b, pay_b, 1 - odd)):
@@ -160,16 +172,16 @@
                     base += 1
 
 
-def corner(flags, own_a, own_b, lat_a, lat_b):
+def corner(flags, own_a, own_b, lat_a, lat_b, after):
     rows = own_a.shape[0] + 2 * H * H + (2 * H if own_a.shape[0] > R * H else 0)
     return pl.pallas_call(
         corner_kernel,
-        in_specs=[smem_spec()] + [vmem_spec()] * 4,
+        in_specs=[smem_spec()] + [vmem_spec()] * 4 + [pl.BlockSpec(memory_space=pl.ANY)],
         out_specs=[vmem_spec()] * 2,
         out_shape=[f32(rows, K)] * 2,
         compiler_params=pltpu.CompilerParams(vmem_limit_bytes=8 * 1024 * 1024),
         name="corner",
-    )(flags, *in_vmem(own_a, own_b), lat_a, lat_b)
+    )(flags, *in_vmem(own_a, own_b), lat_a, lat_b, after)
 
 
 def put_halos(buf, flags, lat_a, lat_b, lon_a, lon_b):
@@ -200,12 +212,11 @@
                 buf[pl.ds(start, H), :] = keep(lat_ok[n], keep(lon_ok[m], lon[part:part + H, :]))
 
 
-def coeffs_kernel(flags, counts, kappa_ref, tail_a, tail_b, lon_a, lon_b, after, kap, act):
+def coeffs_kernel(flags, counts, kappa_ref, tail_a, tail_b, after, *rest):
+    *lon, kap, act = rest
     odd = flags[0]
-    lon_odd = flags[2]
     lat_ok = (None, flags[1] == 1)
     lat_row = (jnp.where(odd == 1, 0, R + H), jnp.where(odd == 1, R + H, 0))
-    lon_col = (jnp.where(lon_odd == 1, 0, C + H), jnp.where(lon_odd == 1, C + H, 0))
     kap_t = kappa_ref[...].T
     for r in range(R):
         kap[pl.ds(at(r + H, 8), C), :] = jnp.broadcast_to(kap_t[:, r:r + 1], (C, K))
@@ -224,6 +235,16 @@
     for r in range(R):
         for s in range(SWEEPS):
             act[s, r + H] = jnp.full((8, K), jnp.where(counts[r] > s, 1.0, 0.0), jnp.float32)
+    if lon:
+        put_lon_kappa(kap, flags, *lon)
+
+
+def put_lon_kappa(kap, flags, lon_a, lon_b):
+    odd = flags[0]
+    lon_odd = flags[2]
+    lat_ok = (None, flags[1] == 1)
+    lat_row = (jnp.where(odd == 1, 0, R + H), jnp.where(odd == 1, R + H, 0))
+    lon_col = (jnp.where(lon_odd == 1, 0, C + H), jnp.where(lon_odd == 1, C + H, 0))
     for m, lon in ((0, lon_a), (1, lon_b)):
         src = (jnp.where(lon_odd == 1, LANES - H, 0), jnp.where(lon_odd == 1, 0, LANES - H))[m]
         own = lon[R * H:R * H + R, :].T
@@ -272,16 +293,16 @@
     lax.fori_loop(0, count // 2, body, 0)
 
 
-def coeffs(flags, counts, kappa, tail_a, tail_b, lon_a, lon_b, after):
+def coeffs(flags, counts, kappa, tail_a, tail_b, after, *lon):
     return pl.pallas_call(
         coeffs_kernel,
-        in_specs=[smem_spec()] * 2 + [vmem_spec()] * 5 + [pl.BlockSpec(memory_space=pl.ANY)],
+        in_specs=[smem_spec()] * 2 + [vmem_spec()] * 3 + [pl.BlockSpec(memory_space=pl.ANY)] + [vmem_spec()] * len(lon),
         out_specs=[vmem_spec()] * 2,
         out_shape=[held(NROW + 16, K), held(SWEEPS, RE, 8, K)],
         compiler_params=pltpu.CompilerParams(vmem_limit_bytes=8 * 1024 * 1024),
         cost_estimate=pl.CostEstimate(flops=0, bytes_accessed=4 * 1024 * 1024, transcendentals=0),
         name="coeffs",
-    )(flags, counts, kappa, tail_a, tail_b, lon_a, lon_b, after)
+    )(flags, counts, kappa, tail_a, tail_b, after, *lon)
 
 
 def places_kernel(count_ref, cell_ref, owner_ref, row_ref, place_ref, seen):
@@ -315,8 +336,9 @@
     )(count, cell, owner)
 
 
-def smooth_kernel(flags, cell_ref, place_ref, y_ref, kap, act, lat_a, lat_b, lon_a, lon_b,
-                  out_ref, tail_a, tail_b, buf_a, buf_b, rows_ref):
+def smooth_kernel(flags, cell_ref, place_ref, y_ref, kap_in, act, lat_a, lat_b, lon_a, lon_b,
+                  out_ref, tail_a, tail_b, kap, buf_a, buf_b, rows_ref):
+    put_lon_kappa(kap, flags, lon_a, lon_b)
     for r in range(R):
         buf_a[pl.ds(at(r + H, 8), C), :] = y_ref[r]
     put_halos(buf_a, flags, lat_a, lat_b, lon_a, lon_b)
@@ -341,8 +363,9 @@
     return pl.pallas_call(
         smooth_kernel,
         in_specs=[smem_spec()] * 3 + [vmem_spec()] * 7,
-        out_specs=[vmem_spec()] * 3,
-        out_shape=[f32(PLACES, K), f32(16, K), f32(16, K)],
+        out_specs=[vmem_spec()] * 4,
+        out_shape=[f32(PLACES, K), f32(16, K), f32(16, K), held(NROW + 16, K)],
+        input_output_aliases={4: 3},
         scratch_shapes=[
             pltpu.VMEM((NROW + 16, K), jnp.float32),
             pltpu.VMEM((NROW + 16, K), jnp.float32),
@@ -463,7 +486,13 @@
             hh = hh + lax.dot_general(high, high, contract, preferred_element_type=jnp.float32)
             hl = hl + lax.dot_general(high, low, contract, preferred_element_type=jnp.float32)
         copy_out(n).start()
-    gram_ref[...] = hh + (hl + hl.T)
+    gram = hh + (hl + hl.T)
+    top = gram[:HALF]
+    turned = pltpu.roll(gram[HALF:], HALF, 1)
+    row = lax.broadcasted_iota(jnp.int32, (HALF, K), 0)
+    lane = lax.broadcasted_iota(jnp.int32, (HALF, K), 1)
+    gram_ref[:HALF, :] = jnp.where((lane < HALF) & (row > lane), turned, top)
+    gram_ref[HALF:, :] = jnp.broadcast_to(jnp.sum(jnp.where(row == lane, turned, 0.0), axis=0, keepdims=True), (8, K))
     for n in range(8):
         copy_out(n).wait()
 
@@ -473,7 +502,7 @@
         finish_kernel,
         in_specs=[smem_spec()] + [vmem_spec()] * 7 + [hbm_spec()],
         out_specs=[hbm_spec(), vmem_spec()],
-        out_shape=[f32(K, R, C), f32(K, K)],
+        out_shape=[f32(K, R, C), f32(HALF + 8, K)],
         scratch_shapes=[
             pltpu.VMEM((NROW + 16, K), jnp.float32),
             pltpu.VMEM((NROW + 16, K), jnp.float32),
@@ -495,19 +524,66 @@
     return lax.ppermute(a, axis, pairs(size, 0)), lax.ppermute(b, axis, pairs(size, 1))
 
 
-def sum_everywhere(x):
-    n_lat, n_lon = lax.axis_size("lat"), lax.axis_size("lon")
-
-    def stage(x, axis, perms):
-        got = [lax.ppermute(x, axis, p) for p in perms]
-        for g in got:
-            x = x + g
-        return x
-
-    x = stage(x, "lat", [[(i, i ^ 1) for i in range(n_lat)]])
-    x = stage(x, "lat", [[(i, i ^ (2 * d)) for i in range(n_lat)] for d in (1, 2, 3)])
-    x = stage(x, "lon", [[(i, i ^ d) for i in range(n_lon)] for d in (1, 2, 3)])
-    return stage(x, "lon", [[(i, i ^ (4 * d)) for i in range(n_lon)] for d in (1, 2, 3)])
+def factor_kernel(scale, x_ref, g1_ref, g2_ref, g3_ref, out_ref, a_ref):
+    total = ((x_ref[...] + g1_ref[...]) + (g2_ref[...] + g3_ref[...])) * scale
+    top = total[:HALF]
+    a_ref[:HALF, :] = top
+    lower = top.T[:HALF]
+    row = lax.broadcasted_iota(jnp.int32, (HALF, HALF), 0)
+    lane = lax.broadcasted_iota(jnp.int32, (HALF, HALF), 1)
+    lower = jnp.where(row == lane, jnp.broadcast_to(total[HALF:HALF + 1, :HALF], (HALF, HALF)), lower)
+    a_ref[HALF:, :] = jnp.concatenate([jnp.zeros((HALF, HALF), jnp.float32), lower], axis=1)
+    sub = lax.broadcasted_iota(jnp.int32, (8, K), 0)
+    col = lax.broadcasted_iota(jnp.int32, (8, K), 1)
+    for q in range(K // 8):
+        c = 8 * q
+        panel = a_ref[c:c + 8, :]
+        if q > 0:
+            done = out_ref[:c, :]
+            panel = panel - lax.dot_general(
+                done[:, c:c + 8], done, (((0,), (0,)), ((), ())),
+                precision=lax.Precision.HIGHEST, preferred_element_type=jnp.float32)
+        b = [[jnp.broadcast_to(panel[i:i + 1, c + m:c + m + 1], (8, K)) if m >= i else None for m in range(8)]
+             for i in range(8)]
+        rows = [jnp.broadcast_to(panel[i:i + 1, :], (8, K)) for i in range(8)]
+        result = jnp.zeros((8, K), jnp.float32)
+        for i in range(8):
+            inv = 1.0 / jnp.sqrt(b[i][i]) if EXACT else lax.rsqrt(b[i][i])
+            u = [b[i][m] * inv if m > i else None for m in range(8)]
+            for m in range(i + 1, 8):
+                for k in range(m, 8):
+                    b[m][k] = b[m][k] - u[m] * u[k]
+            rows[i] = rows[i] * inv
+            for m in range(i + 1, 8):
+                rows[m] = rows[m] - u[m] * rows[i]
+            result = jnp.where(sub == i, rows[i], result)
+        out_ref[c:c + 8, :] = jnp.where(col >= sub + c, result, 0.0)
+
+
+def factor(scale, parts):
+    return pl.pallas_call(
+        functools.partial(factor_kernel, scale),
+        in_specs=[vmem_spec()] * 4,
+        out_specs=vmem_spec(),
+        out_shape=f32(K, K),
+        scratch_shapes=[pltpu.VMEM((K, K), jnp.float32)],
+        compiler_params=pltpu.CompilerParams(vmem_limit_bytes=8 * 1024 * 1024),
+        name="factor",
+    )(*parts)
+
+
+def gather_sums(x):
+    def stage(x, axis, steps):
+        size = lax.axis_size(axis)
+        return (x, *[lax.ppermute(x, axis, [(i, i ^ d) for i in range(size)]) for d in steps])
+
+    def total(x, g1, g2, g3):
+        return (x + g1) + (g2 + g3)
+
+    x, g1 = stage(x, "lat", (1,))
+    x = total(*stage(x + g1, "lat", (2, 4, 6)))
+    x = total(*stage(x, "lon", (1, 2, 3)))
+    return stage(x, "lon", (4, 8, 12))
 
 
 def shards(probes, kappa, sweep_counts, obs_cell, obs_owner, obs_count, r_inv):
@@ -517,23 +593,23 @@
         lat % 2, ((lat > 0) & (lat < n_lat - 1)).astype(jnp.int32),
         lon % 2, ((lon > 0) & (lon < n_lon - 1)).astype(jnp.int32),
     ]).astype(jnp.int32)
-    lat_a, lat_b = swap(*edge_pack(flags, sweep_counts, kappa, probes), "lat")
+    lat_a, lat_b = swap(*edge_pack(sweep_counts, kappa, probes), "lat")
     y, own_a, own_b = turn(flags, kappa, probes)
     count = obs_count.reshape(1)
     cell, place = places(count, obs_cell, obs_owner.reshape(1, SLOTS))
-    lon_a, lon_b = swap(*corner(flags, own_a, own_b, lat_a, lat_b), "lon")
-    kap, act = coeffs(flags, sweep_counts, kappa, lat_a[H * C:], lat_b[H * C:], lon_a, lon_b, count)
-    outgoing, tail_a, tail_b = smooth(flags, cell, place, y, kap, act, (lat_a, lat_b, lon_a, lon_b))
+    lon_a, lon_b = swap(*corner(flags, own_a, own_b, lat_a, lat_b, place), "lon")
+    kap, act = coeffs(flags, sweep_counts, kappa, lat_a[H * C:], lat_b[H * C:], count)
+    outgoing, tail_a, tail_b, _ = smooth(flags, cell, place, y, kap, act, (lat_a, lat_b, lon_a, lon_b))
     buffer = lax.all_to_all(outgoing, "lon", split_axis=0, concat_axis=0, tiled=True)
     mixed = weigh(buffer, r_inv[0, 0])
     returned = lax.all_to_all(mixed, "lon", split_axis=0, concat_axis=0, tiled=True)
     field, pay_a, pay_b, own_a, own_b = spread(flags, cell, place, count, returned)
-    kap, act = coeffs(flags, sweep_counts, kappa, tail_a, tail_b, lon_a, lon_b, pay_a)
+    kap, act = coeffs(flags, sweep_counts, kappa, tail_a, tail_b, pay_a, lon_a, lon_b)
     lat_a, lat_b = swap(pay_a, pay_b, "lat")
-    back = (lat_a, lat_b) + swap(*corner(flags, own_a, own_b, lat_a, lat_b), "lon")
+    back = (lat_a, lat_b) + swap(*corner(flags, own_a, own_b, lat_a, lat_b, act), "lon")
     sketch, gram = finish(flags, field, kap, act, back, probes)
     cells_all = R * C * n_lat * n_lon
-    r_factor = jnp.linalg.cholesky(sum_everywhere(gram) / cells_all, symmetrize_input=False).T
+    r_factor = factor(1.0 / cells_all, gather_sums(gram))
     return (sketch, r_factor)
 
 

time: 138 us -> 127 us (0.920)
  other arithmetic: 13.2 us -> 0.1 us
  Pallas kernels: 41.1 us -> 48.9 us
  waiting for transfers between devices: 27 us -> 22.1 us
  local copies, waits for them, and re-layouts: 2.17 us -> 0.78 us
    another operation x3 -> x0, other arithmetic: 12.4 us -> none  [shards(): jnp.linalg.cholesky(sum_everywhere(gram) / cells_all, symmetrize_input=Fa...]
    pallas_call x3 -> x4, Pallas kernels: 3.38 us -> 11 us  [the longest x1 8.09 us: factor(): pl.pallas_call(functools.partial(factor_kernel, scale), in_specs=[vmem_sp...]
    ppermute x4, waiting for transfers between devices: 15.7 us -> 11.1 us  [swap(): lax.ppermute(b, axis, pairs(size, 1))]
    ppermute x10, waiting for transfers between devices: 11.2 us -> 8.81 us  [stage(): lax.ppermute(x, axis, [(i, i ^ d) for i in range(size)])]
    ppermute x4, waiting for transfers between devices: 0.01 us -> 2.27 us  [swap(): lax.ppermute(a, axis, pairs(size, 0))]
    unnamed x13 -> x10, local copies, waits for them, and re-layouts: 2.16 us -> 0.78 us
  transfers between devices with their start and end apart: 18 -> 18, of which waited for: 11 -> 12; matrix products, arithmetic and copies ran while one was open for 0% -> 0% of each run, Pallas kernels for 7% -> 9%
where the time goes in v3:
time: 127 us
  Pallas kernels  48.9 us (39%)
  blocking collectives  27.7 us (22%)
  starting transfers between devices  25.8 us (20%)
  waiting for transfers between devices  22.1 us (17%)
  between operations  1.5 us (1%)
    all_to_all x1, blocking collectives, shards(): lax.all_to_all(outgoing, 'lon', split_axis=0, concat_axis=0, tiled=True)  15 us
    all_to_all x1, blocking collectives, shards(): lax.all_to_all(mixed, 'lon', split_axis=0, concat_axis=0, tiled=True)  12.6 us
    ppermute x10, starting transfers between devices, stage(): lax.ppermute(x, axis, [(i, i ^ d) for i in range(size)])  12.5 us
    pallas_call x1, Pallas kernels, finish(): pl.pallas_call(finish_kernel, in_specs=[smem_spec()] + [vmem_spec()] * 7...  11.6 us
    ppermute x4, waiting for transfers between devices, swap(): lax.ppermute(b, axis, pairs(size, 1))  11.1 us
    ppermute x4, starting transfers between devices, swap(): lax.ppermute(b, axis, pairs(size, 1))  10.2 us
    ppermute x10, waiting for transfers between devices, stage(): lax.ppermute(x, axis, [(i, i ^ d) for i in range(size)])  8.81 us
    pallas_call x1, Pallas kernels, smooth(): pl.pallas_call(smooth_kernel, in_specs=[smem_spec()] * 3 + [vmem_spec()]...  8.61 us
  transfers between devices with their start and end apart: 18, of which 12 were waited for; matrix products, arithmetic and copies ran while one was open for 0% of the time, Pallas kernels for 9%

profile of v3, /device:TPU:0, one launch (start us, length us, event | category | flops | bytes accessed | tf_op | source)
XLA Modules:
  0.0 126.9 jit_solution(8813428043950616205)
XLA Ops:
  0.7 1.8 %edge_pack.1 = (f32[1040,128]{1,0:T(8,128)S(1)}, f32[1040,128]{1,0:T(8,128)S(1)}) custom-call(s32[32]{0:T(128)} %counts.3, f32[32,256]{1,0:T(8,128)} %kappa_ref.5, f32[128,32,256]{2,1,0:T(8,128)} %p_hbm.5), custom_call_target="tpu_custom_call" | custom-call | tf_op jit(solution)/shard_map/edge_pack/pallas_call | solution.py:104
  2.5 3.2 %collective-permute-start.1 = (f32[1040,128]{1,0:T(8,128)S(1)}, f32[1040,128]{1,0:T(8,128)S(1)}, u32[]{:S(2)}, u32[]{:S(2)}) collective-permute-start(f32[1040,128]{1,0:T(8,128)S(1)} %get-tuple-element.31), channel_id=1, source_target_pairs={{0,112},{16,32},{32,16},{48,64},{64,48},{80,96},{96,80},{112,0},{1... | collective-permute-start | bytes 1597448 | tf_op jit(solution)/shard_map/ppermute | solution.py:524
  7.2 3.3 %turn.1 = (f32[32,256,128]{2,1,0:T(8,128)S(1)}, f32[160,128]{1,0:T(8,128)S(1)}, f32[160,128]{1,0:T(8,128)S(1)}) custom-call(s32[4]{0:T(128)S(1)} %pad_add_fusion.flags, f32[32,256]{1,0:T(8,128)S(1)} %copy-done, f32[128,32,256]{2,1,0:T(8,128)} %p_hbm.5), custom_call_target="tpu_custom_call" | custom-call | bytes 12582912 | tf_op jit(solution)/shard_map/turn/pallas_call | solution.py:145
  10.5 3.7 %places.1 = (s32[384]{0:T(512)S(1)}, s32[384]{0:T(512)S(1)}) custom-call(s32[1]{0:T(128)} %bitcast.11.count_ref, s32[384]{0:T(512)S(1)} %copy-done.3, s32[1,384]{1,0:T(1,128)S(1)} %bitcast.18), custom_call_target="tpu_custom_call" | custom-call | bytes 4194304 | tf_op jit(solution)/shard_map/places/pallas_call | solution.py:327
  14.8 2.0 %collective-permute-start.2 = (f32[200,128]{1,0:T(8,128)S(1)}, f32[200,128]{1,0:T(8,128)S(1)}, u32[]{:S(2)}, u32[]{:S(2)}) collective-permute-start(f32[200,128]{1,0:T(8,128)S(1)} %get-tuple-element.36), channel_id=1, source_target_pairs={{0,1},{1,0},{2,3},{3,2},{4,5},{5,4},{6,7},{7,6},{8,9},{9,8},{10,11... | collective-permute-start | bytes 307208 | tf_op jit(solution)/shard_map/ppermute | solution.py:524
  16.8 4.7 %collective-permute-start.3 = (f32[200,128]{1,0:T(8,128)S(1)}, f32[200,128]{1,0:T(8,128)S(1)}, u32[]{:S(2)}, u32[]{:S(2)}) collective-permute-start(f32[200,128]{1,0:T(8,128)S(1)} %get-tuple-element.37), channel_id=1, source_target_pairs={{0,15},{1,2},{2,1},{3,4},{4,3},{5,6},{6,5},{7,8},{8,7},{9,10},{10,... | collective-permute-start | bytes 307208 | tf_op jit(solution)/shard_map/ppermute | solution.py:524
  21.6 2.2 %coeffs.2 = (f32[10896,128]{1,0:T(8,128)S(1)}, f32[4,40,8,128]{3,2,1,0:T(8,128)S(1)}) custom-call(s32[4]{0:T(128)S(1)} %pad_add_fusion.flags, s32[32]{0:T(128)S(1)} %copy-done.2, f32[32,256]{1,0:T(8,128)S(1)} %copy-done, f32[16,128]{1,0:T(8,128)S(1)} %slice.8.tail_a, f32[16,128]{1,0:T(8,128)S(1)} %slice.9.tail_b, s32[1]{0:T(128)} %bitcast.12.after), custom_call_target="tpu_custom_call" | custom-call | bytes 4194304 | tf_op jit(solution)/shard_map/coeffs/pallas_call | solution.py:297
  24.8 8.6 %smooth.1 = (f32[768,128]{1,0:T(8,128)S(1)}, f32[16,128]{1,0:T(8,128)S(1)}, f32[16,128]{1,0:T(8,128)S(1)}, f32[10896,128]{1,0:T(8,128)S(1)}) custom-call(s32[4]{0:T(128)S(1)} %pad_add_fusion.flags, s32[384]{0:T(512)S(1)} %get-tuple-element.27.cell_ref, s32[384]{0:T(512)S(1)} %get-tuple-element.28.after.place_ref, ...), custom_call_target="tpu_custom_call", output_to_operand_aliasing={{3}: (4, {})} | custom-call | tf_op jit(solution)/shard_map/smooth/pallas_call | solution.py:363
  33.4 15.0 %all_to_all.22 = f32[16,48,128]{2,1,0:T(8,128)S(1)} all-to-all(f32[16,48,128]{2,1,0:T(8,128)S(1)} %bitcast.17), channel_id=1, replica_groups=mesh['lat'=8,'lon'=16] {'lon'}, dimensions={0} | all-to-all | bytes 786432 | tf_op jit(solution)/shard_map/all_to_all | solution.py:603
  48.5 2.7 %weigh.1 = f32[768,128]{1,0:T(8,128)S(1)} custom-call(f32[768,128]{1,0:T(8,128)S(1)} %bitcast.15, f32[768,768]{1,0:T(8,128)} %bitcast.19), custom_call_target="tpu_custom_call" | custom-call | tf_op jit(solution)/shard_map/weigh/pallas_call | solution.py:402
  51.2 12.6 %all_to_all.23 = f32[16,48,128]{2,1,0:T(8,128)S(1)} all-to-all(f32[16,48,128]{2,1,0:T(8,128)S(1)} %bitcast.16), channel_id=1, replica_groups=mesh['lat'=8,'lon'=16] {'lon'}, dimensions={0} | all-to-all | bytes 786432 | tf_op jit(solution)/shard_map/all_to_all | solution.py:605
  63.8 3.4 %spread.1 = (f32[10896,128]{1,0:T(8,128)S(1)}, f32[1024,128]{1,0:T(8,128)S(1)}, f32[1024,128]{1,0:T(8,128)S(1)}, f32[128,128]{1,0:T(8,128)S(1)}, f32[128,128]{1,0:T(8,128)S(1)}) custom-call(s32[4]{0:T(128)S(1)} %pad_add_fusion.flags, s32[384]{0:T(512)S(1)} %get-tuple-element.27.cell_ref, s32[384]{0:T(512)S(1)} %get-tuple-element.28.after.place_ref, ...), custom_call_target="tpu_custom_call" | custom-call | tf_op jit(solution)/shard_map/spread/pallas_call | solution.py:439
  68.2 2.4 %coeffs.3 = (f32[10896,128]{1,0:T(8,128)S(1)}, f32[4,40,8,128]{3,2,1,0:T(8,128)S(1)}) custom-call(s32[4]{0:T(128)S(1)} %pad_add_fusion.flags, s32[32]{0:T(128)S(1)} %copy-done.2, f32[32,256]{1,0:T(8,128)S(1)} %copy-done.1, f32[16,128]{1,0:T(8,128)S(1)} %get-tuple-element.40.tail_a, f32[16,128]{1,0:T(8,128)S(1)} %get-tuple-element.41.tail_b, ...), custom_call_target="tpu_custom_call" | custom-call | bytes 4194304 | tf_op jit(solution)/shard_map/coeffs/pallas_call | solution.py:297
  70.7 6.4 %collective-permute-done.5.lat_b = f32[1024,128]{1,0:T(8,128)S(1)} collective-permute-done((f32[1024,128]{1,0:T(8,128)S(1)}, f32[1024,128]{1,0:T(8,128)S(1)}, u32[]{:S(2)}, u32[]{:S(2)}) %collective-permute-start.5) | collective-permute-done | bytes 524320 | tf_op jit(solution)/shard_map/ppermute | solution.py:524
  77.8 2.2 %collective-permute-start.7 = (f32[160,128]{1,0:T(8,128)S(1)}, f32[160,128]{1,0:T(8,128)S(1)}, u32[]{:S(2)}, u32[]{:S(2)}) collective-permute-start(f32[160,128]{1,0:T(8,128)S(1)} %get-tuple-element.49), channel_id=1, source_target_pairs={{0,15},{1,2},{2,1},{3,4},{4,3},{5,6},{6,5},{7,8},{8,7},{9,10},{10,... | collective-permute-start | bytes 245768 | tf_op jit(solution)/shard_map/ppermute | solution.py:524
  79.9 2.3 %collective-permute-done.6.lon_a = f32[160,128]{1,0:T(8,128)S(1)} collective-permute-done((f32[160,128]{1,0:T(8,128)S(1)}, f32[160,128]{1,0:T(8,128)S(1)}, u32[]{:S(2)}, u32[]{:S(2)}) %collective-permute-start.6) | collective-permute-done | bytes 81952 | tf_op jit(solution)/shard_map/ppermute | solution.py:524
  82.2 3.6 %collective-permute-done.7.lon_b = f32[160,128]{1,0:T(8,128)S(1)} collective-permute-done((f32[160,128]{1,0:T(8,128)S(1)}, f32[160,128]{1,0:T(8,128)S(1)}, u32[]{:S(2)}, u32[]{:S(2)}) %collective-permute-start.7) | collective-permute-done | bytes 81952 | tf_op jit(solution)/shard_map/ppermute | solution.py:524
  85.8 11.6 %finish.1 = (f32[128,32,256]{2,1,0:T(8,128)}, f32[72,128]{1,0:T(8,128)S(1)}) custom-call(s32[4]{0:T(128)S(1)} %pad_add_fusion.flags, f32[10896,128]{1,0:T(8,128)S(1)} %get-tuple-element.39.field, f32[10896,128]{1,0:T(8,128)S(1)} %get-tuple-element.43.kap, f32[4,40,8,128]{3,2,1,0:T(8,128)S(1)} %get-tuple-element.44.after.act, ...), custom_call_target="tpu_custom_call" | custom-call | tf_op jit(solution)/shard_map/finish/pallas_call | solution.py:501
  100.4 2.4 %collective-permute-start.9 = (f32[72,128]{1,0:T(8,128)S(1)}, f32[72,128]{1,0:T(8,128)S(1)}, u32[]{:S(2)}, u32[]{:S(2)}) collective-permute-start(f32[72,128]{1,0:T(8,128)S(1)} %add.30), channel_id=1, source_target_pairs={{0,32},{16,48},{32,0},{48,16},{64,96},{80,112},{96,64},{112,80},{1... | collective-permute-start | bytes 110600 | tf_op jit(solution)/shard_map/ppermute | solution.py:578
  105.9 3.6 %collective-permute-start.12 = (f32[72,128]{1,0:T(8,128)S(1)}, f32[72,128]{1,0:T(8,128)S(1)}, u32[]{:S(2)}, u32[]{:S(2)}) collective-permute-start(f32[72,128]{1,0:T(8,128)S(1)} %add_add_fusion.1), channel_id=1, source_target_pairs={{0,1},{1,0},{2,3},{3,2},{4,5},{5,4},{6,7},{7,6},{8,9},{9,8},{10,11... | collective-permute-start | bytes 110600 | tf_op jit(solution)/shard_map/ppermute | solution.py:578
  111.9 1.5 %collective-permute-start.17 = (f32[72,128]{1,0:T(8,128)S(1)}, f32[72,128]{1,0:T(8,128)S(1)}, u32[]{:S(2)}, u32[]{:S(2)}) collective-permute-start(f32[72,128]{1,0:T(8,128)S(1)} %add_add_fusion.x_ref), channel_id=1, source_target_pairs={{0,12},{1,13},{2,14},{3,15},{4,8},{5,9},{6,10},{7,11},{8,4},{9,5},... | collective-permute-start | bytes 110600 | tf_op jit(solution)/shard_map/ppermute | solution.py:578
  113.6 2.4 %collective-permute-start.15 = (f32[72,128]{1,0:T(8,128)S(1)}, f32[72,128]{1,0:T(8,128)S(1)}, u32[]{:S(2)}, u32[]{:S(2)}) collective-permute-start(f32[72,128]{1,0:T(8,128)S(1)} %add_add_fusion.x_ref), channel_id=1, source_target_pairs={{0,4},{1,5},{2,6},{3,7},{4,0},{5,1},{6,2},{7,3},{8,12},{9,13},{10,... | collective-permute-start | bytes 110600 | tf_op jit(solution)/shard_map/ppermute | solution.py:578
  117.1 1.7 %collective-permute-done.16.g2_ref = f32[72,128]{1,0:T(8,128)S(1)} collective-permute-done((f32[72,128]{1,0:T(8,128)S(1)}, f32[72,128]{1,0:T(8,128)S(1)}, u32[]{:S(2)}, u32[]{:S(2)}) %collective-permute-start.16) | collective-permute-done | bytes 36896 | tf_op jit(solution)/shard_map/ppermute | solution.py:578
  118.8 8.1 %factor.1 = f32[128,128]{1,0:T(8,128)} custom-call(f32[72,128]{1,0:T(8,128)S(1)} %add_add_fusion.x_ref, f32[72,128]{1,0:T(8,128)S(1)} %collective-permute-done.15.g1_ref, f32[72,128]{1,0:T(8,128)S(1)} %collective-permute-done.16.g2_ref, f32[72,128]{1,0:T(8,128)S(1)} %collective-permute-done.17.g3_ref), custom_call_target="tpu_custom_call" | custom-call | tf_op jit(solution)/shard_map/factor/pallas_call | solution.py:564
  (42 shorter events, 14.0 us)
Async XLA Ops:
  0.6 20.9 %copy-start.2 = (s32[32]{0:T(128)S(1)}, s32[32]{0:T(128)}, u32[]{:S(2)}) copy-start(s32[32]{0:T(128)} %counts.3) | copy-start | bytes 388
  0.6 9.9 %copy-start.4 = (s32[384,1]{0,1:T(1,128)S(1)}, s32[384,1]{0,1:T(1,128)}, u32[]{:S(2)}) copy-start(s32[384,1]{0,1:T(1,128)} %param.11) | copy-start | bytes 4612
  0.7 9.9 %copy-start.3 = (s32[384]{0:T(512)S(1)}, s32[384]{0:T(512)}, u32[]{:S(2)}) copy-start(s32[384]{0:T(512)} %cell_ref.1) | copy-start | bytes 4612
  2.4 11.8 %collective-permute-start = (f32[1040,128]{1,0:T(8,128)S(1)}, f32[1040,128]{1,0:T(8,128)S(1)}, u32[]{:S(2)}, u32[]{:S(2)}) collective-permute-start(f32[1040,128]{1,0:T(8,128)S(1)} %get-tuple-element.30), channel_id=1, source_target_pairs={{0,16},{16,0},{32,48},{48,32},{64,80},{80,64},{96,112},{112,96},{1... | collective-permute-start | bytes 1597448 | tf_op jit(solution)/shard_map/ppermute | solution.py:524
  2.5 11.7 %collective-permute-start.1 = (f32[1040,128]{1,0:T(8,128)S(1)}, f32[1040,128]{1,0:T(8,128)S(1)}, u32[]{:S(2)}, u32[]{:S(2)}) collective-permute-start(f32[1040,128]{1,0:T(8,128)S(1)} %get-tuple-element.31), channel_id=1, source_target_pairs={{0,112},{16,32},{32,16},{48,64},{64,48},{80,96},{96,80},{112,0},{1... | collective-permute-start | bytes 1597448 | tf_op jit(solution)/shard_map/ppermute | solution.py:524
  6.5 0.8 copy-start
  14.8 8.9 %collective-permute-start.2 = (f32[200,128]{1,0:T(8,128)S(1)}, f32[200,128]{1,0:T(8,128)S(1)}, u32[]{:S(2)}, u32[]{:S(2)}) collective-permute-start(f32[200,128]{1,0:T(8,128)S(1)} %get-tuple-element.36), channel_id=1, source_target_pairs={{0,1},{1,0},{2,3},{3,2},{4,5},{5,4},{6,7},{7,6},{8,9},{9,8},{10,11... | collective-permute-start | bytes 307208 | tf_op jit(solution)/shard_map/ppermute | solution.py:524
  16.8 8.0 %collective-permute-start.3 = (f32[200,128]{1,0:T(8,128)S(1)}, f32[200,128]{1,0:T(8,128)S(1)}, u32[]{:S(2)}, u32[]{:S(2)}) collective-permute-start(f32[200,128]{1,0:T(8,128)S(1)} %get-tuple-element.37), channel_id=1, source_target_pairs={{0,15},{1,2},{2,1},{3,4},{4,3},{5,6},{6,5},{7,8},{8,7},{9,10},{10,... | collective-permute-start | bytes 307208 | tf_op jit(solution)/shard_map/ppermute | solution.py:524
  24.8 43.4 %copy-start.1 = (f32[32,256]{1,0:T(8,128)S(1)}, f32[32,256]{1,0:T(8,128)}, u32[]{:S(2)}) copy-start(f32[32,256]{1,0:T(8,128)} %kappa_ref.5) | copy-start | bytes 98308
  67.2 9.9 %collective-permute-start.5 = (f32[1024,128]{1,0:T(8,128)S(1)}, f32[1024,128]{1,0:T(8,128)S(1)}, u32[]{:S(2)}, u32[]{:S(2)}) collective-permute-start(f32[1024,128]{1,0:T(8,128)S(1)} %get-tuple-element.45), channel_id=1, source_target_pairs={{0,112},{16,32},{32,16},{48,64},{64,48},{80,96},{96,80},{112,0},{1... | collective-permute-start | bytes 1572872 | tf_op jit(solution)/shard_map/ppermute | solution.py:524
  67.3 9.8 %collective-permute-start.4 = (f32[1024,128]{1,0:T(8,128)S(1)}, f32[1024,128]{1,0:T(8,128)S(1)}, u32[]{:S(2)}, u32[]{:S(2)}) collective-permute-start(f32[1024,128]{1,0:T(8,128)S(1)} %get-tuple-element.42.after), channel_id=1, source_target_pairs={{0,16},{16,0},{32,48},{48,32},{64,80},{80,64},{96,112},{112,96},{1... | collective-permute-start | bytes 1572872 | tf_op jit(solution)/shard_map/ppermute | solution.py:524
  77.7 4.5 %collective-permute-start.6 = (f32[160,128]{1,0:T(8,128)S(1)}, f32[160,128]{1,0:T(8,128)S(1)}, u32[]{:S(2)}, u32[]{:S(2)}) collective-permute-start(f32[160,128]{1,0:T(8,128)S(1)} %get-tuple-element.48), channel_id=1, source_target_pairs={{0,1},{1,0},{2,3},{3,2},{4,5},{5,4},{6,7},{7,6},{8,9},{9,8},{10,11... | collective-permute-start | bytes 245768 | tf_op jit(solution)/shard_map/ppermute | solution.py:524
  77.8 8.0 %collective-permute-start.7 = (f32[160,128]{1,0:T(8,128)S(1)}, f32[160,128]{1,0:T(8,128)S(1)}, u32[]{:S(2)}, u32[]{:S(2)}) collective-permute-start(f32[160,128]{1,0:T(8,128)S(1)} %get-tuple-element.49), channel_id=1, source_target_pairs={{0,15},{1,2},{2,1},{3,4},{4,3},{5,6},{6,5},{7,8},{8,7},{9,10},{10,... | collective-permute-start | bytes 245768 | tf_op jit(solution)/shard_map/ppermute | solution.py:524
  97.4 1.3 %collective-permute-start.8 = (f32[72,128]{1,0:T(8,128)S(1)}, f32[72,128]{1,0:T(8,128)S(1)}, u32[]{:S(2)}, u32[]{:S(2)}) collective-permute-start(f32[72,128]{1,0:T(8,128)S(1)} %get-tuple-element.51), channel_id=1, source_target_pairs={{0,16},{16,0},{32,48},{48,32},{64,80},{80,64},{96,112},{112,96},{1... | collective-permute-start | bytes 110600 | tf_op jit(solution)/shard_map/ppermute | solution.py:578
  98.7 5.2 %collective-permute-start.11 = (f32[72,128]{1,0:T(8,128)S(1)}, f32[72,128]{1,0:T(8,128)S(1)}, u32[]{:S(2)}, u32[]{:S(2)}) collective-permute-start(f32[72,128]{1,0:T(8,128)S(1)} %add.30), channel_id=1, source_target_pairs={{0,96},{16,112},{32,64},{48,80},{64,32},{80,48},{96,0},{112,16},{1... | collective-permute-start | bytes 110600 | tf_op jit(solution)/shard_map/ppermute | solution.py:578
  99.9 5.5 %collective-permute-start.10 = (f32[72,128]{1,0:T(8,128)S(1)}, f32[72,128]{1,0:T(8,128)S(1)}, u32[]{:S(2)}, u32[]{:S(2)}) collective-permute-start(f32[72,128]{1,0:T(8,128)S(1)} %add.30), channel_id=1, source_target_pairs={{0,64},{16,80},{32,96},{48,112},{64,0},{80,16},{96,32},{112,48},{1... | collective-permute-start | bytes 110600 | tf_op jit(solution)/shard_map/ppermute | solution.py:578
  100.4 4.9 %collective-permute-start.9 = (f32[72,128]{1,0:T(8,128)S(1)}, f32[72,128]{1,0:T(8,128)S(1)}, u32[]{:S(2)}, u32[]{:S(2)}) collective-permute-start(f32[72,128]{1,0:T(8,128)S(1)} %add.30), channel_id=1, source_target_pairs={{0,32},{16,48},{32,0},{48,16},{64,96},{80,112},{96,64},{112,80},{1... | collective-permute-start | bytes 110600 | tf_op jit(solution)/shard_map/ppermute | solution.py:578
  105.3 5.2 %collective-permute-start.14 = (f32[72,128]{1,0:T(8,128)S(1)}, f32[72,128]{1,0:T(8,128)S(1)}, u32[]{:S(2)}, u32[]{:S(2)}) collective-permute-start(f32[72,128]{1,0:T(8,128)S(1)} %add_add_fusion.1), channel_id=1, source_target_pairs={{0,3},{1,2},{2,1},{3,0},{4,7},{5,6},{6,5},{7,4},{8,11},{9,10},{10,... | collective-permute-start | bytes 110600 | tf_op jit(solution)/shard_map/ppermute | solution.py:578
  105.7 5.5 %collective-permute-start.13 = (f32[72,128]{1,0:T(8,128)S(1)}, f32[72,128]{1,0:T(8,128)S(1)}, u32[]{:S(2)}, u32[]{:S(2)}) collective-permute-start(f32[72,128]{1,0:T(8,128)S(1)} %add_add_fusion.1), channel_id=1, source_target_pairs={{0,2},{1,3},{2,0},{3,1},{4,6},{5,7},{6,4},{7,5},{8,10},{9,11},{10,... | collective-permute-start | bytes 110600 | tf_op jit(solution)/shard_map/ppermute | solution.py:578
  105.9 5.9 %collective-permute-start.12 = (f32[72,128]{1,0:T(8,128)S(1)}, f32[72,128]{1,0:T(8,128)S(1)}, u32[]{:S(2)}, u32[]{:S(2)}) collective-permute-start(f32[72,128]{1,0:T(8,128)S(1)} %add_add_fusion.1), channel_id=1, source_target_pairs={{0,1},{1,0},{2,3},{3,2},{4,5},{5,4},{6,7},{7,6},{8,9},{9,8},{10,11... | collective-permute-start | bytes 110600 | tf_op jit(solution)/shard_map/ppermute | solution.py:578
  111.9 5.2 %collective-permute-start.17 = (f32[72,128]{1,0:T(8,128)S(1)}, f32[72,128]{1,0:T(8,128)S(1)}, u32[]{:S(2)}, u32[]{:S(2)}) collective-permute-start(f32[72,128]{1,0:T(8,128)S(1)} %add_add_fusion.x_ref), channel_id=1, source_target_pairs={{0,12},{1,13},{2,14},{3,15},{4,8},{5,9},{6,10},{7,11},{8,4},{9,5},... | collective-permute-start | bytes 110600 | tf_op jit(solution)/shard_map/ppermute | solution.py:578
  113.3 5.5 %collective-permute-start.16 = (f32[72,128]{1,0:T(8,128)S(1)}, f32[72,128]{1,0:T(8,128)S(1)}, u32[]{:S(2)}, u32[]{:S(2)}) collective-permute-start(f32[72,128]{1,0:T(8,128)S(1)} %add_add_fusion.x_ref), channel_id=1, source_target_pairs={{0,8},{1,9},{2,10},{3,11},{4,12},{5,13},{6,14},{7,15},{8,0},{9,1},... | collective-permute-start | bytes 110600 | tf_op jit(solution)/shard_map/ppermute | solution.py:578
  113.6 5.1 %collective-permute-start.15 = (f32[72,128]{1,0:T(8,128)S(1)}, f32[72,128]{1,0:T(8,128)S(1)}, u32[]{:S(2)}, u32[]{:S(2)}) collective-permute-start(f32[72,128]{1,0:T(8,128)S(1)} %add_add_fusion.x_ref), channel_id=1, source_target_pairs={{0,4},{1,5},{2,6},{3,7},{4,0},{5,1},{6,2},{7,3},{8,12},{9,13},{10,... | collective-permute-start | bytes 110600 | tf_op jit(solution)/shard_map/ppermute | solution.py:578

commit v4 on v3

--- a/solution.py
+++ b/solution.py
@@ -117,7 +117,7 @@
     )(in_hbm(counts), in_hbm(kappa), in_hbm(probes))
 
 
-def turn_kernel(flags, kappa_ref, p_hbm, y_ref, own_a, own_b, chunk, sems):
+def turn_kernel(flags, kappa_ref, p_hbm, ext, own_a, own_b, chunk, sems):
     def copy(n):
         half, block = n // 4, n % 4
         return pltpu.make_async_copy(
@@ -131,13 +131,13 @@
         half, block = n // 4, n % 4
         for i in range(8):
             r = block * 8 + i
-            y_ref[r, half * LANES:(half + 1) * LANES, :] = flat[pl.ds(n * K * 8 + i, K, stride=8), :].T
+            ext[pl.ds(at(r + H, 8) + half * LANES, LANES), :] = flat[pl.ds(n * K * 8 + i, K, stride=8), :].T
     odd = flags[2]
     for own, low in ((own_a, odd), (own_b, 1 - odd)):
         col = jnp.where(low == 1, 0, C - H)
         lane = pl.multiple_of(jnp.where(low == 1, 0, LANES), LANES)
         for r in range(R):
-            own[r * H:(r + 1) * H, :] = y_ref[r, pl.ds(col, H), :]
+            own[r * H:(r + 1) * H, :] = ext[pl.ds(at(r + H, 8) + col, H), :]
         own[R * H:, :] = kappa_ref[:, pl.ds(lane, LANES)]
 
 
@@ -146,7 +146,7 @@
         turn_kernel,
         in_specs=[smem_spec(), vmem_spec(), hbm_spec()],
         out_specs=[vmem_spec()] * 3,
-        out_shape=[held(R, C, K), held(OWN_ROWS, K), held(OWN_ROWS, K)],
+        out_shape=[held(NROW + 16, K), held(OWN_ROWS, K), held(OWN_ROWS, K)],
         scratch_shapes=[pltpu.VMEM((8, K, 8, LANES), jnp.float32), pltpu.SemaphoreType.DMA((8,))],
         compiler_params=pltpu.CompilerParams(vmem_limit_bytes=12 * 1024 * 1024),
         cost_estimate=pl.CostEstimate(flops=0, bytes_accessed=12 * 1024 * 1024, transcendentals=0),
@@ -212,14 +212,18 @@
                 buf[pl.ds(start, H), :] = keep(lat_ok[n], keep(lon_ok[m], lon[part:part + H, :]))
 
 
-def coeffs_kernel(flags, counts, kappa_ref, tail_a, tail_b, after, *rest):
-    *lon, kap, act = rest
+def put_own_kappa(kap, act, counts, kappa_ref):
+    kap_t = kappa_ref[...].T
+    for r in range(R):
+        kap[pl.ds(at(r + H, 8), C), :] = jnp.broadcast_to(kap_t[:, r:r + 1], (C, K))
+        for s in range(SWEEPS):
+            act[s, r + H] = jnp.full((8, K), jnp.where(counts[r] > s, 1.0, 0.0), jnp.float32)
+
+
+def put_lat_kappa(kap, act, flags, tail_a, tail_b):
     odd = flags[0]
     lat_ok = (None, flags[1] == 1)
     lat_row = (jnp.where(odd == 1, 0, R + H), jnp.where(odd == 1, R + H, 0))
-    kap_t = kappa_ref[...].T
-    for r in range(R):
-        kap[pl.ds(at(r + H, 8), C), :] = jnp.broadcast_to(kap_t[:, r:r + 1], (C, K))
     for n, lat in ((0, tail_a), (1, tail_b)):
         turned = lat[:8, :].T
         if n == 1:
@@ -228,15 +232,9 @@
             for h in range(2):
                 start = pl.multiple_of(OFF + (lat_row[n] + r) * CB + 8 + h * LANES, 8)
                 kap[pl.ds(start, LANES), :] = jnp.broadcast_to(turned[:, 2 * r + h:2 * r + h + 1], (LANES, K))
-        for r in range(H):
             wide = jnp.broadcast_to(lat[8 + r:9 + r, :], (8, K))
             for s in range(SWEEPS):
                 act[s, lat_row[n] + r] = jnp.where(wide > s, 1.0, 0.0)
-    for r in range(R):
-        for s in range(SWEEPS):
-            act[s, r + H] = jnp.full((8, K), jnp.where(counts[r] > s, 1.0, 0.0), jnp.float32)
-    if lon:
-        put_lon_kappa(kap, flags, *lon)
 
 
 def put_lon_kappa(kap, flags, lon_a, lon_b):
@@ -265,47 +263,94 @@
                 kap[pl.ds(OFF + (lat_row[n] + r) * CB + 4 + lon_col[m], H), :] = part
 
 
-def sweep(src, dst, kap, act, s):
-    first = s + 1
-    count = RE - 2 * first
-
-    def body(i, _):
-        r = first + 2 * i
-        base = pl.multiple_of(r * CB, 8)
-        a0 = act[s, r]
-        a1 = act[s, r + 1]
-        for t in range(CB // 8):
-            o = base + OFF + t * 8
-            up = src[pl.ds(o - CB, 8), :]
-            c0 = src[pl.ds(o, 8), :]
-            c1 = src[pl.ds(o + CB, 8), :]
-            dn = src[pl.ds(o + 2 * CB, 8), :]
-            l0 = src[pl.ds(o - 1, 8), :]
-            r0 = src[pl.ds(o + 1, 8), :]
-            l1 = src[pl.ds(o + CB - 1, 8), :]
-            r1 = src[pl.ds(o + CB + 1, 8), :]
-            lap0 = (up + c1) + (l0 + r0) - 4.0 * c0
-            lap1 = (c0 + dn) + (l1 + r1) - 4.0 * c1
-            dst[pl.ds(o, 8), :] = c0 + (a0 * kap[pl.ds(o, 8), :]) * lap0
-            dst[pl.ds(o + CB, 8), :] = c1 + (a1 * kap[pl.ds(o + CB, 8), :]) * lap1
-        return 0
-
-    lax.fori_loop(0, count // 2, body, 0)
-
-
-def coeffs(flags, counts, kappa, tail_a, tail_b, after, *lon):
+def relax(src, dst, kap, act, s, r, tiles):
+    base = pl.multiple_of(r * CB, 8)
+    a0 = act[s, r]
+    a1 = act[s, r + 1]
+    for t in tiles:
+        o = base + OFF + t * 8
+        up = src[pl.ds(o - CB, 8), :]
+        c0 = src[pl.ds(o, 8), :]
+        c1 = src[pl.ds(o + CB, 8), :]
+        dn = src[pl.ds(o + 2 * CB, 8), :]
+        l0 = src[pl.ds(o - 1, 8), :]
+        r0 = src[pl.ds(o + 1, 8), :]
+        l1 = src[pl.ds(o + CB - 1, 8), :]
+        r1 = src[pl.ds(o + CB + 1, 8), :]
+        lap0 = (up + c1) + (l0 + r0) - 4.0 * c0
+        lap1 = (c0 + dn) + (l1 + r1) - 4.0 * c1
+        dst[pl.ds(o, 8), :] = c0 + (a0 * kap[pl.ds(o, 8), :]) * lap0
+        dst[pl.ds(o + CB, 8), :] = c1 + (a1 * kap[pl.ds(o + CB, 8), :]) * lap1
+
+
+INNER = tuple(range(1, CB // 8 - 1))
+EDGE = (0, 1, CB // 8 - 2, CB // 8 - 1)
+
+
+def inner_kernel(ext, kap, act, *levels):
+    src = ext
+    for s in range(SWEEPS):
+        t = s + 1
+
+        def body(i, _):
+            relax(src, levels[s], kap, act, s, t + H + 2 * i, INNER)
+            return 0
+
+        lax.fori_loop(0, (R - 2 * t) // 2, body, 0)
+        src = levels[s]
+
+
+def inner(ext, kap, act):
+    return pl.pallas_call(
+        inner_kernel,
+        in_specs=[vmem_spec()] * 3,
+        out_specs=[vmem_spec()] * SWEEPS,
+        out_shape=[held(NROW + 16, K)] * SWEEPS,
+        compiler_params=pltpu.CompilerParams(vmem_limit_bytes=2 * 1024 * 1024),
+        cost_estimate=pl.CostEstimate(flops=0, bytes_accessed=16 * 1024 * 1024, transcendentals=0),
+        name="inner",
+    )(*in_vmem(ext, kap, act))
+
+
+def outer(levels, kap, act):
+    for s in range(SWEEPS):
+        t = s + 1
+        tiles = INNER if t == SWEEPS else tuple(range(CB // 8))
+        sides = tuple(c for c in EDGE if c in tiles)
+
+        def ends(i, _):
+            relax(levels[s], levels[t], kap, act, s, jnp.where(i < 2, t + 2 * i, R + H - t + 2 * i - 4), tiles)
+            return 0
+
+        def middle(i, _):
+            relax(levels[s], levels[t], kap, act, s, t + H + 2 * i, sides)
+            return 0
+
+        lax.fori_loop(0, 4, ends, 0)
+        lax.fori_loop(0, (R - 2 * t) // 2, middle, 0, unroll=2)
+
+
+def coeffs_kernel(flags, counts, kappa_ref, after, *rest):
+    *halos, kap, act = rest
+    put_own_kappa(kap, act, counts, kappa_ref)
+    if halos:
+        put_lat_kappa(kap, act, flags, *halos[:2])
+        put_lon_kappa(kap, flags, *halos[2:])
+
+
+def coeffs(flags, counts, kappa, after, *halos):
     return pl.pallas_call(
         coeffs_kernel,
-        in_specs=[smem_spec()] * 2 + [vmem_spec()] * 3 + [pl.BlockSpec(memory_space=pl.ANY)] + [vmem_spec()] * len(lon),
+        in_specs=[smem_spec()] * 2 + [vmem_spec(), pl.BlockSpec(memory_space=pl.ANY)] + [vmem_spec()] * len(halos),
         out_specs=[vmem_spec()] * 2,
         out_shape=[held(NROW + 16, K), held(SWEEPS, RE, 8, K)],
         compiler_params=pltpu.CompilerParams(vmem_limit_bytes=8 * 1024 * 1024),
         cost_estimate=pl.CostEstimate(flops=0, bytes_accessed=4 * 1024 * 1024, transcendentals=0),
         name="coeffs",
-    )(flags, counts, kappa, tail_a, tail_b, after, *lon)
-
-
-def places_kernel(count_ref, cell_ref, owner_ref, row_ref, place_ref, seen):
+    )(flags, counts, kappa, after, *halos)
+
+
+def places_kernel(count_ref, cell_ref, owner_ref, after, row_ref, place_ref, seen):
     for i in range(LON_OWNERS):
         seen[i] = 0
     count = count_ref[0]
@@ -323,57 +368,51 @@
     lax.fori_loop(0, SLOTS, one, 0, unroll=8)
 
 
-def places(count, cell, owner):
+def places(count, cell, owner, after):
     return pl.pallas_call(
         places_kernel,
-        in_specs=[smem_spec()] * 3,
+        in_specs=[smem_spec()] * 3 + [pl.BlockSpec(memory_space=pl.ANY)],
         out_specs=[smem_spec()] * 2,
         out_shape=[jax.ShapeDtypeStruct((SLOTS,), jnp.int32)] * 2,
         scratch_shapes=[pltpu.SMEM((LON_OWNERS,), jnp.int32)],
         cost_estimate=pl.CostEstimate(flops=0, bytes_accessed=4 * 1024 * 1024, transcendentals=0),
         compiler_params=pltpu.CompilerParams(vmem_limit_bytes=1024 * 1024),
         name="places",
-    )(count, cell, owner)
-
-
-def smooth_kernel(flags, cell_ref, place_ref, y_ref, kap_in, act, lat_a, lat_b, lon_a, lon_b,
-                  out_ref, tail_a, tail_b, kap, buf_a, buf_b, rows_ref):
-    put_lon_kappa(kap, flags, lon_a, lon_b)
-    for r in range(R):
-        buf_a[pl.ds(at(r + H, 8), C), :] = y_ref[r]
-    put_halos(buf_a, flags, lat_a, lat_b, lon_a, lon_b)
+    )(count, cell, owner, after)
+
+
+def smooth_kernel(flags, cell_ref, place_ref, *refs):
+    (ext_in, l1_in, l2_in, l3_in, l4_in, kap_in, act_in, lat_a, lat_b, lon_a, lon_b,
+     out_ref, tail_a, tail_b, ext, l1, l2, l3, l4, kap, act, rows_ref) = refs
     tail_a[...] = lat_a[H * C:, :]
     tail_b[...] = lat_b[H * C:, :]
-    bufs = (buf_a, buf_b)
-    for s in range(SWEEPS):
-        sweep(bufs[s % 2], bufs[(s + 1) % 2], kap, act, s)
+    put_lat_kappa(kap, act, flags, tail_a, tail_b)
+    put_lon_kappa(kap, flags, lon_a, lon_b)
+    put_halos(ext, flags, lat_a, lat_b, lon_a, lon_b)
+    outer((ext, l1, l2, l3, l4), kap, act)
     rows_ref[...] = jnp.zeros_like(rows_ref)
 
     def copy(i, _):
         for j in range(8):
             t = i * 8 + j
-            rows_ref[pl.ds(place_ref[t], 1), :] = buf_a[pl.ds(cell_ref[t], 1), :]
+            rows_ref[pl.ds(place_ref[t], 1), :] = l4[pl.ds(cell_ref[t], 1), :]
         return 0
 
     lax.fori_loop(0, SLOTS // 8, copy, 0)
     out_ref[...] = rows_ref[:PLACES]
 
 
-def smooth(flags, cell, place, y, kap, act, halos):
+def smooth(flags, cell, place, ext, levels, kap, act, halos):
     return pl.pallas_call(
         smooth_kernel,
-        in_specs=[smem_spec()] * 3 + [vmem_spec()] * 7,
-        out_specs=[vmem_spec()] * 4,
-        out_shape=[f32(PLACES, K), f32(16, K), f32(16, K), held(NROW + 16, K)],
-        input_output_aliases={4: 3},
-        scratch_shapes=[
-            pltpu.VMEM((NROW + 16, K), jnp.float32),
-            pltpu.VMEM((NROW + 16, K), jnp.float32),
-            pltpu.VMEM((PLACES + 8, K), jnp.float32),
-        ],
-        compiler_params=params(),
+        in_specs=[smem_spec()] * 3 + [vmem_spec()] * 11,
+        out_specs=[vmem_spec()] * 10,
+        out_shape=[f32(PLACES, K), f32(16, K), f32(16, K)] + [held(NROW + 16, K)] * 6 + [held(SWEEPS, RE, 8, K)],
+        input_output_aliases={3 + i: 3 + i for i in range(7)},
+        scratch_shapes=[pltpu.VMEM((PLACES + 8, K), jnp.float32)],
+        compiler_params=pltpu.CompilerParams(vmem_limit_bytes=8 * 1024 * 1024),
         name="smooth",
-    )(flags, cell, place, *in_vmem(y, kap, act), *halos)
+    )(flags, cell, place, *in_vmem(ext, *levels, kap, act), *halos)[:3]
 
 
 def weigh_kernel(b_ref, r_hbm, out_ref, r_ref, sems):
@@ -446,8 +485,10 @@
     )(flags, cell, place, count, returned)
 
 
-def finish_kernel(flags, field, kap, act, lat_a, lat_b, lon_a, lon_b, p_hbm, out_hbm, gram_ref,
-                  buf_a, buf_b, chunk, in_sems, out_sems):
+def finish_kernel(flags, *refs):
+    (ext_in, l1_in, l2_in, l3_in, l4_in, kap, act, lat_a, lat_b, lon_a, lon_b, p_hbm,
+     out_hbm, gram_ref, ext, l1, l2, l3, l4, chunk, in_sems, out_sems) = refs
+
     def part(ref, n):
         half, block = n // 4, n % 4
         return ref.at[:, pl.ds(block * 8, 8), pl.ds(half * LANES, LANES)]
@@ -460,11 +501,8 @@
 
     for n in range(8):
         copy_in(n).start()
-    buf_a[...] = field[...]
-    put_halos(buf_a, flags, lat_a, lat_b, lon_a, lon_b)
-    bufs = (buf_a, buf_b)
-    for s in range(SWEEPS):
-        sweep(bufs[s % 2], bufs[(s + 1) % 2], kap, act, s)
+    put_halos(ext, flags, lat_a, lat_b, lon_a, lon_b)
+    outer((ext, l1, l2, l3, l4), kap, act)
     flat = chunk.reshape(8 * K * 8, LANES)
     contract = (((1,), (1,)), ((), ()))
     hh = jnp.zeros((K, K), jnp.float32)
@@ -477,7 +515,7 @@
             for j in range(2):
                 where = pl.ds(n * K * 8 + i + j, K, stride=8)
                 start = at(block * 8 + i + j + H, 8) + half * LANES
-                sk = flat[where, :] + buf_a[pl.ds(start, LANES), :].T
+                sk = flat[where, :] + l4[pl.ds(start, LANES), :].T
                 flat[where, :] = sk
                 parts.append(sk)
             sk = jnp.concatenate(parts, axis=1)
@@ -497,22 +535,21 @@
         copy_out(n).wait()
 
 
-def finish(flags, field, kap, act, halos, probes):
+def finish(flags, ext, levels, kap, act, halos, probes):
     return pl.pallas_call(
         finish_kernel,
-        in_specs=[smem_spec()] + [vmem_spec()] * 7 + [hbm_spec()],
-        out_specs=[hbm_spec(), vmem_spec()],
-        out_shape=[f32(K, R, C), f32(HALF + 8, K)],
+        in_specs=[smem_spec()] + [vmem_spec()] * 11 + [hbm_spec()],
+        out_specs=[hbm_spec()] + [vmem_spec()] * 6,
+        out_shape=[f32(K, R, C), f32(HALF + 8, K)] + [held(NROW + 16, K)] * 5,
+        input_output_aliases={1 + i: 2 + i for i in range(5)},
         scratch_shapes=[
-            pltpu.VMEM((NROW + 16, K), jnp.float32),
-            pltpu.VMEM((NROW + 16, K), jnp.float32),
             pltpu.VMEM((8, K, 8, LANES), jnp.float32),
             pltpu.SemaphoreType.DMA((8,)),
             pltpu.SemaphoreType.DMA((8,)),
         ],
-        compiler_params=params(),
+        compiler_params=pltpu.CompilerParams(vmem_limit_bytes=12 * 1024 * 1024),
         name="finish",
-    )(flags, *in_vmem(field, kap, act), *halos, in_hbm(probes))
+    )(flags, *in_vmem(ext, *levels, kap, act), *halos, in_hbm(probes))[:2]
 
 
 def pairs(size, first):
@@ -594,20 +631,23 @@
         lon % 2, ((lon > 0) & (lon < n_lon - 1)).astype(jnp.int32),
     ]).astype(jnp.int32)
     lat_a, lat_b = swap(*edge_pack(sweep_counts, kappa, probes), "lat")
-    y, own_a, own_b = turn(flags, kappa, probes)
+    ext, own_a, own_b = turn(flags, kappa, probes)
+    kap, act = coeffs(flags, sweep_counts, kappa, own_a)
+    levels = inner(ext, kap, act)
     count = obs_count.reshape(1)
-    cell, place = places(count, obs_cell, obs_owner.reshape(1, SLOTS))
-    lon_a, lon_b = swap(*corner(flags, own_a, own_b, lat_a, lat_b, place), "lon")
-    kap, act = coeffs(flags, sweep_counts, kappa, lat_a[H * C:], lat_b[H * C:], count)
-    outgoing, tail_a, tail_b, _ = smooth(flags, cell, place, y, kap, act, (lat_a, lat_b, lon_a, lon_b))
+    lon_pay = corner(flags, own_a, own_b, lat_a, lat_b, levels[-1])
+    cell, place = places(count, obs_cell, obs_owner.reshape(1, SLOTS), lon_pay[0])
+    lon_a, lon_b = swap(*lon_pay, "lon")
+    outgoing, tail_a, tail_b = smooth(flags, cell, place, ext, levels, kap, act, (lat_a, lat_b, lon_a, lon_b))
     buffer = lax.all_to_all(outgoing, "lon", split_axis=0, concat_axis=0, tiled=True)
     mixed = weigh(buffer, r_inv[0, 0])
     returned = lax.all_to_all(mixed, "lon", split_axis=0, concat_axis=0, tiled=True)
     field, pay_a, pay_b, own_a, own_b = spread(flags, cell, place, count, returned)
-    kap, act = coeffs(flags, sweep_counts, kappa, tail_a, tail_b, pay_a, lon_a, lon_b)
+    kap, act = coeffs(flags, sweep_counts, kappa, pay_a, tail_a, tail_b, lon_a, lon_b)
+    levels = inner(field, kap, act)
     lat_a, lat_b = swap(pay_a, pay_b, "lat")
-    back = (lat_a, lat_b) + swap(*corner(flags, own_a, own_b, lat_a, lat_b, act), "lon")
-    sketch, gram = finish(flags, field, kap, act, back, probes)
+    back = (lat_a, lat_b) + swap(*corner(flags, own_a, own_b, lat_a, lat_b, levels[-1]), "lon")
+    sketch, gram = finish(flags, field, levels, kap, act, back, probes)
     cells_all = R * C * n_lat * n_lon
     r_factor = factor(1.0 / cells_all, gather_sums(gram))
     return (sketch, r_factor)

time: 127 us -> 122 us (0.961)
  waiting for transfers between devices: 22.1 us -> 16.2 us
  Pallas kernels: 48.9 us -> 50.5 us
  blocking collectives: 27.7 us -> 26.3 us
    ppermute x4, waiting for transfers between devices: 11.1 us -> 5.09 us  [swap(): lax.ppermute(b, axis, pairs(size, 1))]
    pallas_call x4 -> x6, Pallas kernels: 19.9 us -> 24.5 us  [the longest x2 9.79 us: inner(): pl.pallas_call(inner_kernel, in_specs=[vmem_spec()] * 3, out_specs=[vmem_...]
    pallas_call x1, Pallas kernels: 8.61 us -> 4.61 us  [smooth(): pl.pallas_call(smooth_kernel, in_specs=[smem_spec()] * 3 + [vmem_spec()]...]
    ppermute x4, starting transfers between devices: 10.2 us -> 11.9 us  [swap(): lax.ppermute(b, axis, pairs(size, 1))]
    ppermute x4, starting transfers between devices: 3.1 us -> 1.7 us  [swap(): lax.ppermute(a, axis, pairs(size, 0))]
    all_to_all x1, blocking collectives: 15 us -> 13.6 us  [shards(): lax.all_to_all(outgoing, 'lon', split_axis=0, concat_axis=0, tiled=True)]
  transfers between devices with their start and end apart: 18 -> 18, of which waited for: 12 -> 12; matrix products, arithmetic and copies ran while one was open for 0% -> 0% of each run, Pallas kernels for 9% -> 17%
where the time goes in v4:
time: 122 us
  Pallas kernels  50.5 us (41%)
  blocking collectives  26.3 us (22%)
  starting transfers between devices  26.2 us (21%)
  waiting for transfers between devices  16.2 us (13%)
  between operations  1.49 us (1%)
    all_to_all x1, blocking collectives, shards(): lax.all_to_all(outgoing, 'lon', split_axis=0, concat_axis=0, tiled=True)  13.6 us
    all_to_all x1, blocking collectives, shards(): lax.all_to_all(mixed, 'lon', split_axis=0, concat_axis=0, tiled=True)  12.6 us
    ppermute x10, starting transfers between devices, stage(): lax.ppermute(x, axis, [(i, i ^ d) for i in range(size)])  12.5 us
    ppermute x4, starting transfers between devices, swap(): lax.ppermute(b, axis, pairs(size, 1))  11.9 us
    pallas_call x2, Pallas kernels, inner(): pl.pallas_call(inner_kernel, in_specs=[vmem_spec()] * 3, out_specs=[vmem_...  9.79 us
    ppermute x10, waiting for transfers between devices, stage(): lax.ppermute(x, axis, [(i, i ^ d) for i in range(size)])  9.28 us
    pallas_call x1, Pallas kernels, factor(): pl.pallas_call(functools.partial(factor_kernel, scale), in_specs=[vmem_sp...  8.09 us
    pallas_call x1, Pallas kernels, finish(): pl.pallas_call(finish_kernel, in_specs=[smem_spec()] + [vmem_spec()] * 11...  6.76 us
  transfers between devices with their start and end apart: 18, of which 12 were waited for; matrix products, arithmetic and copies ran while one was open for 0% of the time, Pallas kernels for 17%

profile of v4, /device:TPU:0, one launch (start us, length us, event | category | flops | bytes accessed | tf_op | source)
XLA Modules:
  0.0 121.5 jit_solution(16945671698908267212)
XLA Ops:
  0.6 2.6 %edge_pack.1 = (f32[1040,128]{1,0:T(8,128)}, f32[1040,128]{1,0:T(8,128)}) custom-call(s32[32]{0:T(128)} %counts.3, f32[32,256]{1,0:T(8,128)} %kappa_ref.5, f32[128,32,256]{2,1,0:T(8,128)} %refs_11_.1), custom_call_target="tpu_custom_call" | custom-call | tf_op jit(solution)/shard_map/edge_pack/pallas_call | solution.py:104
  3.4 3.2 %collective-permute-start.1 = (f32[1040,128]{1,0:T(8,128)}, f32[1040,128]{1,0:T(8,128)}, u32[]{:S(2)}, u32[]{:S(2)}) collective-permute-start(f32[1040,128]{1,0:T(8,128)} %get-tuple-element.38), channel_id=1, source_target_pairs={{0,112},{16,32},{32,16},{48,64},{64,48},{80,96},{96,80},{112,0},{1... | collective-permute-start | bytes 1597448 | tf_op jit(solution)/shard_map/ppermute | solution.py:561
  7.4 3.3 %turn.1 = (f32[10896,128]{1,0:T(8,128)S(1)}, f32[160,128]{1,0:T(8,128)S(1)}, f32[160,128]{1,0:T(8,128)S(1)}) custom-call(s32[4]{0:T(128)S(1)} %pad_add_fusion.flags, f32[32,256]{1,0:T(8,128)S(1)} %copy-done, f32[128,32,256]{2,1,0:T(8,128)} %refs_11_.1), custom_call_target="tpu_custom_call" | custom-call | bytes 12582912 | tf_op jit(solution)/shard_map/turn/pallas_call | solution.py:145
  10.7 1.8 %coeffs.2 = (f32[10896,128]{1,0:T(8,128)S(1)}, f32[4,40,8,128]{3,2,1,0:T(8,128)S(1)}) custom-call(s32[4]{0:T(128)S(1)} %pad_add_fusion.flags, s32[32]{0:T(128)S(1)} %copy-done.2, f32[32,256]{1,0:T(8,128)S(1)} %copy-done, f32[160,128]{1,0:T(8,128)S(1)} %get-tuple-element.35.after.own_a), custom_call_target="tpu_custom_call" | custom-call | bytes 4194304 | tf_op jit(solution)/shard_map/coeffs/pallas_call | solution.py:342
  12.5 4.7 %inner.2 = (f32[10896,128]{1,0:T(8,128)S(1)}, f32[10896,128]{1,0:T(8,128)S(1)}, f32[10896,128]{1,0:T(8,128)S(1)}, f32[10896,128]{1,0:T(8,128)S(1)}) custom-call(f32[10896,128]{1,0:T(8,128)S(1)} %get-tuple-element.39.ext.refs_0_, f32[10896,128]{1,0:T(8,128)S(1)} %get-tuple-element.40.kap.refs_5_, f32[4,40,8,128]{3,2,1,0:T(8,128)S(1)} %get-tuple-element.41.act.refs_6_), custom_call_target="tpu_custom_call" | custom-call | bytes 16777216 | tf_op jit(solution)/shard_map/inner/pallas_call | solution.py:304
  18.5 6.3 %collective-permute-start.3 = (f32[200,128]{1,0:T(8,128)S(1)}, f32[200,128]{1,0:T(8,128)S(1)}, u32[]{:S(2)}, u32[]{:S(2)}) collective-permute-start(f32[200,128]{1,0:T(8,128)S(1)} %get-tuple-element.49), channel_id=1, source_target_pairs={{0,15},{1,2},{2,1},{3,4},{4,3},{5,6},{6,5},{7,8},{8,7},{9,10},{10,... | collective-permute-start | bytes 307208 | tf_op jit(solution)/shard_map/ppermute | solution.py:561
  25.5 3.7 %places.1 = (s32[384]{0:T(512)S(1)}, s32[384]{0:T(512)S(1)}) custom-call(s32[1]{0:T(128)} %bitcast.11.count_ref, s32[384]{0:T(512)S(1)} %copy-done.3, s32[1,384]{1,0:T(1,128)S(1)} %bitcast.17, f32[200,128]{1,0:T(8,128)S(1)} %get-tuple-element.43.after), custom_call_target="tpu_custom_call" | custom-call | bytes 4194304 | tf_op jit(solution)/shard_map/places/pallas_call | solution.py:372
  29.5 4.6 %smooth.1 = (f32[768,128]{1,0:T(8,128)S(1)}, f32[16,128]{1,0:T(8,128)S(1)}, f32[16,128]{1,0:T(8,128)S(1)}, f32[10896,128]{1,0:T(8,128)S(1)}, f32[10896,128]{1,0:...) custom-call(s32[4]{0:T(128)S(1)} %pad_add_fusion.flags, ...), custom_call_target="tpu_custom_call", output_to_operand_aliasing={{3}: (3, {}), {4}: (4, {}), {5}: (5, {}), {6}: (6, {}), {7}... | custom-call | tf_op jit(solution)/shard_map/smooth/pallas_call | solution.py:406
  34.1 13.6 %all_to_all.22 = f32[16,48,128]{2,1,0:T(8,128)S(1)} all-to-all(f32[16,48,128]{2,1,0:T(8,128)S(1)} %bitcast.16), channel_id=1, replica_groups=mesh['lat'=8,'lon'=16] {'lon'}, dimensions={0} | all-to-all | bytes 786432 | tf_op jit(solution)/shard_map/all_to_all | solution.py:642
  47.8 2.7 %weigh.1 = f32[768,128]{1,0:T(8,128)S(1)} custom-call(f32[768,128]{1,0:T(8,128)S(1)} %bitcast.14, f32[768,768]{1,0:T(8,128)} %bitcast.18), custom_call_target="tpu_custom_call" | custom-call | tf_op jit(solution)/shard_map/weigh/pallas_call | solution.py:441
  50.5 12.6 %all_to_all.23 = f32[16,48,128]{2,1,0:T(8,128)S(1)} all-to-all(f32[16,48,128]{2,1,0:T(8,128)S(1)} %bitcast.15), channel_id=1, replica_groups=mesh['lat'=8,'lon'=16] {'lon'}, dimensions={0} | all-to-all | bytes 786432 | tf_op jit(solution)/shard_map/all_to_all | solution.py:644
  63.1 2.9 %spread.1 = (f32[10896,128]{1,0:T(8,128)S(1)}, f32[1024,128]{1,0:T(8,128)S(1)}, f32[1024,128]{1,0:T(8,128)S(1)}, f32[128,128]{1,0:T(8,128)S(1)}, f32[128,128]{1,0:T(8,128)S(1)}) custom-call(s32[4]{0:T(128)S(1)} %pad_add_fusion.flags, s32[384]{0:T(512)S(1)} %get-tuple-element.44.cell_ref, s32[384]{0:T(512)S(1)} %get-tuple-element.45.place_ref, ...), custom_call_target="tpu_custom_call" | custom-call | tf_op jit(solution)/shard_map/spread/pallas_call | solution.py:478
  67.2 2.4 %coeffs.3 = (f32[10896,128]{1,0:T(8,128)S(1)}, f32[4,40,8,128]{3,2,1,0:T(8,128)S(1)}) custom-call(s32[4]{0:T(128)S(1)} %pad_add_fusion.flags, s32[32]{0:T(128)S(1)} %copy-done.2, f32[32,256]{1,0:T(8,128)S(1)} %copy-done.1, f32[1024,128]{1,0:T(8,128)S(1)} %get-tuple-element.52.after, f32[16,128]{1,0:T(8,128)S(1)} %get-tuple-element.53.rest_0_, ...), custom_call_target="tpu_custom_call" | custom-call | bytes 4194304 | tf_op jit(solution)/shard_map/coeffs/pallas_call | solution.py:342
  69.6 5.1 %inner.3 = (f32[10896,128]{1,0:T(8,128)S(1)}, f32[10896,128]{1,0:T(8,128)S(1)}, f32[10896,128]{1,0:T(8,128)S(1)}, f32[10896,128]{1,0:T(8,128)S(1)}) custom-call(f32[10896,128]{1,0:T(8,128)S(1)} %get-tuple-element.51.ext.refs_0_, f32[10896,128]{1,0:T(8,128)S(1)} %get-tuple-element.55.kap.refs_5_, f32[4,40,8,128]{3,2,1,0:T(8,128)S(1)} %get-tuple-element.56.act.refs_6_), custom_call_target="tpu_custom_call" | custom-call | bytes 16777216 | tf_op jit(solution)/shard_map/inner/pallas_call | solution.py:304
  77.1 2.4 %collective-permute-start.7 = (f32[160,128]{1,0:T(8,128)S(1)}, f32[160,128]{1,0:T(8,128)S(1)}, u32[]{:S(2)}, u32[]{:S(2)}) collective-permute-start(f32[160,128]{1,0:T(8,128)S(1)} %get-tuple-element.65), channel_id=1, source_target_pairs={{0,15},{1,2},{2,1},{3,4},{4,3},{5,6},{6,5},{7,8},{8,7},{9,10},{10,... | collective-permute-start | bytes 245768 | tf_op jit(solution)/shard_map/ppermute | solution.py:561
  79.4 1.6 %collective-permute-done.6.refs_9_ = f32[160,128]{1,0:T(8,128)S(1)} collective-permute-done((f32[160,128]{1,0:T(8,128)S(1)}, f32[160,128]{1,0:T(8,128)S(1)}, u32[]{:S(2)}, u32[]{:S(2)}) %collective-permute-start.6) | collective-permute-done | bytes 81952 | tf_op jit(solution)/shard_map/ppermute | solution.py:561
  81.0 3.8 %collective-permute-done.7.refs_10_ = f32[160,128]{1,0:T(8,128)S(1)} collective-permute-done((f32[160,128]{1,0:T(8,128)S(1)}, f32[160,128]{1,0:T(8,128)S(1)}, u32[]{:S(2)}, u32[]{:S(2)}) %collective-permute-start.7) | collective-permute-done | bytes 81952 | tf_op jit(solution)/shard_map/ppermute | solution.py:561
  84.8 6.8 %finish.1 = (f32[128,32,256]{2,1,0:T(8,128)}, f32[72,128]{1,0:T(8,128)S(1)}, f32[10896,128]{1,0:T(8,128)S(1)}, f32[10896,128]{1,0:T(8,128)S(1)}, f32[10896,128]{...) custom-call(s32[4]{0:T(128)S(1)} %pad_add_fusion.flags, ...), custom_call_target="tpu_custom_call", output_to_operand_aliasing={{2}: (1, {}), {3}: (2, {}), {4}: (3, {}), {5}: (4, {}), {6}... | custom-call | tf_op jit(solution)/shard_map/finish/pallas_call | solution.py:539
  94.0 1.7 %collective-permute-start.10 = (f32[72,128]{1,0:T(8,128)S(1)}, f32[72,128]{1,0:T(8,128)S(1)}, u32[]{:S(2)}, u32[]{:S(2)}) collective-permute-start(f32[72,128]{1,0:T(8,128)S(1)} %add.30), channel_id=1, source_target_pairs={{0,64},{16,80},{32,96},{48,112},{64,0},{80,16},{96,32},{112,48},{1... | collective-permute-start | bytes 110600 | tf_op jit(solution)/shard_map/ppermute | solution.py:615
  100.3 3.6 %collective-permute-start.12 = (f32[72,128]{1,0:T(8,128)S(1)}, f32[72,128]{1,0:T(8,128)S(1)}, u32[]{:S(2)}, u32[]{:S(2)}) collective-permute-start(f32[72,128]{1,0:T(8,128)S(1)} %add_add_fusion.1), channel_id=1, source_target_pairs={{0,1},{1,0},{2,3},{3,2},{4,5},{5,4},{6,7},{7,6},{8,9},{9,8},{10,11... | collective-permute-start | bytes 110600 | tf_op jit(solution)/shard_map/ppermute | solution.py:615
  106.2 1.8 %collective-permute-start.17 = (f32[72,128]{1,0:T(8,128)S(1)}, f32[72,128]{1,0:T(8,128)S(1)}, u32[]{:S(2)}, u32[]{:S(2)}) collective-permute-start(f32[72,128]{1,0:T(8,128)S(1)} %add_add_fusion.x_ref), channel_id=1, source_target_pairs={{0,12},{1,13},{2,14},{3,15},{4,8},{5,9},{6,10},{7,11},{8,4},{9,5},... | collective-permute-start | bytes 110600 | tf_op jit(solution)/shard_map/ppermute | solution.py:615
  108.1 2.3 %collective-permute-start.15 = (f32[72,128]{1,0:T(8,128)S(1)}, f32[72,128]{1,0:T(8,128)S(1)}, u32[]{:S(2)}, u32[]{:S(2)}) collective-permute-start(f32[72,128]{1,0:T(8,128)S(1)} %add_add_fusion.x_ref), channel_id=1, source_target_pairs={{0,4},{1,5},{2,6},{3,7},{4,0},{5,1},{6,2},{7,3},{8,12},{9,13},{10,... | collective-permute-start | bytes 110600 | tf_op jit(solution)/shard_map/ppermute | solution.py:615
  111.4 2.0 %collective-permute-done.16.g2_ref = f32[72,128]{1,0:T(8,128)S(1)} collective-permute-done((f32[72,128]{1,0:T(8,128)S(1)}, f32[72,128]{1,0:T(8,128)S(1)}, u32[]{:S(2)}, u32[]{:S(2)}) %collective-permute-start.16) | collective-permute-done | bytes 36896 | tf_op jit(solution)/shard_map/ppermute | solution.py:615
  113.5 8.1 %factor.1 = f32[128,128]{1,0:T(8,128)} custom-call(f32[72,128]{1,0:T(8,128)S(1)} %add_add_fusion.x_ref, f32[72,128]{1,0:T(8,128)S(1)} %collective-permute-done.15.g1_ref, f32[72,128]{1,0:T(8,128)S(1)} %collective-permute-done.16.g2_ref, f32[72,128]{1,0:T(8,128)S(1)} %collective-permute-done.17.g3_ref), custom_call_target="tpu_custom_call" | custom-call | tf_op jit(solution)/shard_map/factor/pallas_call | solution.py:601
  (42 shorter events, 16.4 us)
Async XLA Ops:
  0.6 10.1 %copy-start.2 = (s32[32]{0:T(128)S(1)}, s32[32]{0:T(128)}, u32[]{:S(2)}) copy-start(s32[32]{0:T(128)} %counts.3) | copy-start | bytes 388
  3.3 14.0 %collective-permute-start = (f32[1040,128]{1,0:T(8,128)}, f32[1040,128]{1,0:T(8,128)}, u32[]{:S(2)}, u32[]{:S(2)}) collective-permute-start(f32[1040,128]{1,0:T(8,128)} %get-tuple-element.37), channel_id=1, source_target_pairs={{0,16},{16,0},{32,48},{48,32},{64,80},{80,64},{96,112},{112,96},{1... | collective-permute-start | bytes 1597448 | tf_op jit(solution)/shard_map/ppermute | solution.py:561
  3.4 13.9 %collective-permute-start.1 = (f32[1040,128]{1,0:T(8,128)}, f32[1040,128]{1,0:T(8,128)}, u32[]{:S(2)}, u32[]{:S(2)}) collective-permute-start(f32[1040,128]{1,0:T(8,128)} %get-tuple-element.38), channel_id=1, source_target_pairs={{0,112},{16,32},{32,16},{48,64},{64,48},{80,96},{96,80},{112,0},{1... | collective-permute-start | bytes 1597448 | tf_op jit(solution)/shard_map/ppermute | solution.py:561
  6.6 0.8 copy-start
  17.2 8.3 %copy-start.3 = (s32[384]{0:T(512)S(1)}, s32[384]{0:T(512)}, u32[]{:S(2)}) copy-start(s32[384]{0:T(512)} %cell_ref.1) | copy-start | bytes 4612
  17.3 8.3 %copy-start.4 = (s32[384,1]{0,1:T(1,128)S(1)}, s32[384,1]{0,1:T(1,128)}, u32[]{:S(2)}) copy-start(s32[384,1]{0,1:T(1,128)} %param.11) | copy-start | bytes 4612
  18.5 10.7 %collective-permute-start.3 = (f32[200,128]{1,0:T(8,128)S(1)}, f32[200,128]{1,0:T(8,128)S(1)}, u32[]{:S(2)}, u32[]{:S(2)}) collective-permute-start(f32[200,128]{1,0:T(8,128)S(1)} %get-tuple-element.49), channel_id=1, source_target_pairs={{0,15},{1,2},{2,1},{3,4},{4,3},{5,6},{6,5},{7,8},{8,7},{9,10},{10,... | collective-permute-start | bytes 307208 | tf_op jit(solution)/shard_map/ppermute | solution.py:561
  24.8 4.7 %collective-permute-start.2 = (f32[200,128]{1,0:T(8,128)S(1)}, f32[200,128]{1,0:T(8,128)S(1)}, u32[]{:S(2)}, u32[]{:S(2)}) collective-permute-start(f32[200,128]{1,0:T(8,128)S(1)} %get-tuple-element.43.after), channel_id=1, source_target_pairs={{0,1},{1,0},{2,3},{3,2},{4,5},{5,4},{6,7},{7,6},{8,9},{9,8},{10,11... | collective-permute-start | bytes 307208 | tf_op jit(solution)/shard_map/ppermute | solution.py:561
  29.5 37.6 %copy-start.1 = (f32[32,256]{1,0:T(8,128)S(1)}, f32[32,256]{1,0:T(8,128)}, u32[]{:S(2)}) copy-start(f32[32,256]{1,0:T(8,128)} %kappa_ref.5) | copy-start | bytes 98308
  66.0 9.9 %collective-permute-start.5 = (f32[1024,128]{1,0:T(8,128)S(1)}, f32[1024,128]{1,0:T(8,128)S(1)}, u32[]{:S(2)}, u32[]{:S(2)}) collective-permute-start(f32[1024,128]{1,0:T(8,128)S(1)} %get-tuple-element.61), channel_id=1, source_target_pairs={{0,112},{16,32},{32,16},{48,64},{64,48},{80,96},{96,80},{112,0},{1... | collective-permute-start | bytes 1572872 | tf_op jit(solution)/shard_map/ppermute | solution.py:561
  66.1 9.8 %collective-permute-start.4 = (f32[1024,128]{1,0:T(8,128)S(1)}, f32[1024,128]{1,0:T(8,128)S(1)}, u32[]{:S(2)}, u32[]{:S(2)}) collective-permute-start(f32[1024,128]{1,0:T(8,128)S(1)} %get-tuple-element.52.after), channel_id=1, source_target_pairs={{0,16},{16,0},{32,48},{48,32},{64,80},{80,64},{96,112},{112,96},{1... | collective-permute-start | bytes 1572872 | tf_op jit(solution)/shard_map/ppermute | solution.py:561
  76.5 4.5 %collective-permute-start.6 = (f32[160,128]{1,0:T(8,128)S(1)}, f32[160,128]{1,0:T(8,128)S(1)}, u32[]{:S(2)}, u32[]{:S(2)}) collective-permute-start(f32[160,128]{1,0:T(8,128)S(1)} %get-tuple-element.64), channel_id=1, source_target_pairs={{0,1},{1,0},{2,3},{3,2},{4,5},{5,4},{6,7},{7,6},{8,9},{9,8},{10,11... | collective-permute-start | bytes 245768 | tf_op jit(solution)/shard_map/ppermute | solution.py:561
  77.1 7.8 %collective-permute-start.7 = (f32[160,128]{1,0:T(8,128)S(1)}, f32[160,128]{1,0:T(8,128)S(1)}, u32[]{:S(2)}, u32[]{:S(2)}) collective-permute-start(f32[160,128]{1,0:T(8,128)S(1)} %get-tuple-element.65), channel_id=1, source_target_pairs={{0,15},{1,2},{2,1},{3,4},{4,3},{5,6},{6,5},{7,8},{8,7},{9,10},{10,... | collective-permute-start | bytes 245768 | tf_op jit(solution)/shard_map/ppermute | solution.py:561
  91.6 1.3 %collective-permute-start.8 = (f32[72,128]{1,0:T(8,128)S(1)}, f32[72,128]{1,0:T(8,128)S(1)}, u32[]{:S(2)}, u32[]{:S(2)}) collective-permute-start(f32[72,128]{1,0:T(8,128)S(1)} %get-tuple-element.67), channel_id=1, source_target_pairs={{0,16},{16,0},{32,48},{48,32},{64,80},{80,64},{96,112},{112,96},{1... | collective-permute-start | bytes 110600 | tf_op jit(solution)/shard_map/ppermute | solution.py:615
  92.9 5.6 %collective-permute-start.11 = (f32[72,128]{1,0:T(8,128)S(1)}, f32[72,128]{1,0:T(8,128)S(1)}, u32[]{:S(2)}, u32[]{:S(2)}) collective-permute-start(f32[72,128]{1,0:T(8,128)S(1)} %add.30), channel_id=1, source_target_pairs={{0,96},{16,112},{32,64},{48,80},{64,32},{80,48},{96,0},{112,16},{1... | collective-permute-start | bytes 110600 | tf_op jit(solution)/shard_map/ppermute | solution.py:615
  94.0 5.7 %collective-permute-start.10 = (f32[72,128]{1,0:T(8,128)S(1)}, f32[72,128]{1,0:T(8,128)S(1)}, u32[]{:S(2)}, u32[]{:S(2)}) collective-permute-start(f32[72,128]{1,0:T(8,128)S(1)} %add.30), channel_id=1, source_target_pairs={{0,64},{16,80},{32,96},{48,112},{64,0},{80,16},{96,32},{112,48},{1... | collective-permute-start | bytes 110600 | tf_op jit(solution)/shard_map/ppermute | solution.py:615
  95.6 4.0 %collective-permute-start.9 = (f32[72,128]{1,0:T(8,128)S(1)}, f32[72,128]{1,0:T(8,128)S(1)}, u32[]{:S(2)}, u32[]{:S(2)}) collective-permute-start(f32[72,128]{1,0:T(8,128)S(1)} %add.30), channel_id=1, source_target_pairs={{0,32},{16,48},{32,0},{48,16},{64,96},{80,112},{96,64},{112,80},{1... | collective-permute-start | bytes 110600 | tf_op jit(solution)/shard_map/ppermute | solution.py:615
  99.7 5.2 %collective-permute-start.14 = (f32[72,128]{1,0:T(8,128)S(1)}, f32[72,128]{1,0:T(8,128)S(1)}, u32[]{:S(2)}, u32[]{:S(2)}) collective-permute-start(f32[72,128]{1,0:T(8,128)S(1)} %add_add_fusion.1), channel_id=1, source_target_pairs={{0,3},{1,2},{2,1},{3,0},{4,7},{5,6},{6,5},{7,4},{8,11},{9,10},{10,... | collective-permute-start | bytes 110600 | tf_op jit(solution)/shard_map/ppermute | solution.py:615
  100.2 5.5 %collective-permute-start.13 = (f32[72,128]{1,0:T(8,128)S(1)}, f32[72,128]{1,0:T(8,128)S(1)}, u32[]{:S(2)}, u32[]{:S(2)}) collective-permute-start(f32[72,128]{1,0:T(8,128)S(1)} %add_add_fusion.1), channel_id=1, source_target_pairs={{0,2},{1,3},{2,0},{3,1},{4,6},{5,7},{6,4},{7,5},{8,10},{9,11},{10,... | collective-permute-start | bytes 110600 | tf_op jit(solution)/shard_map/ppermute | solution.py:615
  100.3 5.9 %collective-permute-start.12 = (f32[72,128]{1,0:T(8,128)S(1)}, f32[72,128]{1,0:T(8,128)S(1)}, u32[]{:S(2)}, u32[]{:S(2)}) collective-permute-start(f32[72,128]{1,0:T(8,128)S(1)} %add_add_fusion.1), channel_id=1, source_target_pairs={{0,1},{1,0},{2,3},{3,2},{4,5},{5,4},{6,7},{7,6},{8,9},{9,8},{10,11... | collective-permute-start | bytes 110600 | tf_op jit(solution)/shard_map/ppermute | solution.py:615
  106.2 5.2 %collective-permute-start.17 = (f32[72,128]{1,0:T(8,128)S(1)}, f32[72,128]{1,0:T(8,128)S(1)}, u32[]{:S(2)}, u32[]{:S(2)}) collective-permute-start(f32[72,128]{1,0:T(8,128)S(1)} %add_add_fusion.x_ref), channel_id=1, source_target_pairs={{0,12},{1,13},{2,14},{3,15},{4,8},{5,9},{6,10},{7,11},{8,4},{9,5},... | collective-permute-start | bytes 110600 | tf_op jit(solution)/shard_map/ppermute | solution.py:615
  108.0 5.5 %collective-permute-start.16 = (f32[72,128]{1,0:T(8,128)S(1)}, f32[72,128]{1,0:T(8,128)S(1)}, u32[]{:S(2)}, u32[]{:S(2)}) collective-permute-start(f32[72,128]{1,0:T(8,128)S(1)} %add_add_fusion.x_ref), channel_id=1, source_target_pairs={{0,8},{1,9},{2,10},{3,11},{4,12},{5,13},{6,14},{7,15},{8,0},{9,1},... | collective-permute-start | bytes 110600 | tf_op jit(solution)/shard_map/ppermute | solution.py:615
  108.1 5.4 %collective-permute-start.15 = (f32[72,128]{1,0:T(8,128)S(1)}, f32[72,128]{1,0:T(8,128)S(1)}, u32[]{:S(2)}, u32[]{:S(2)}) collective-permute-start(f32[72,128]{1,0:T(8,128)S(1)} %add_add_fusion.x_ref), channel_id=1, source_target_pairs={{0,4},{1,5},{2,6},{3,7},{4,0},{5,1},{6,2},{7,3},{8,12},{9,13},{10,... | collective-permute-start | bytes 110600 | tf_op jit(solution)/shard_map/ppermute | solution.py:615

commit v5 on v4

--- a/solution.py
+++ b/solution.py
@@ -23,10 +23,8 @@
 VMEM_LIMIT = 30 * 1024 * 1024
 LAT_ROWS = H * C + 16
 OWN_ROWS = R * H + R
-LON_OWNERS = 16
 WEIGH_PARTS = 3
 HALF = 64
-EXACT = False
 
 
 def vmem_spec():
@@ -350,33 +348,29 @@
     )(flags, counts, kappa, after, *halos)
 
 
-def places_kernel(count_ref, cell_ref, owner_ref, after, row_ref, place_ref, seen):
-    for i in range(LON_OWNERS):
-        seen[i] = 0
+def places_kernel(count_ref, cell_ref, owner_ref, after, row_ref, place_ref):
     count = count_ref[0]
-
-    def one(t, _):
-        owner = owner_ref[0, t]
-        rank = seen[owner]
-        live = t < count
-        seen[owner] = rank + jnp.where(live, 1, 0)
-        place_ref[t] = jnp.where(live, owner * CAP + rank, PLACES)
-        cell = cell_ref[t]
-        row_ref[t] = OFF + 8 + H * CB + (cell >> 8) * CB + (cell & (C - 1))
-        return 0
-
-    lax.fori_loop(0, SLOTS, one, 0, unroll=8)
+    owner = owner_ref[...]
+    cell = cell_ref[...]
+    row_ref[...] = OFF + 8 + H * CB + (cell >> 8) * CB + (cell & (C - 1))
+    owners = jnp.broadcast_to(owner, (SLOTS, SLOTS))
+    later = lax.broadcasted_iota(jnp.int32, (SLOTS, SLOTS), 1)
+    earlier = lax.broadcasted_iota(jnp.int32, (SLOTS, SLOTS), 0)
+    column = jnp.broadcast_to(owner.astype(jnp.float32), (8, SLOTS)).T[:, :1].astype(jnp.int32)
+    same = (owners == column) & (earlier < later)
+    rank = jnp.sum(jnp.where(same, 1.0, 0.0), axis=0, keepdims=True).astype(jnp.int32)
+    slot = lax.broadcasted_iota(jnp.int32, (1, SLOTS), 1)
+    place_ref[...] = jnp.where(slot < count, owner * CAP + rank, PLACES)
 
 
 def places(count, cell, owner, after):
     return pl.pallas_call(
         places_kernel,
-        in_specs=[smem_spec()] * 3 + [pl.BlockSpec(memory_space=pl.ANY)],
-        out_specs=[smem_spec()] * 2,
-        out_shape=[jax.ShapeDtypeStruct((SLOTS,), jnp.int32)] * 2,
-        scratch_shapes=[pltpu.SMEM((LON_OWNERS,), jnp.int32)],
+        in_specs=[smem_spec()] + [vmem_spec()] * 2 + [pl.BlockSpec(memory_space=pl.ANY)],
+        out_specs=[vmem_spec()] * 2,
+        out_shape=[jax.ShapeDtypeStruct((1, SLOTS), jnp.int32)] * 2,
         cost_estimate=pl.CostEstimate(flops=0, bytes_accessed=4 * 1024 * 1024, transcendentals=0),
-        compiler_params=pltpu.CompilerParams(vmem_limit_bytes=1024 * 1024),
+        compiler_params=pltpu.CompilerParams(vmem_limit_bytes=4 * 1024 * 1024),
         name="places",
     )(count, cell, owner, after)
 
@@ -395,7 +389,7 @@
     def copy(i, _):
         for j in range(8):
             t = i * 8 + j
-            rows_ref[pl.ds(place_ref[t], 1), :] = l4[pl.ds(cell_ref[t], 1), :]
+            rows_ref[pl.ds(place_ref[0, t], 1), :] = l4[pl.ds(cell_ref[0, t], 1), :]
         return 0
 
     lax.fori_loop(0, SLOTS // 8, copy, 0)
@@ -455,12 +449,20 @@
 def spread_kernel(flags, cell_ref, place_ref, count_ref, ret_ref, field, pay_a, pay_b, own_a, own_b):
     field[...] = jnp.zeros_like(field)
 
-    def add(t, _):
-        i = pl.ds(cell_ref[t], 1)
-        field[i, :] = field[i, :] + ret_ref[pl.ds(place_ref[t], 1), :]
+    count = count_ref[0]
+
+    def add(i, _):
+        rows, cells = [], []
+        for j in range(8):
+            t = i * 8 + j
+            live = t < count
+            rows.append(ret_ref[pl.ds(jnp.where(live, place_ref[0, t], 0), 1), :])
+            cells.append(jnp.where(live, cell_ref[0, t], NROW + OFF))
+        for row, cell in zip(rows, cells):
+            field[pl.ds(cell, 1), :] = field[pl.ds(cell, 1), :] + row
         return 0
 
-    lax.fori_loop(0, count_ref[0], add, 0)
+    lax.fori_loop(0, (count + 7) // 8, add, 0)
     odd = flags[0]
     lon_odd = flags[2]
     for pay, low in ((pay_a, odd), (pay_b, 1 - odd)):
@@ -572,28 +574,38 @@
     a_ref[HALF:, :] = jnp.concatenate([jnp.zeros((HALF, HALF), jnp.float32), lower], axis=1)
     sub = lax.broadcasted_iota(jnp.int32, (8, K), 0)
     col = lax.broadcasted_iota(jnp.int32, (8, K), 1)
+    wide = lambda x: jnp.broadcast_to(x, (8, K))
+    panels, last = [], None
     for q in range(K // 8):
         c = 8 * q
         panel = a_ref[c:c + 8, :]
-        if q > 0:
-            done = out_ref[:c, :]
+        if q > 1:
+            done = jnp.concatenate(panels[:q - 1], axis=0)
             panel = panel - lax.dot_general(
                 done[:, c:c + 8], done, (((0,), (0,)), ((), ())),
                 precision=lax.Precision.HIGHEST, preferred_element_type=jnp.float32)
-        b = [[jnp.broadcast_to(panel[i:i + 1, c + m:c + m + 1], (8, K)) if m >= i else None for m in range(8)]
-             for i in range(8)]
-        rows = [jnp.broadcast_to(panel[i:i + 1, :], (8, K)) for i in range(8)]
+        b = {(i, m): wide(panel[i:i + 1, c + m:c + m + 1]) for i in range(8) for m in range(i, 8)}
+        rows = [wide(panel[i:i + 1, :]) for i in range(8)]
+        if q > 0:
+            for k in range(8):
+                e = [wide(last[k][:, c + m:c + m + 1]) for m in range(8)]
+                for i in range(8):
+                    for m in range(i, 8):
+                        b[i, m] = b[i, m] - e[i] * e[m]
+                    rows[i] = rows[i] - e[i] * last[k]
         result = jnp.zeros((8, K), jnp.float32)
         for i in range(8):
-            inv = 1.0 / jnp.sqrt(b[i][i]) if EXACT else lax.rsqrt(b[i][i])
-            u = [b[i][m] * inv if m > i else None for m in range(8)]
+            inv = lax.rsqrt(b[i, i])
+            u = {m: b[i, m] * inv for m in range(i + 1, 8)}
             for m in range(i + 1, 8):
                 for k in range(m, 8):
-                    b[m][k] = b[m][k] - u[m] * u[k]
+                    b[m, k] = b[m, k] - u[m] * u[k]
             rows[i] = rows[i] * inv
             for m in range(i + 1, 8):
                 rows[m] = rows[m] - u[m] * rows[i]
             result = jnp.where(sub == i, rows[i], result)
+        last = rows
+        panels.append(result)
         out_ref[c:c + 8, :] = jnp.where(col >= sub + c, result, 0.0)
 
 
@@ -636,7 +648,7 @@
     levels = inner(ext, kap, act)
     count = obs_count.reshape(1)
     lon_pay = corner(flags, own_a, own_b, lat_a, lat_b, levels[-1])
-    cell, place = places(count, obs_cell, obs_owner.reshape(1, SLOTS), lon_pay[0])
+    cell, place = places(count, obs_cell.reshape(1, SLOTS), obs_owner.reshape(1, SLOTS), lon_pay[0])
     lon_a, lon_b = swap(*lon_pay, "lon")
     outgoing, tail_a, tail_b = smooth(flags, cell, place, ext, levels, kap, act, (lat_a, lat_b, lon_a, lon_b))
     buffer = lax.all_to_all(outgoing, "lon", split_axis=0, concat_axis=0, tiled=True)

time: 122 us -> 119 us (0.975)
  Pallas kernels: 50.5 us -> 44.1 us
  waiting for transfers between devices: 16.2 us -> 19.9 us
    pallas_call x1, Pallas kernels: 3.7 us -> 0.28 us  [places(): pl.pallas_call(places_kernel, in_specs=[smem_spec()] + [vmem_spec()] * 2...]
    pallas_call x1, Pallas kernels: 8.09 us -> 5.68 us  [factor(): pl.pallas_call(functools.partial(factor_kernel, scale), in_specs=[vmem_sp...]
    ppermute x4, waiting for transfers between devices: 1.87 us -> 3.86 us  [swap(): lax.ppermute(a, axis, pairs(size, 0))]
    ppermute x4, waiting for transfers between devices: 5.09 us -> 6.75 us  [swap(): lax.ppermute(b, axis, pairs(size, 1))]
  transfers between devices with their start and end apart: 18 -> 18, of which waited for: 12 -> 13; matrix products, arithmetic and copies ran while one was open for 0% -> 0% of each run, Pallas kernels for 17% -> 15%
where the time goes in v5:
time: 119 us; the launch traced here: 118 us
  Pallas kernels  44.1 us (37%)
  blocking collectives  26.3 us (22%)
  starting transfers between devices  25.7 us (22%)
  waiting for transfers between devices  19.9 us (17%)
  between operations  1.49 us (1%)
    all_to_all x1, blocking collectives, shards(): lax.all_to_all(outgoing, 'lon', split_axis=0, concat_axis=0, tiled=True)  13.6 us
    all_to_all x1, blocking collectives, shards(): lax.all_to_all(mixed, 'lon', split_axis=0, concat_axis=0, tiled=True)  12.6 us
    ppermute x10, starting transfers between devices, stage(): lax.ppermute(x, axis, [(i, i ^ d) for i in range(size)])  12.5 us
    ppermute x4, starting transfers between devices, swap(): lax.ppermute(b, axis, pairs(size, 1))  12.1 us
    pallas_call x2, Pallas kernels, inner(): pl.pallas_call(inner_kernel, in_specs=[vmem_spec()] * 3, out_specs=[vmem_...  9.79 us
    ppermute x10, waiting for transfers between devices, stage(): lax.ppermute(x, axis, [(i, i ^ d) for i in range(size)])  9.27 us
    pallas_call x1, Pallas kernels, finish(): pl.pallas_call(finish_kernel, in_specs=[smem_spec()] + [vmem_spec()] * 11...  6.76 us
    ppermute x4, waiting for transfers between devices, swap(): lax.ppermute(b, axis, pairs(size, 1))  6.75 us
  transfers between devices with their start and end apart: 18, of which 13 were waited for; matrix products, arithmetic and copies ran while one was open for 0% of the time, Pallas kernels for 15%

profile of v5, /device:TPU:0, one launch (start us, length us, event | category | flops | bytes accessed | tf_op | source)
XLA Modules:
  0.0 118.3 jit_solution(3727985434055039476)
XLA Ops:
  0.6 2.6 %edge_pack.1 = (f32[1040,128]{1,0:T(8,128)}, f32[1040,128]{1,0:T(8,128)}) custom-call(s32[32]{0:T(128)} %counts.3, f32[32,256]{1,0:T(8,128)} %kappa_ref.5, f32[128,32,256]{2,1,0:T(8,128)} %refs_11_.1), custom_call_target="tpu_custom_call" | custom-call | tf_op jit(solution)/shard_map/edge_pack/pallas_call | solution.py:102
  3.4 3.2 %collective-permute-start.1 = (f32[1040,128]{1,0:T(8,128)}, f32[1040,128]{1,0:T(8,128)}, u32[]{:S(2)}, u32[]{:S(2)}) collective-permute-start(f32[1040,128]{1,0:T(8,128)} %get-tuple-element.38), channel_id=1, source_target_pairs={{0,112},{16,32},{32,16},{48,64},{64,48},{80,96},{96,80},{112,0},{1... | collective-permute-start | bytes 1597448 | tf_op jit(solution)/shard_map/ppermute | solution.py:563
  7.4 3.3 %turn.1 = (f32[10896,128]{1,0:T(8,128)S(1)}, f32[160,128]{1,0:T(8,128)S(1)}, f32[160,128]{1,0:T(8,128)S(1)}) custom-call(s32[4]{0:T(128)S(1)} %pad_add_fusion.flags, f32[32,256]{1,0:T(8,128)S(1)} %copy-done, f32[128,32,256]{2,1,0:T(8,128)} %refs_11_.1), custom_call_target="tpu_custom_call" | custom-call | bytes 12582912 | tf_op jit(solution)/shard_map/turn/pallas_call | solution.py:143
  10.7 1.8 %coeffs.2 = (f32[10896,128]{1,0:T(8,128)S(1)}, f32[4,40,8,128]{3,2,1,0:T(8,128)S(1)}) custom-call(s32[4]{0:T(128)S(1)} %pad_add_fusion.flags, s32[32]{0:T(128)S(1)} %copy-done.2, f32[32,256]{1,0:T(8,128)S(1)} %copy-done, f32[160,128]{1,0:T(8,128)S(1)} %get-tuple-element.35.after.own_a), custom_call_target="tpu_custom_call" | custom-call | bytes 4194304 | tf_op jit(solution)/shard_map/coeffs/pallas_call | solution.py:340
  12.5 4.7 %inner.2 = (f32[10896,128]{1,0:T(8,128)S(1)}, f32[10896,128]{1,0:T(8,128)S(1)}, f32[10896,128]{1,0:T(8,128)S(1)}, f32[10896,128]{1,0:T(8,128)S(1)}) custom-call(f32[10896,128]{1,0:T(8,128)S(1)} %get-tuple-element.39.ext.refs_0_, f32[10896,128]{1,0:T(8,128)S(1)} %get-tuple-element.40.kap.refs_5_, f32[4,40,8,128]{3,2,1,0:T(8,128)S(1)} %get-tuple-element.41.act.refs_6_), custom_call_target="tpu_custom_call" | custom-call | bytes 16777216 | tf_op jit(solution)/shard_map/inner/pallas_call | solution.py:302
  18.5 6.3 %collective-permute-start.3 = (f32[200,128]{1,0:T(8,128)S(1)}, f32[200,128]{1,0:T(8,128)S(1)}, u32[]{:S(2)}, u32[]{:S(2)}) collective-permute-start(f32[200,128]{1,0:T(8,128)S(1)} %get-tuple-element.49), channel_id=1, source_target_pairs={{0,15},{1,2},{2,1},{3,4},{4,3},{5,6},{6,5},{7,8},{8,7},{9,10},{10,... | collective-permute-start | bytes 307208 | tf_op jit(solution)/shard_map/ppermute | solution.py:563
  27.5 2.0 %collective-permute-done.2.refs_9_.rest_2_ = f32[200,128]{1,0:T(8,128)S(1)} collective-permute-done((f32[200,128]{1,0:T(8,128)S(1)}, f32[200,128]{1,0:T(8,128)S(1)}, u32[]{:S(2)}, u32[]{:S(2)}) %collective-permute-start.2) | collective-permute-done | bytes 102432 | tf_op jit(solution)/shard_map/ppermute | solution.py:563
  29.5 4.6 %smooth.1 = (f32[768,128]{1,0:T(8,128)S(1)}, f32[16,128]{1,0:T(8,128)S(1)}, f32[16,128]{1,0:T(8,128)S(1)}, f32[10896,128]{1,0:T(8,128)S(1)}, f32[10896,128]{1,0:...) custom-call(s32[4]{0:T(128)S(1)} %pad_add_fusion.flags, ...), custom_call_target="tpu_custom_call", output_to_operand_aliasing={{3}: (3, {}), {4}: (4, {}), {5}: (5, {}), {6}: (6, {}), {7}... | custom-call | tf_op jit(solution)/shard_map/smooth/pallas_call | solution.py:400
  34.1 13.6 %all_to_all.22 = f32[16,48,128]{2,1,0:T(8,128)S(1)} all-to-all(f32[16,48,128]{2,1,0:T(8,128)S(1)} %bitcast.16), channel_id=1, replica_groups=mesh['lat'=8,'lon'=16] {'lon'}, dimensions={0} | all-to-all | bytes 786432 | tf_op jit(solution)/shard_map/all_to_all | solution.py:654
  47.8 2.7 %weigh.1 = f32[768,128]{1,0:T(8,128)S(1)} custom-call(f32[768,128]{1,0:T(8,128)S(1)} %bitcast.14, f32[768,768]{1,0:T(8,128)} %bitcast.18), custom_call_target="tpu_custom_call" | custom-call | tf_op jit(solution)/shard_map/weigh/pallas_call | solution.py:435
  50.5 12.6 %all_to_all.23 = f32[16,48,128]{2,1,0:T(8,128)S(1)} all-to-all(f32[16,48,128]{2,1,0:T(8,128)S(1)} %bitcast.15), channel_id=1, replica_groups=mesh['lat'=8,'lon'=16] {'lon'}, dimensions={0} | all-to-all | bytes 786432 | tf_op jit(solution)/shard_map/all_to_all | solution.py:656
  63.1 2.3 %spread.1 = (f32[10896,128]{1,0:T(8,128)S(1)}, f32[1024,128]{1,0:T(8,128)S(1)}, f32[1024,128]{1,0:T(8,128)S(1)}, f32[128,128]{1,0:T(8,128)S(1)}, f32[128,128]{1,0:T(8,128)S(1)}) custom-call(s32[4]{0:T(128)S(1)} %pad_add_fusion.flags, s32[1,384]{1,0:T(1,128)S(1)} %get-tuple-element.44.cell_ref, s32[1,384]{1,0:T(1,128)S(1)} %get-tuple-element.45.place_ref, ...), custom_call_target="tpu_custom_call" | custom-call | tf_op jit(solution)/shard_map/spread/pallas_call | solution.py:480
  66.4 2.4 %coeffs.3 = (f32[10896,128]{1,0:T(8,128)S(1)}, f32[4,40,8,128]{3,2,1,0:T(8,128)S(1)}) custom-call(s32[4]{0:T(128)S(1)} %pad_add_fusion.flags, s32[32]{0:T(128)S(1)} %copy-done.2, f32[32,256]{1,0:T(8,128)S(1)} %copy-done.1, f32[1024,128]{1,0:T(8,128)S(1)} %get-tuple-element.52.after, f32[16,128]{1,0:T(8,128)S(1)} %get-tuple-element.53.rest_0_, ...), custom_call_target="tpu_custom_call" | custom-call | bytes 4194304 | tf_op jit(solution)/shard_map/coeffs/pallas_call | solution.py:340
  68.8 5.1 %inner.3 = (f32[10896,128]{1,0:T(8,128)S(1)}, f32[10896,128]{1,0:T(8,128)S(1)}, f32[10896,128]{1,0:T(8,128)S(1)}, f32[10896,128]{1,0:T(8,128)S(1)}) custom-call(f32[10896,128]{1,0:T(8,128)S(1)} %get-tuple-element.51.ext.refs_0_, f32[10896,128]{1,0:T(8,128)S(1)} %get-tuple-element.55.kap.refs_5_, f32[4,40,8,128]{3,2,1,0:T(8,128)S(1)} %get-tuple-element.56.act.refs_6_), custom_call_target="tpu_custom_call" | custom-call | bytes 16777216 | tf_op jit(solution)/shard_map/inner/pallas_call | solution.py:302
  76.1 2.5 %collective-permute-start.7 = (f32[160,128]{1,0:T(8,128)S(1)}, f32[160,128]{1,0:T(8,128)S(1)}, u32[]{:S(2)}, u32[]{:S(2)}) collective-permute-start(f32[160,128]{1,0:T(8,128)S(1)} %get-tuple-element.65), channel_id=1, source_target_pairs={{0,15},{1,2},{2,1},{3,4},{4,3},{5,6},{6,5},{7,8},{8,7},{9,10},{10,... | collective-permute-start | bytes 245768 | tf_op jit(solution)/shard_map/ppermute | solution.py:563
  78.6 1.8 %collective-permute-done.6.refs_9_ = f32[160,128]{1,0:T(8,128)S(1)} collective-permute-done((f32[160,128]{1,0:T(8,128)S(1)}, f32[160,128]{1,0:T(8,128)S(1)}, u32[]{:S(2)}, u32[]{:S(2)}) %collective-permute-start.6) | collective-permute-done | bytes 81952 | tf_op jit(solution)/shard_map/ppermute | solution.py:563
  80.5 3.6 %collective-permute-done.7.refs_10_ = f32[160,128]{1,0:T(8,128)S(1)} collective-permute-done((f32[160,128]{1,0:T(8,128)S(1)}, f32[160,128]{1,0:T(8,128)S(1)}, u32[]{:S(2)}, u32[]{:S(2)}) %collective-permute-start.7) | collective-permute-done | bytes 81952 | tf_op jit(solution)/shard_map/ppermute | solution.py:563
  84.0 6.8 %finish.1 = (f32[128,32,256]{2,1,0:T(8,128)}, f32[72,128]{1,0:T(8,128)S(1)}, f32[10896,128]{1,0:T(8,128)S(1)}, f32[10896,128]{1,0:T(8,128)S(1)}, f32[10896,128]{...) custom-call(s32[4]{0:T(128)S(1)} %pad_add_fusion.flags, ...), custom_call_target="tpu_custom_call", output_to_operand_aliasing={{2}: (1, {}), {3}: (2, {}), {4}: (3, {}), {5}: (4, {}), {6}... | custom-call | tf_op jit(solution)/shard_map/finish/pallas_call | solution.py:541
  94.5 1.7 %collective-permute-start.9 = (f32[72,128]{1,0:T(8,128)S(1)}, f32[72,128]{1,0:T(8,128)S(1)}, u32[]{:S(2)}, u32[]{:S(2)}) collective-permute-start(f32[72,128]{1,0:T(8,128)S(1)} %add.30), channel_id=1, source_target_pairs={{0,32},{16,48},{32,0},{48,16},{64,96},{80,112},{96,64},{112,80},{1... | collective-permute-start | bytes 110600 | tf_op jit(solution)/shard_map/ppermute | solution.py:627
  99.2 3.6 %collective-permute-start.12 = (f32[72,128]{1,0:T(8,128)S(1)}, f32[72,128]{1,0:T(8,128)S(1)}, u32[]{:S(2)}, u32[]{:S(2)}) collective-permute-start(f32[72,128]{1,0:T(8,128)S(1)} %add_add_fusion.1), channel_id=1, source_target_pairs={{0,1},{1,0},{2,3},{3,2},{4,5},{5,4},{6,7},{7,6},{8,9},{9,8},{10,11... | collective-permute-start | bytes 110600 | tf_op jit(solution)/shard_map/ppermute | solution.py:627
  105.2 2.0 %collective-permute-start.17 = (f32[72,128]{1,0:T(8,128)S(1)}, f32[72,128]{1,0:T(8,128)S(1)}, u32[]{:S(2)}, u32[]{:S(2)}) collective-permute-start(f32[72,128]{1,0:T(8,128)S(1)} %add_add_fusion.x_ref), channel_id=1, source_target_pairs={{0,12},{1,13},{2,14},{3,15},{4,8},{5,9},{6,10},{7,11},{8,4},{9,5},... | collective-permute-start | bytes 110600 | tf_op jit(solution)/shard_map/ppermute | solution.py:627
  107.2 2.1 %collective-permute-start.15 = (f32[72,128]{1,0:T(8,128)S(1)}, f32[72,128]{1,0:T(8,128)S(1)}, u32[]{:S(2)}, u32[]{:S(2)}) collective-permute-start(f32[72,128]{1,0:T(8,128)S(1)} %add_add_fusion.x_ref), channel_id=1, source_target_pairs={{0,4},{1,5},{2,6},{3,7},{4,0},{5,1},{6,2},{7,3},{8,12},{9,13},{10,... | collective-permute-start | bytes 110600 | tf_op jit(solution)/shard_map/ppermute | solution.py:627
  110.4 2.2 %collective-permute-done.16.g2_ref = f32[72,128]{1,0:T(8,128)S(1)} collective-permute-done((f32[72,128]{1,0:T(8,128)S(1)}, f32[72,128]{1,0:T(8,128)S(1)}, u32[]{:S(2)}, u32[]{:S(2)}) %collective-permute-start.16) | collective-permute-done | bytes 36896 | tf_op jit(solution)/shard_map/ppermute | solution.py:627
  112.7 5.7 %factor.1 = f32[128,128]{1,0:T(8,128)} custom-call(f32[72,128]{1,0:T(8,128)S(1)} %add_add_fusion.x_ref, f32[72,128]{1,0:T(8,128)S(1)} %collective-permute-done.15.g1_ref, f32[72,128]{1,0:T(8,128)S(1)} %collective-permute-done.16.g2_ref, f32[72,128]{1,0:T(8,128)S(1)} %collective-permute-done.17.g3_ref), custom_call_target="tpu_custom_call" | custom-call | tf_op jit(solution)/shard_map/factor/pallas_call | solution.py:613
  (43 shorter events, 17.3 us)
Async XLA Ops:
  0.6 10.1 %copy-start.2 = (s32[32]{0:T(128)S(1)}, s32[32]{0:T(128)}, u32[]{:S(2)}) copy-start(s32[32]{0:T(128)} %counts.3) | copy-start | bytes 388
  3.3 14.0 %collective-permute-start = (f32[1040,128]{1,0:T(8,128)}, f32[1040,128]{1,0:T(8,128)}, u32[]{:S(2)}, u32[]{:S(2)}) collective-permute-start(f32[1040,128]{1,0:T(8,128)} %get-tuple-element.37), channel_id=1, source_target_pairs={{0,16},{16,0},{32,48},{48,32},{64,80},{80,64},{96,112},{112,96},{1... | collective-permute-start | bytes 1597448 | tf_op jit(solution)/shard_map/ppermute | solution.py:563
  3.4 13.9 %collective-permute-start.1 = (f32[1040,128]{1,0:T(8,128)}, f32[1040,128]{1,0:T(8,128)}, u32[]{:S(2)}, u32[]{:S(2)}) collective-permute-start(f32[1040,128]{1,0:T(8,128)} %get-tuple-element.38), channel_id=1, source_target_pairs={{0,112},{16,32},{32,16},{48,64},{64,48},{80,96},{96,80},{112,0},{1... | collective-permute-start | bytes 1597448 | tf_op jit(solution)/shard_map/ppermute | solution.py:563
  6.6 0.8 copy-start
  17.2 8.3 %copy-start.4 = (s32[384]{0:T(512)S(1)}, s32[384]{0:T(512)}, u32[]{:S(2)}) copy-start(s32[384]{0:T(512)} %param.10) | copy-start | bytes 4612
  17.3 8.3 %copy-start.3 = (s32[384,1]{0,1:T(1,128)S(1)}, s32[384,1]{0,1:T(1,128)}, u32[]{:S(2)}) copy-start(s32[384,1]{0,1:T(1,128)} %param.11) | copy-start | bytes 4612
  18.5 9.0 %collective-permute-start.3 = (f32[200,128]{1,0:T(8,128)S(1)}, f32[200,128]{1,0:T(8,128)S(1)}, u32[]{:S(2)}, u32[]{:S(2)}) collective-permute-start(f32[200,128]{1,0:T(8,128)S(1)} %get-tuple-element.49), channel_id=1, source_target_pairs={{0,15},{1,2},{2,1},{3,4},{4,3},{5,6},{6,5},{7,8},{8,7},{9,10},{10,... | collective-permute-start | bytes 307208 | tf_op jit(solution)/shard_map/ppermute | solution.py:563
  24.8 4.7 %collective-permute-start.2 = (f32[200,128]{1,0:T(8,128)S(1)}, f32[200,128]{1,0:T(8,128)S(1)}, u32[]{:S(2)}, u32[]{:S(2)}) collective-permute-start(f32[200,128]{1,0:T(8,128)S(1)} %get-tuple-element.43.after), channel_id=1, source_target_pairs={{0,1},{1,0},{2,3},{3,2},{4,5},{5,4},{6,7},{7,6},{8,9},{9,8},{10,11... | collective-permute-start | bytes 307208 | tf_op jit(solution)/shard_map/ppermute | solution.py:563
  29.5 36.9 %copy-start.1 = (f32[32,256]{1,0:T(8,128)S(1)}, f32[32,256]{1,0:T(8,128)}, u32[]{:S(2)}) copy-start(f32[32,256]{1,0:T(8,128)} %kappa_ref.5) | copy-start | bytes 98308
  65.5 9.9 %collective-permute-start.5 = (f32[1024,128]{1,0:T(8,128)S(1)}, f32[1024,128]{1,0:T(8,128)S(1)}, u32[]{:S(2)}, u32[]{:S(2)}) collective-permute-start(f32[1024,128]{1,0:T(8,128)S(1)} %get-tuple-element.61), channel_id=1, source_target_pairs={{0,112},{16,32},{32,16},{48,64},{64,48},{80,96},{96,80},{112,0},{1... | collective-permute-start | bytes 1572872 | tf_op jit(solution)/shard_map/ppermute | solution.py:563
  65.6 9.8 %collective-permute-start.4 = (f32[1024,128]{1,0:T(8,128)S(1)}, f32[1024,128]{1,0:T(8,128)S(1)}, u32[]{:S(2)}, u32[]{:S(2)}) collective-permute-start(f32[1024,128]{1,0:T(8,128)S(1)} %get-tuple-element.52.after), channel_id=1, source_target_pairs={{0,16},{16,0},{32,48},{48,32},{64,80},{80,64},{96,112},{112,96},{1... | collective-permute-start | bytes 1572872 | tf_op jit(solution)/shard_map/ppermute | solution.py:563
  75.9 4.5 %collective-permute-start.6 = (f32[160,128]{1,0:T(8,128)S(1)}, f32[160,128]{1,0:T(8,128)S(1)}, u32[]{:S(2)}, u32[]{:S(2)}) collective-permute-start(f32[160,128]{1,0:T(8,128)S(1)} %get-tuple-element.64), channel_id=1, source_target_pairs={{0,1},{1,0},{2,3},{3,2},{4,5},{5,4},{6,7},{7,6},{8,9},{9,8},{10,11... | collective-permute-start | bytes 245768 | tf_op jit(solution)/shard_map/ppermute | solution.py:563
  76.1 8.0 %collective-permute-start.7 = (f32[160,128]{1,0:T(8,128)S(1)}, f32[160,128]{1,0:T(8,128)S(1)}, u32[]{:S(2)}, u32[]{:S(2)}) collective-permute-start(f32[160,128]{1,0:T(8,128)S(1)} %get-tuple-element.65), channel_id=1, source_target_pairs={{0,15},{1,2},{2,1},{3,4},{4,3},{5,6},{6,5},{7,8},{8,7},{9,10},{10,... | collective-permute-start | bytes 245768 | tf_op jit(solution)/shard_map/ppermute | solution.py:563
  90.8 1.3 %collective-permute-start.8 = (f32[72,128]{1,0:T(8,128)S(1)}, f32[72,128]{1,0:T(8,128)S(1)}, u32[]{:S(2)}, u32[]{:S(2)}) collective-permute-start(f32[72,128]{1,0:T(8,128)S(1)} %get-tuple-element.67), channel_id=1, source_target_pairs={{0,16},{16,0},{32,48},{48,32},{64,80},{80,64},{96,112},{112,96},{1... | collective-permute-start | bytes 110600 | tf_op jit(solution)/shard_map/ppermute | solution.py:627
  92.1 5.6 %collective-permute-start.11 = (f32[72,128]{1,0:T(8,128)S(1)}, f32[72,128]{1,0:T(8,128)S(1)}, u32[]{:S(2)}, u32[]{:S(2)}) collective-permute-start(f32[72,128]{1,0:T(8,128)S(1)} %add.30), channel_id=1, source_target_pairs={{0,96},{16,112},{32,64},{48,80},{64,32},{80,48},{96,0},{112,16},{1... | collective-permute-start | bytes 110600 | tf_op jit(solution)/shard_map/ppermute | solution.py:627
  93.2 5.5 %collective-permute-start.10 = (f32[72,128]{1,0:T(8,128)S(1)}, f32[72,128]{1,0:T(8,128)S(1)}, u32[]{:S(2)}, u32[]{:S(2)}) collective-permute-start(f32[72,128]{1,0:T(8,128)S(1)} %add.30), channel_id=1, source_target_pairs={{0,64},{16,80},{32,96},{48,112},{64,0},{80,16},{96,32},{112,48},{1... | collective-permute-start | bytes 110600 | tf_op jit(solution)/shard_map/ppermute | solution.py:627
  94.5 4.2 %collective-permute-start.9 = (f32[72,128]{1,0:T(8,128)S(1)}, f32[72,128]{1,0:T(8,128)S(1)}, u32[]{:S(2)}, u32[]{:S(2)}) collective-permute-start(f32[72,128]{1,0:T(8,128)S(1)} %add.30), channel_id=1, source_target_pairs={{0,32},{16,48},{32,0},{48,16},{64,96},{80,112},{96,64},{112,80},{1... | collective-permute-start | bytes 110600 | tf_op jit(solution)/shard_map/ppermute | solution.py:627
  98.7 5.2 %collective-permute-start.14 = (f32[72,128]{1,0:T(8,128)S(1)}, f32[72,128]{1,0:T(8,128)S(1)}, u32[]{:S(2)}, u32[]{:S(2)}) collective-permute-start(f32[72,128]{1,0:T(8,128)S(1)} %add_add_fusion.1), channel_id=1, source_target_pairs={{0,3},{1,2},{2,1},{3,0},{4,7},{5,6},{6,5},{7,4},{8,11},{9,10},{10,... | collective-permute-start | bytes 110600 | tf_op jit(solution)/shard_map/ppermute | solution.py:627
  99.2 5.5 %collective-permute-start.13 = (f32[72,128]{1,0:T(8,128)S(1)}, f32[72,128]{1,0:T(8,128)S(1)}, u32[]{:S(2)}, u32[]{:S(2)}) collective-permute-start(f32[72,128]{1,0:T(8,128)S(1)} %add_add_fusion.1), channel_id=1, source_target_pairs={{0,2},{1,3},{2,0},{3,1},{4,6},{5,7},{6,4},{7,5},{8,10},{9,11},{10,... | collective-permute-start | bytes 110600 | tf_op jit(solution)/shard_map/ppermute | solution.py:627
  99.2 5.9 %collective-permute-start.12 = (f32[72,128]{1,0:T(8,128)S(1)}, f32[72,128]{1,0:T(8,128)S(1)}, u32[]{:S(2)}, u32[]{:S(2)}) collective-permute-start(f32[72,128]{1,0:T(8,128)S(1)} %add_add_fusion.1), channel_id=1, source_target_pairs={{0,1},{1,0},{2,3},{3,2},{4,5},{5,4},{6,7},{7,6},{8,9},{9,8},{10,11... | collective-permute-start | bytes 110600 | tf_op jit(solution)/shard_map/ppermute | solution.py:627
  105.2 5.2 %collective-permute-start.17 = (f32[72,128]{1,0:T(8,128)S(1)}, f32[72,128]{1,0:T(8,128)S(1)}, u32[]{:S(2)}, u32[]{:S(2)}) collective-permute-start(f32[72,128]{1,0:T(8,128)S(1)} %add_add_fusion.x_ref), channel_id=1, source_target_pairs={{0,12},{1,13},{2,14},{3,15},{4,8},{5,9},{6,10},{7,11},{8,4},{9,5},... | collective-permute-start | bytes 110600 | tf_op jit(solution)/shard_map/ppermute | solution.py:627
  107.2 5.5 %collective-permute-start.16 = (f32[72,128]{1,0:T(8,128)S(1)}, f32[72,128]{1,0:T(8,128)S(1)}, u32[]{:S(2)}, u32[]{:S(2)}) collective-permute-start(f32[72,128]{1,0:T(8,128)S(1)} %add_add_fusion.x_ref), channel_id=1, source_target_pairs={{0,8},{1,9},{2,10},{3,11},{4,12},{5,13},{6,14},{7,15},{8,0},{9,1},... | collective-permute-start | bytes 110600 | tf_op jit(solution)/shard_map/ppermute | solution.py:627
  107.2 5.5 %collective-permute-start.15 = (f32[72,128]{1,0:T(8,128)S(1)}, f32[72,128]{1,0:T(8,128)S(1)}, u32[]{:S(2)}, u32[]{:S(2)}) collective-permute-start(f32[72,128]{1,0:T(8,128)S(1)} %add_add_fusion.x_ref), channel_id=1, source_target_pairs={{0,4},{1,5},{2,6},{3,7},{4,0},{5,1},{6,2},{7,3},{8,12},{9,13},{10,... | collective-permute-start | bytes 110600 | tf_op jit(solution)/shard_map/ppermute | solution.py:627

commit v6 on v5

--- a/solution.py
+++ b/solution.py
@@ -146,7 +146,7 @@
         out_specs=[vmem_spec()] * 3,
         out_shape=[held(NROW + 16, K), held(OWN_ROWS, K), held(OWN_ROWS, K)],
         scratch_shapes=[pltpu.VMEM((8, K, 8, LANES), jnp.float32), pltpu.SemaphoreType.DMA((8,))],
-        compiler_params=pltpu.CompilerParams(vmem_limit_bytes=12 * 1024 * 1024),
+        compiler_params=pltpu.CompilerParams(vmem_limit_bytes=6 * 1024 * 1024),
         cost_estimate=pl.CostEstimate(flops=0, bytes_accessed=12 * 1024 * 1024, transcendentals=0),
         name="turn",
     )(flags, kappa, in_hbm(probes))
@@ -177,28 +177,33 @@
         in_specs=[smem_spec()] + [vmem_spec()] * 4 + [pl.BlockSpec(memory_space=pl.ANY)],
         out_specs=[vmem_spec()] * 2,
         out_shape=[f32(rows, K)] * 2,
-        compiler_params=pltpu.CompilerParams(vmem_limit_bytes=8 * 1024 * 1024),
+        compiler_params=pltpu.CompilerParams(vmem_limit_bytes=2 * 1024 * 1024),
         name="corner",
     )(flags, *in_vmem(own_a, own_b), lat_a, lat_b, after)
 
 
-def put_halos(buf, flags, lat_a, lat_b, lon_a, lon_b):
+def keep(ok, x):
+    return x if ok is None else jnp.where(ok, x, 0.0)
+
+
+def put_lat_halos(buf, flags, lat_a, lat_b):
+    odd = flags[0]
+    lat_ok = (None, flags[1] == 1)
+    lat_row = (jnp.where(odd == 1, 0, R + H), jnp.where(odd == 1, R + H, 0))
+    for n, lat in ((0, lat_a), (1, lat_b)):
+        for r in range(H):
+            start = pl.multiple_of(OFF + (lat_row[n] + r) * CB + 8, 8)
+            buf[pl.ds(start, C), :] = keep(lat_ok[n], lat[r * C:(r + 1) * C, :])
+
+
+def put_lon_halos(buf, flags, lon_a, lon_b):
     odd = flags[0]
     lon_odd = flags[2]
     lat_ok = (None, flags[1] == 1)
     lon_ok = (None, flags[3] == 1)
     lat_row = (jnp.where(odd == 1, 0, R + H), jnp.where(odd == 1, R + H, 0))
     lon_col = (jnp.where(lon_odd == 1, 0, C + H), jnp.where(lon_odd == 1, C + H, 0))
-
-    def keep(ok, x):
-        return x if ok is None else jnp.where(ok, x, 0.0)
-
-    own_rows = lon_a.shape[0] - 2 * H * H
-    own_rows = R * H if own_rows == R * H else OWN_ROWS
-    for n, lat in ((0, lat_a), (1, lat_b)):
-        for r in range(H):
-            start = pl.multiple_of(OFF + (lat_row[n] + r) * CB + 8, 8)
-            buf[pl.ds(start, C), :] = keep(lat_ok[n], lat[r * C:(r + 1) * C, :])
+    own_rows = R * H if lon_a.shape[0] == R * H + 2 * H * H else OWN_ROWS
     for m, lon in ((0, lon_a), (1, lon_b)):
         for r in range(R):
             start = at(r + H, 4) + lon_col[m]
@@ -304,28 +309,57 @@
         in_specs=[vmem_spec()] * 3,
         out_specs=[vmem_spec()] * SWEEPS,
         out_shape=[held(NROW + 16, K)] * SWEEPS,
-        compiler_params=pltpu.CompilerParams(vmem_limit_bytes=2 * 1024 * 1024),
+        compiler_params=pltpu.CompilerParams(vmem_limit_bytes=1024 * 1024),
         cost_estimate=pl.CostEstimate(flops=0, bytes_accessed=16 * 1024 * 1024, transcendentals=0),
         name="inner",
     )(*in_vmem(ext, kap, act))
 
 
-def outer(levels, kap, act):
+def sweep_ends(levels, kap, act):
     for s in range(SWEEPS):
         t = s + 1
-        tiles = INNER if t == SWEEPS else tuple(range(CB // 8))
-        sides = tuple(c for c in EDGE if c in tiles)
 
         def ends(i, _):
-            relax(levels[s], levels[t], kap, act, s, jnp.where(i < 2, t + 2 * i, R + H - t + 2 * i - 4), tiles)
+            relax(levels[s], levels[t], kap, act, s, jnp.where(i < 2, t + 2 * i, R + H - t + 2 * i - 4), INNER)
             return 0
 
-        def middle(i, _):
-            relax(levels[s], levels[t], kap, act, s, t + H + 2 * i, sides)
+        lax.fori_loop(0, 4, ends, 0)
+
+
+def sweep_sides(levels, kap, act):
+    for s in range(SWEEPS):
+        t = s + 1
+        sides = EDGE[1:3] if t == SWEEPS else EDGE
+
+        def body(i, _):
+            relax(levels[s], levels[t], kap, act, s, t + 2 * i, sides)
             return 0
 
-        lax.fori_loop(0, 4, ends, 0)
-        lax.fori_loop(0, (R - 2 * t) // 2, middle, 0, unroll=2)
+        lax.fori_loop(0, (RE - 2 * t) // 2, body, 0, unroll=2)
+
+
+def ends_kernel(flags, *refs):
+    (ext_in, l1_in, l2_in, l3_in, l4_in, kap_in, act_in, lat_a, lat_b, after,
+     tail_a, tail_b, ext, l1, l2, l3, l4, kap, act) = refs
+    tail_a[...] = lat_a[H * C:, :]
+    tail_b[...] = lat_b[H * C:, :]
+    put_lat_kappa(kap, act, flags, tail_a, tail_b)
+    put_lat_halos(ext, flags, lat_a, lat_b)
+    sweep_ends((ext, l1, l2, l3, l4), kap, act)
+
+
+def ends(flags, ext, levels, kap, act, lat, after):
+    tail_a, tail_b, ext, *levels, kap, act = pl.pallas_call(
+        ends_kernel,
+        in_specs=[smem_spec()] + [vmem_spec()] * 9 + [pl.BlockSpec(memory_space=pl.ANY)],
+        out_specs=[vmem_spec()] * 9,
+        out_shape=[f32(16, K), f32(16, K)] + [held(NROW + 16, K)] * 6 + [held(SWEEPS, RE, 8, K)],
+        input_output_aliases={1 + i: 2 + i for i in range(7)},
+        compiler_params=pltpu.CompilerParams(vmem_limit_bytes=2 * 1024 * 1024),
+        cost_estimate=pl.CostEstimate(flops=0, bytes_accessed=8 * 1024 * 1024, transcendentals=0),
+        name="ends",
+    )(flags, *in_vmem(ext, *levels, kap, act), *lat, after)
+    return tail_a, tail_b, ext, levels, kap, act
 
 
 def coeffs_kernel(flags, counts, kappa_ref, after, *rest):
@@ -342,7 +376,7 @@
         in_specs=[smem_spec()] * 2 + [vmem_spec(), pl.BlockSpec(memory_space=pl.ANY)] + [vmem_spec()] * len(halos),
         out_specs=[vmem_spec()] * 2,
         out_shape=[held(NROW + 16, K), held(SWEEPS, RE, 8, K)],
-        compiler_params=pltpu.CompilerParams(vmem_limit_bytes=8 * 1024 * 1024),
+        compiler_params=pltpu.CompilerParams(vmem_limit_bytes=1024 * 1024),
         cost_estimate=pl.CostEstimate(flops=0, bytes_accessed=4 * 1024 * 1024, transcendentals=0),
         name="coeffs",
     )(flags, counts, kappa, after, *halos)
@@ -370,20 +404,17 @@
         out_specs=[vmem_spec()] * 2,
         out_shape=[jax.ShapeDtypeStruct((1, SLOTS), jnp.int32)] * 2,
         cost_estimate=pl.CostEstimate(flops=0, bytes_accessed=4 * 1024 * 1024, transcendentals=0),
-        compiler_params=pltpu.CompilerParams(vmem_limit_bytes=4 * 1024 * 1024),
+        compiler_params=pltpu.CompilerParams(vmem_limit_bytes=2 * 1024 * 1024),
         name="places",
     )(count, cell, owner, after)
 
 
 def smooth_kernel(flags, cell_ref, place_ref, *refs):
-    (ext_in, l1_in, l2_in, l3_in, l4_in, kap_in, act_in, lat_a, lat_b, lon_a, lon_b,
-     out_ref, tail_a, tail_b, ext, l1, l2, l3, l4, kap, act, rows_ref) = refs
-    tail_a[...] = lat_a[H * C:, :]
-    tail_b[...] = lat_b[H * C:, :]
-    put_lat_kappa(kap, act, flags, tail_a, tail_b)
+    (ext_in, l1_in, l2_in, l3_in, l4_in, kap_in, act, lon_a, lon_b,
+     out_ref, ext, l1, l2, l3, l4, kap, rows_ref) = refs
     put_lon_kappa(kap, flags, lon_a, lon_b)
-    put_halos(ext, flags, lat_a, lat_b, lon_a, lon_b)
-    outer((ext, l1, l2, l3, l4), kap, act)
+    put_lon_halos(ext, flags, lon_a, lon_b)
+    sweep_sides((ext, l1, l2, l3, l4), kap, act)
     rows_ref[...] = jnp.zeros_like(rows_ref)
 
     def copy(i, _):
@@ -396,17 +427,17 @@
     out_ref[...] = rows_ref[:PLACES]
 
 
-def smooth(flags, cell, place, ext, levels, kap, act, halos):
+def smooth(flags, cell, place, ext, levels, kap, act, lon):
     return pl.pallas_call(
         smooth_kernel,
-        in_specs=[smem_spec()] * 3 + [vmem_spec()] * 11,
-        out_specs=[vmem_spec()] * 10,
-        out_shape=[f32(PLACES, K), f32(16, K), f32(16, K)] + [held(NROW + 16, K)] * 6 + [held(SWEEPS, RE, 8, K)],
-        input_output_aliases={3 + i: 3 + i for i in range(7)},
+        in_specs=[smem_spec()] * 3 + [vmem_spec()] * 9,
+        out_specs=[vmem_spec()] * 7,
+        out_shape=[f32(PLACES, K)] + [held(NROW + 16, K)] * 6,
+        input_output_aliases={3 + i: 1 + i for i in range(6)},
         scratch_shapes=[pltpu.VMEM((PLACES + 8, K), jnp.float32)],
-        compiler_params=pltpu.CompilerParams(vmem_limit_bytes=8 * 1024 * 1024),
+        compiler_params=pltpu.CompilerParams(vmem_limit_bytes=2 * 1024 * 1024),
         name="smooth",
-    )(flags, cell, place, *in_vmem(ext, *levels, kap, act), *halos)[:3]
+    )(flags, cell, place, *in_vmem(ext, *levels, kap, act), *lon)[0]
 
 
 def weigh_kernel(b_ref, r_hbm, out_ref, r_ref, sems):
@@ -441,7 +472,7 @@
             pltpu.VMEM((WEIGH_PARTS, PLACES, PLACES // WEIGH_PARTS), jnp.float32),
             pltpu.SemaphoreType.DMA((WEIGH_PARTS,)),
         ],
-        compiler_params=pltpu.CompilerParams(vmem_limit_bytes=12 * 1024 * 1024),
+        compiler_params=pltpu.CompilerParams(vmem_limit_bytes=6 * 1024 * 1024),
         name="weigh",
     )(buffer, in_hbm(r))
 
@@ -482,50 +513,102 @@
         in_specs=[smem_spec()] * 4 + [vmem_spec()],
         out_specs=[vmem_spec()] * 5,
         out_shape=[held(NROW + 16, K), f32(H * C, K), f32(H * C, K), held(R * H, K), held(R * H, K)],
-        compiler_params=pltpu.CompilerParams(vmem_limit_bytes=10 * 1024 * 1024),
+        compiler_params=pltpu.CompilerParams(vmem_limit_bytes=2 * 1024 * 1024),
         name="spread",
     )(flags, cell, place, count, returned)
 
 
-def finish_kernel(flags, *refs):
-    (ext_in, l1_in, l2_in, l3_in, l4_in, kap, act, lat_a, lat_b, lon_a, lon_b, p_hbm,
-     out_hbm, gram_ref, ext, l1, l2, l3, l4, chunk, in_sems, out_sems) = refs
-
-    def part(ref, n):
-        half, block = n // 4, n % 4
-        return ref.at[:, pl.ds(block * 8, 8), pl.ds(half * LANES, LANES)]
+def gram_terms(sk):
+    high = sk.astype(jnp.bfloat16)
+    low = (sk - high.astype(jnp.float32)).astype(jnp.bfloat16)
+    dot = lambda a, b: lax.dot_general(a, b, (((1,), (1,)), ((), ())), preferred_element_type=jnp.float32)
+    return dot(high, high), dot(high, low)
+
+
+def part(ref, n):
+    half, block = n // 4, n % 4
+    return ref.at[:, pl.ds(block * 8, 8), pl.ds(half * LANES, LANES)]
+
+
+def bulk_kernel(flags, *refs):
+    (ext_in, l1_in, l2_in, l3_in, l4_in, kap, act, lat_a, lat_b, after, p_hbm,
+     ext, l1, l2, l3, l4, chunk, hh_ref, hl_ref, sems) = refs
 
     def copy_in(n):
-        return pltpu.make_async_copy(part(p_hbm, n), chunk.at[n], in_sems.at[n])
-
-    def copy_out(n):
-        return pltpu.make_async_copy(chunk.at[n], part(out_hbm, n), out_sems.at[n])
+        return pltpu.make_async_copy(part(p_hbm, n), chunk.at[n], sems.at[n])
 
     for n in range(8):
         copy_in(n).start()
-    put_halos(ext, flags, lat_a, lat_b, lon_a, lon_b)
-    outer((ext, l1, l2, l3, l4), kap, act)
+    put_lat_halos(ext, flags, lat_a, lat_b)
+    sweep_ends((ext, l1, l2, l3, l4), kap, act)
     flat = chunk.reshape(8 * K * 8, LANES)
-    contract = (((1,), (1,)), ((), ()))
+    lane = lax.broadcasted_iota(jnp.int32, (K, LANES), 1)
     hh = jnp.zeros((K, K), jnp.float32)
     hl = jnp.zeros((K, K), jnp.float32)
     for n in range(8):
         half, block = n // 4, n % 4
+        ready = lane >= 8 if half == 0 else lane < LANES - 8
         copy_in(n).wait()
         for i in range(0, 8, 2):
             parts = []
             for j in range(2):
                 where = pl.ds(n * K * 8 + i + j, K, stride=8)
                 start = at(block * 8 + i + j + H, 8) + half * LANES
-                sk = flat[where, :] + l4[pl.ds(start, LANES), :].T
+                raw = flat[where, :]
+                sk = raw + jnp.where(ready, l4[pl.ds(start, LANES), :].T, 0.0)
                 flat[where, :] = sk
-                parts.append(sk)
-            sk = jnp.concatenate(parts, axis=1)
-            high = sk.astype(jnp.bfloat16)
-            low = (sk - high.astype(jnp.float32)).astype(jnp.bfloat16)
-            hh = hh + lax.dot_general(high, high, contract, preferred_element_type=jnp.float32)
-            hl = hl + lax.dot_general(high, low, contract, preferred_element_type=jnp.float32)
-        copy_out(n).start()
+                parts.append(jnp.where(ready, sk, 0.0))
+            one, two = gram_terms(jnp.concatenate(parts, axis=1))
+            hh = hh + one
+            hl = hl + two
+    hh_ref[...] = hh
+    hl_ref[...] = hl
+
+
+def bulk(flags, ext, levels, kap, act, lat, after, probes):
+    ext, *levels, chunk, hh, hl = pl.pallas_call(
+        bulk_kernel,
+        in_specs=[smem_spec()] + [vmem_spec()] * 9 + [pl.BlockSpec(memory_space=pl.ANY), hbm_spec()],
+        out_specs=[vmem_spec()] * 8,
+        out_shape=[held(NROW + 16, K)] * 5 + [held(8, K, 8, LANES), held(K, K), held(K, K)],
+        input_output_aliases={1 + i: i for i in range(5)},
+        scratch_shapes=[pltpu.SemaphoreType.DMA((8,))],
+        compiler_params=pltpu.CompilerParams(vmem_limit_bytes=2 * 1024 * 1024),
+        cost_estimate=pl.CostEstimate(flops=0, bytes_accessed=16 * 1024 * 1024, transcendentals=0),
+        name="bulk",
+    )(flags, *in_vmem(ext, *levels, kap, act), *lat, after, in_hbm(probes))
+    return ext, levels, chunk, hh, hl
+
+
+def finish_kernel(flags, *refs):
+    (ext_in, l1_in, l2_in, l3_in, l4_in, kap, act, chunk_in, hh_ref, hl_ref, lon_a, lon_b,
+     gram_ref, ext, l1, l2, l3, l4, chunk) = refs
+    put_lon_halos(ext, flags, lon_a, lon_b)
+    sweep_sides((ext, l1, l2, l3, l4), kap, act)
+    flat = chunk.reshape(8 * K * 8, LANES)
+    lane = lax.broadcasted_iota(jnp.int32, (K, LANES), 1)
+    hh = hh_ref[...]
+    hl = hl_ref[...]
+    for block in range(4):
+        tiles = []
+        for i in range(8):
+            r = block * 8 + i + H
+            tiles += [l4[pl.ds(at(r, C), 8), :], l4[pl.ds(at(r, 8), 8), :]]
+        turned = jnp.concatenate(tiles, axis=0).T
+        for i in range(0, 8, 2):
+            parts = []
+            for j in range(2):
+                moved = pltpu.roll(turned, (LANES - 16 * (i + j) - 8) % LANES, 1)
+                first = pl.ds(block * K * 8 + i + j, K, stride=8)
+                last = pl.ds((4 + block) * K * 8 + i + j, K, stride=8)
+                a = flat[first, :] + jnp.where(lane < 8, moved, 0.0)
+                b = flat[last, :] + jnp.where(lane >= LANES - 8, moved, 0.0)
+                flat[first, :] = a
+                flat[last, :] = b
+                parts.append(jnp.where(lane < 8, a, jnp.where(lane >= LANES - 8, b, 0.0)))
+            one, two = gram_terms(jnp.concatenate(parts, axis=1))
+            hh = hh + one
+            hl = hl + two
     gram = hh + (hl + hl.T)
     top = gram[:HALF]
     turned = pltpu.roll(gram[HALF:], HALF, 1)
@@ -533,25 +616,40 @@
     lane = lax.broadcasted_iota(jnp.int32, (HALF, K), 1)
     gram_ref[:HALF, :] = jnp.where((lane < HALF) & (row > lane), turned, top)
     gram_ref[HALF:, :] = jnp.broadcast_to(jnp.sum(jnp.where(row == lane, turned, 0.0), axis=0, keepdims=True), (8, K))
-    for n in range(8):
-        copy_out(n).wait()
-
-
-def finish(flags, ext, levels, kap, act, halos, probes):
-    return pl.pallas_call(
+
+
+def finish(flags, ext, levels, kap, act, chunk, hh, hl, lon):
+    outs = pl.pallas_call(
         finish_kernel,
-        in_specs=[smem_spec()] + [vmem_spec()] * 11 + [hbm_spec()],
-        out_specs=[hbm_spec()] + [vmem_spec()] * 6,
-        out_shape=[f32(K, R, C), f32(HALF + 8, K)] + [held(NROW + 16, K)] * 5,
-        input_output_aliases={1 + i: 2 + i for i in range(5)},
-        scratch_shapes=[
-            pltpu.VMEM((8, K, 8, LANES), jnp.float32),
-            pltpu.SemaphoreType.DMA((8,)),
-            pltpu.SemaphoreType.DMA((8,)),
-        ],
-        compiler_params=pltpu.CompilerParams(vmem_limit_bytes=12 * 1024 * 1024),
+        in_specs=[smem_spec()] + [vmem_spec()] * 12,
+        out_specs=[vmem_spec()] * 7,
+        out_shape=[f32(HALF + 8, K)] + [held(NROW + 16, K)] * 5 + [held(8, K, 8, LANES)],
+        input_output_aliases={**{1 + i: 1 + i for i in range(5)}, 8: 6},
+        compiler_params=pltpu.CompilerParams(vmem_limit_bytes=3 * 1024 * 1024),
         name="finish",
-    )(flags, *in_vmem(ext, *levels, kap, act), *halos, in_hbm(probes))[:2]
+    )(flags, *in_vmem(ext, *levels, kap, act, chunk, hh, hl), *lon)
+    return outs[0], outs[6]
+
+
+def store_kernel(chunk, after, out_hbm, sems):
+    copies = [pltpu.make_async_copy(chunk.at[n], part(out_hbm, n), sems.at[n]) for n in range(8)]
+    for copy in copies:
+        copy.start()
+    for copy in copies:
+        copy.wait()
+
+
+def store(chunk, after):
+    return pl.pallas_call(
+        store_kernel,
+        in_specs=[vmem_spec(), pl.BlockSpec(memory_space=pl.ANY)],
+        out_specs=hbm_spec(),
+        out_shape=f32(K, R, C),
+        scratch_shapes=[pltpu.SemaphoreType.DMA((8,))],
+        compiler_params=pltpu.CompilerParams(vmem_limit_bytes=1024 * 1024),
+        cost_estimate=pl.CostEstimate(flops=0, bytes_accessed=8 * 1024 * 1024, transcendentals=0),
+        name="store",
+    )(*in_vmem(chunk), after)
 
 
 def pairs(size, first):
@@ -630,9 +728,11 @@
         return (x + g1) + (g2 + g3)
 
     x, g1 = stage(x, "lat", (1,))
-    x = total(*stage(x + g1, "lat", (2, 4, 6)))
+    x = x + g1
+    early = x
+    x = total(*stage(x, "lat", (2, 4, 6)))
     x = total(*stage(x, "lon", (1, 2, 3)))
-    return stage(x, "lon", (4, 8, 12))
+    return early, stage(x, "lon", (4, 8, 12))
 
 
 def shards(probes, kappa, sweep_counts, obs_cell, obs_owner, obs_count, r_inv):
@@ -649,8 +749,9 @@
     count = obs_count.reshape(1)
     lon_pay = corner(flags, own_a, own_b, lat_a, lat_b, levels[-1])
     cell, place = places(count, obs_cell.reshape(1, SLOTS), obs_owner.reshape(1, SLOTS), lon_pay[0])
+    tail_a, tail_b, ext, levels, kap, act = ends(flags, ext, levels, kap, act, (lat_a, lat_b), lon_pay[0])
     lon_a, lon_b = swap(*lon_pay, "lon")
-    outgoing, tail_a, tail_b = smooth(flags, cell, place, ext, levels, kap, act, (lat_a, lat_b, lon_a, lon_b))
+    outgoing = smooth(flags, cell, place, ext, levels, kap, act, (lon_a, lon_b))
     buffer = lax.all_to_all(outgoing, "lon", split_axis=0, concat_axis=0, tiled=True)
     mixed = weigh(buffer, r_inv[0, 0])
     returned = lax.all_to_all(mixed, "lon", split_axis=0, concat_axis=0, tiled=True)
@@ -658,10 +759,13 @@
     kap, act = coeffs(flags, sweep_counts, kappa, pay_a, tail_a, tail_b, lon_a, lon_b)
     levels = inner(field, kap, act)
     lat_a, lat_b = swap(pay_a, pay_b, "lat")
-    back = (lat_a, lat_b) + swap(*corner(flags, own_a, own_b, lat_a, lat_b, levels[-1]), "lon")
-    sketch, gram = finish(flags, field, levels, kap, act, back, probes)
+    lon_pay = corner(flags, own_a, own_b, lat_a, lat_b, levels[-1])
+    field, levels, chunk, hh, hl = bulk(flags, field, levels, kap, act, (lat_a, lat_b), lon_pay[0], probes)
+    gram, chunk = finish(flags, field, levels, kap, act, chunk, hh, hl, swap(*lon_pay, "lon"))
+    early, parts = gather_sums(gram)
+    sketch = store(chunk, early)
     cells_all = R * C * n_lat * n_lon
-    r_factor = factor(1.0 / cells_all, gather_sums(gram))
+    r_factor = factor(1.0 / cells_all, parts)
     return (sketch, r_factor)
 
 

time: 119 us -> 112 us (0.941)
  waiting for transfers between devices: 19.9 us -> 11.5 us
  Pallas kernels: 44.1 us -> 46.2 us
    pallas_call x1 -> x4, Pallas kernels: 6.76 us -> 12.6 us  [the longest x1 4.67 us: bulk(): pl.pallas_call(bulk_kernel, in_specs=[smem_spec()] + [vmem_spec()] * 9 +...]
    ppermute x4, waiting for transfers between devices: 6.75 us -> 3.02 us  [swap(): lax.ppermute(b, axis, pairs(size, 1))]
    ppermute x4, waiting for transfers between devices: 3.86 us -> 1.26 us  [swap(): lax.ppermute(a, axis, pairs(size, 0))]
    pallas_call x1, Pallas kernels: 4.61 us -> 2.49 us  [smooth(): pl.pallas_call(smooth_kernel, in_specs=[smem_spec()] * 3 + [vmem_spec()]...]
    ppermute x10, waiting for transfers between devices: 9.27 us -> 7.17 us  [stage(): lax.ppermute(x, axis, [(i, i ^ d) for i in range(size)])]
  transfers between devices with their start and end apart: 18 -> 18, of which waited for: 13 -> 10; matrix products, arithmetic and copies ran while one was open for 0% -> 0% of each run, Pallas kernels for 15% -> 24%
where the time goes in v6:
time: 112 us; the launch traced here: 111 us
  Pallas kernels  46.2 us (41%)
  blocking collectives  26.3 us (23%)
  starting transfers between devices  25 us (22%)
  waiting for transfers between devices  11.5 us (10%)
  between operations  1.53 us (1%)
    all_to_all x1, blocking collectives, shards(): lax.all_to_all(outgoing, 'lon', split_axis=0, concat_axis=0, tiled=True)  13.6 us
    all_to_all x1, blocking collectives, shards(): lax.all_to_all(mixed, 'lon', split_axis=0, concat_axis=0, tiled=True)  12.6 us
    ppermute x10, starting transfers between devices, stage(): lax.ppermute(x, axis, [(i, i ^ d) for i in range(size)])  12.5 us
    ppermute x4, starting transfers between devices, swap(): lax.ppermute(b, axis, pairs(size, 1))  11.2 us
    pallas_call x2, Pallas kernels, inner(): pl.pallas_call(inner_kernel, in_specs=[vmem_spec()] * 3, out_specs=[vmem_...  9.85 us
    ppermute x10, waiting for transfers between devices, stage(): lax.ppermute(x, axis, [(i, i ^ d) for i in range(size)])  7.17 us
    pallas_call x1, Pallas kernels, factor(): pl.pallas_call(functools.partial(factor_kernel, scale), in_specs=[vmem_sp...  5.68 us
    pallas_call x1, Pallas kernels, bulk(): pl.pallas_call(bulk_kernel, in_specs=[smem_spec()] + [vmem_spec()] * 9 +...  4.67 us
  transfers between devices with their start and end apart: 18, of which 10 were waited for; matrix products, arithmetic and copies ran while one was open for 0% of the time, Pallas kernels for 24%

profile of v6, /device:TPU:0, one launch (start us, length us, event | category | flops | bytes accessed | tf_op | source)
XLA Modules:
  0.0 111.3 jit_solution(8654812704909658298)
XLA Ops:
  0.6 1.8 %edge_pack.1 = (f32[1040,128]{1,0:T(8,128)S(1)}, f32[1040,128]{1,0:T(8,128)S(1)}) custom-call(s32[32]{0:T(128)} %counts.3, f32[32,256]{1,0:T(8,128)} %kappa_ref.5, f32[128,32,256]{2,1,0:T(8,128)} %refs_10_.1), custom_call_target="tpu_custom_call" | custom-call | tf_op jit(solution)/shard_map/edge_pack/pallas_call | solution.py:102
  2.5 3.2 %collective-permute-start.1 = (f32[1040,128]{1,0:T(8,128)S(1)}, f32[1040,128]{1,0:T(8,128)S(1)}, u32[]{:S(2)}, u32[]{:S(2)}) collective-permute-start(f32[1040,128]{1,0:T(8,128)S(1)} %get-tuple-element.53), channel_id=1, source_target_pairs={{0,112},{16,32},{32,16},{48,64},{64,48},{80,96},{96,80},{112,0},{1... | collective-permute-start | bytes 1597448 | tf_op jit(solution)/shard_map/ppermute | solution.py:661
  6.5 3.3 %turn.1 = (f32[10896,128]{1,0:T(8,128)S(1)}, f32[160,128]{1,0:T(8,128)S(1)}, f32[160,128]{1,0:T(8,128)S(1)}) custom-call(s32[4]{0:T(128)S(1)} %pad_add_fusion.flags, f32[32,256]{1,0:T(8,128)S(1)} %copy-done, f32[128,32,256]{2,1,0:T(8,128)} %refs_10_.1), custom_call_target="tpu_custom_call" | custom-call | bytes 12582912 | tf_op jit(solution)/shard_map/turn/pallas_call | solution.py:143
  9.8 1.8 %coeffs.2 = (f32[10896,128]{1,0:T(8,128)S(1)}, f32[4,40,8,128]{3,2,1,0:T(8,128)S(1)}) custom-call(s32[4]{0:T(128)S(1)} %pad_add_fusion.flags, s32[32]{0:T(128)S(1)} %copy-done.2, f32[32,256]{1,0:T(8,128)S(1)} %copy-done, f32[160,128]{1,0:T(8,128)S(1)} %get-tuple-element.50.after.own_a), custom_call_target="tpu_custom_call" | custom-call | bytes 4194304 | tf_op jit(solution)/shard_map/coeffs/pallas_call | solution.py:374
  11.7 5.1 %inner.2 = (f32[10896,128]{1,0:T(8,128)S(1)}, f32[10896,128]{1,0:T(8,128)S(1)}, f32[10896,128]{1,0:T(8,128)S(1)}, f32[10896,128]{1,0:T(8,128)S(1)}) custom-call(f32[10896,128]{1,0:T(8,128)S(1)} %get-tuple-element.54.ext.refs_0_, f32[10896,128]{1,0:T(8,128)S(1)} %get-tuple-element.55.kap.refs_5_, f32[4,40,8,128]{3,2,1,0:T(8,128)S(1)} %get-tuple-element.56.act.refs_6_), custom_call_target="tpu_custom_call" | custom-call | bytes 16777216 | tf_op jit(solution)/shard_map/inner/pallas_call | solution.py:307
  17.4 6.3 %collective-permute-start.3 = (f32[200,128]{1,0:T(8,128)S(1)}, f32[200,128]{1,0:T(8,128)S(1)}, u32[]{:S(2)}, u32[]{:S(2)}) collective-permute-start(f32[200,128]{1,0:T(8,128)S(1)} %get-tuple-element.71), channel_id=1, source_target_pairs={{0,15},{1,2},{2,1},{3,4},{4,3},{5,6},{6,5},{7,8},{8,7},{9,10},{10,... | collective-permute-start | bytes 307208 | tf_op jit(solution)/shard_map/ppermute | solution.py:661
  24.6 2.4 %ends.1 = (f32[16,128]{1,0:T(8,128)S(1)}, f32[16,128]{1,0:T(8,128)S(1)}, f32[10896,128]{1,0:T(8,128)S(1)}, f32[10896,128]{1,0:T(8,128)S(1)}, f32[10896,128]{1,0:...) custom-call(s32[4]{0:T(128)S(1)} %pad_add_fusion.flags, ...), custom_call_target="tpu_custom_call", output_to_operand_aliasing={{2}: (1, {}), {3}: (2, {}), {4}: (3, {}), {5}: (4, {}), {6}... | custom-call | bytes 8388608 | tf_op jit(solution)/shard_map/ends/pallas_call | solution.py:352
  28.3 2.5 %smooth.1 = (f32[768,128]{1,0:T(8,128)S(1)}, f32[10896,128]{1,0:T(8,128)S(1)}, f32[10896,128]{1,0:T(8,128)S(1)}, f32[10896,128]{1,0:T(8,128)S(1)}, f32[10896,128...) custom-call(s32[4]{0:T(128)S(1)} %pad_add_fusion.flags, ...), custom_call_target="tpu_custom_call", output_to_operand_aliasing={{1}: (3, {}), {2}: (4, {}), {3}: (5, {}), {4}: (6, {}), {5}... | custom-call | tf_op jit(solution)/shard_map/smooth/pallas_call | solution.py:431
  30.8 13.6 %all_to_all.22 = f32[16,48,128]{2,1,0:T(8,128)S(1)} all-to-all(f32[16,48,128]{2,1,0:T(8,128)S(1)} %bitcast.16), channel_id=1, replica_groups=mesh['lat'=8,'lon'=16] {'lon'}, dimensions={0} | all-to-all | bytes 786432 | tf_op jit(solution)/shard_map/all_to_all | solution.py:755
  44.5 2.7 %weigh.1 = f32[768,128]{1,0:T(8,128)S(1)} custom-call(f32[768,128]{1,0:T(8,128)S(1)} %bitcast.14, f32[768,768]{1,0:T(8,128)} %bitcast.18), custom_call_target="tpu_custom_call" | custom-call | tf_op jit(solution)/shard_map/weigh/pallas_call | solution.py:466
  47.2 12.6 %all_to_all.23 = f32[16,48,128]{2,1,0:T(8,128)S(1)} all-to-all(f32[16,48,128]{2,1,0:T(8,128)S(1)} %bitcast.15), channel_id=1, replica_groups=mesh['lat'=8,'lon'=16] {'lon'}, dimensions={0} | all-to-all | bytes 786432 | tf_op jit(solution)/shard_map/all_to_all | solution.py:757
  59.8 2.1 %spread.1 = (f32[10896,128]{1,0:T(8,128)S(1)}, f32[1024,128]{1,0:T(8,128)S(1)}, f32[1024,128]{1,0:T(8,128)S(1)}, f32[128,128]{1,0:T(8,128)S(1)}, f32[128,128]{1,0:T(8,128)S(1)}) custom-call(s32[4]{0:T(128)S(1)} %pad_add_fusion.flags, s32[1,384]{1,0:T(1,128)S(1)} %get-tuple-element.59.cell_ref, s32[1,384]{1,0:T(1,128)S(1)} %get-tuple-element.60.place_ref, ...), custom_call_target="tpu_custom_call" | custom-call | tf_op jit(solution)/shard_map/spread/pallas_call | solution.py:511
  63.1 2.4 %coeffs.3 = (f32[10896,128]{1,0:T(8,128)S(1)}, f32[4,40,8,128]{3,2,1,0:T(8,128)S(1)}) custom-call(s32[4]{0:T(128)S(1)} %pad_add_fusion.flags, s32[32]{0:T(128)S(1)} %copy-done.2, f32[32,256]{1,0:T(8,128)S(1)} %copy-done.1, f32[1024,128]{1,0:T(8,128)S(1)} %get-tuple-element.74.after, f32[16,128]{1,0:T(8,128)S(1)} %get-tuple-element.75.rest_0_, ...), custom_call_target="tpu_custom_call" | custom-call | bytes 4194304 | tf_op jit(solution)/shard_map/coeffs/pallas_call | solution.py:374
  65.6 4.8 %inner.3 = (f32[10896,128]{1,0:T(8,128)S(1)}, f32[10896,128]{1,0:T(8,128)S(1)}, f32[10896,128]{1,0:T(8,128)S(1)}, f32[10896,128]{1,0:T(8,128)S(1)}) custom-call(f32[10896,128]{1,0:T(8,128)S(1)} %get-tuple-element.73.ext.refs_0_, f32[10896,128]{1,0:T(8,128)S(1)} %get-tuple-element.77.kap.refs_5_, f32[4,40,8,128]{3,2,1,0:T(8,128)S(1)} %get-tuple-element.78.act.refs_6_), custom_call_target="tpu_custom_call" | custom-call | bytes 16777216 | tf_op jit(solution)/shard_map/inner/pallas_call | solution.py:307
  70.3 1.5 %collective-permute-done.5.lat_b.refs_8_ = f32[1024,128]{1,0:T(8,128)S(1)} collective-permute-done((f32[1024,128]{1,0:T(8,128)S(1)}, f32[1024,128]{1,0:T(8,128)S(1)}, u32[]{:S(2)}, u32[]{:S(2)}) %collective-permute-start.5) | collective-permute-done | bytes 524320 | tf_op jit(solution)/shard_map/ppermute | solution.py:661
  72.4 1.6 %collective-permute-start.7 = (f32[160,128]{1,0:T(8,128)S(1)}, f32[160,128]{1,0:T(8,128)S(1)}, u32[]{:S(2)}, u32[]{:S(2)}) collective-permute-start(f32[160,128]{1,0:T(8,128)S(1)} %get-tuple-element.95), channel_id=1, source_target_pairs={{0,15},{1,2},{2,1},{3,4},{4,3},{5,6},{6,5},{7,8},{8,7},{9,10},{10,... | collective-permute-start | bytes 245768 | tf_op jit(solution)/shard_map/ppermute | solution.py:661
  74.1 4.7 %bulk.1 = (f32[10896,128]{1,0:T(8,128)S(1)}, f32[10896,128]{1,0:T(8,128)S(1)}, f32[10896,128]{1,0:T(8,128)S(1)}, f32[10896,128]{1,0:T(8,128)S(1)}, f32[10896,128...) custom-call(s32[4]{0:T(128)S(1)} %pad_add_fusion.flags, ...), custom_call_target="tpu_custom_call", output_to_operand_aliasing={{0}: (1, {}), {1}: (2, {}), {2}: (3, {}), {3}: (4, {}), {4}... | custom-call | bytes 16777216 | tf_op jit(solution)/shard_map/bulk/pallas_call | solution.py:569
  78.8 1.5 %collective-permute-done.7.refs_11_ = f32[160,128]{1,0:T(8,128)S(1)} collective-permute-done((f32[160,128]{1,0:T(8,128)S(1)}, f32[160,128]{1,0:T(8,128)S(1)}, u32[]{:S(2)}, u32[]{:S(2)}) %collective-permute-start.7) | collective-permute-done | bytes 81952 | tf_op jit(solution)/shard_map/ppermute | solution.py:661
  80.3 3.5 %finish.1 = (f32[72,128]{1,0:T(8,128)S(1)}, f32[10896,128]{1,0:T(8,128)S(1)}, f32[10896,128]{1,0:T(8,128)S(1)}, f32[10896,128]{1,0:T(8,128)S(1)}, f32[10896,128]...) custom-call(s32[4]{0:T(128)S(1)} %pad_add_fusion.flags, ...), custom_call_target="tpu_custom_call", output_to_operand_aliasing={{1}: (1, {}), {2}: (2, {}), {3}: (3, {}), {4}: (4, {}), {5}... | custom-call | tf_op jit(solution)/shard_map/finish/pallas_call | solution.py:622
  87.2 1.9 %collective-permute-start.9 = (f32[72,128]{1,0:T(8,128)S(1)}, f32[72,128]{1,0:T(8,128)S(1)}, u32[]{:S(2)}, u32[]{:S(2)}) collective-permute-start(f32[72,128]{1,0:T(8,128)S(1)} %add.30.after), channel_id=1, source_target_pairs={{0,32},{16,48},{32,0},{48,16},{64,96},{80,112},{96,64},{112,80},{1... | collective-permute-start | bytes 110600 | tf_op jit(solution)/shard_map/ppermute | solution.py:725
  91.7 2.6 %collective-permute-start.13 = (f32[72,128]{1,0:T(8,128)S(1)}, f32[72,128]{1,0:T(8,128)S(1)}, u32[]{:S(2)}, u32[]{:S(2)}) collective-permute-start(f32[72,128]{1,0:T(8,128)S(1)} %add_add_fusion.1), channel_id=1, source_target_pairs={{0,2},{1,3},{2,0},{3,1},{4,6},{5,7},{6,4},{7,5},{8,10},{9,11},{10,... | collective-permute-start | bytes 110600 | tf_op jit(solution)/shard_map/ppermute | solution.py:725
  98.3 1.8 %collective-permute-start.17 = (f32[72,128]{1,0:T(8,128)S(1)}, f32[72,128]{1,0:T(8,128)S(1)}, u32[]{:S(2)}, u32[]{:S(2)}) collective-permute-start(f32[72,128]{1,0:T(8,128)S(1)} %add_add_fusion.x_ref), channel_id=1, source_target_pairs={{0,12},{1,13},{2,14},{3,15},{4,8},{5,9},{6,10},{7,11},{8,4},{9,5},... | collective-permute-start | bytes 110600 | tf_op jit(solution)/shard_map/ppermute | solution.py:725
  102.4 2.1 %store.1 = f32[128,32,256]{2,1,0:T(8,128)} custom-call(f32[8,128,8,128]{3,2,1,0:T(8,128)S(1)} %get-tuple-element.96.chunk, f32[72,128]{1,0:T(8,128)S(1)} %add.30.after), custom_call_target="tpu_custom_call" | custom-call | bytes 8388608 | tf_op jit(solution)/shard_map/store/pallas_call | solution.py:643
  105.6 5.7 %factor.1 = f32[128,128]{1,0:T(8,128)} custom-call(f32[72,128]{1,0:T(8,128)S(1)} %add_add_fusion.x_ref, f32[72,128]{1,0:T(8,128)S(1)} %collective-permute-done.15.g1_ref, f32[72,128]{1,0:T(8,128)S(1)} %collective-permute-done.16.g2_ref, f32[72,128]{1,0:T(8,128)S(1)} %collective-permute-done.17.g3_ref), custom_call_target="tpu_custom_call" | custom-call | tf_op jit(solution)/shard_map/factor/pallas_call | solution.py:711
  (46 shorter events, 18.2 us)
Async XLA Ops:
  0.6 9.2 %copy-start.2 = (s32[32]{0:T(128)S(1)}, s32[32]{0:T(128)}, u32[]{:S(2)}) copy-start(s32[32]{0:T(128)} %counts.3) | copy-start | bytes 388
  2.4 14.4 %collective-permute-start = (f32[1040,128]{1,0:T(8,128)S(1)}, f32[1040,128]{1,0:T(8,128)S(1)}, u32[]{:S(2)}, u32[]{:S(2)}) collective-permute-start(f32[1040,128]{1,0:T(8,128)S(1)} %get-tuple-element.52), channel_id=1, source_target_pairs={{0,16},{16,0},{32,48},{48,32},{64,80},{80,64},{96,112},{112,96},{1... | collective-permute-start | bytes 1597448 | tf_op jit(solution)/shard_map/ppermute | solution.py:661
  2.5 14.3 %collective-permute-start.1 = (f32[1040,128]{1,0:T(8,128)S(1)}, f32[1040,128]{1,0:T(8,128)S(1)}, u32[]{:S(2)}, u32[]{:S(2)}) collective-permute-start(f32[1040,128]{1,0:T(8,128)S(1)} %get-tuple-element.53), channel_id=1, source_target_pairs={{0,112},{16,32},{32,16},{48,64},{64,48},{80,96},{96,80},{112,0},{1... | collective-permute-start | bytes 1597448 | tf_op jit(solution)/shard_map/ppermute | solution.py:661
  5.8 0.8 copy-start
  16.8 7.6 %copy-start.4 = (s32[384]{0:T(512)S(1)}, s32[384]{0:T(512)}, u32[]{:S(2)}) copy-start(s32[384]{0:T(512)} %param.10) | copy-start | bytes 4612
  16.8 7.6 %copy-start.3 = (s32[384,1]{0,1:T(1,128)S(1)}, s32[384,1]{0,1:T(1,128)}, u32[]{:S(2)}) copy-start(s32[384,1]{0,1:T(1,128)} %param.11) | copy-start | bytes 4612
  17.4 9.7 %collective-permute-start.3 = (f32[200,128]{1,0:T(8,128)S(1)}, f32[200,128]{1,0:T(8,128)S(1)}, u32[]{:S(2)}, u32[]{:S(2)}) collective-permute-start(f32[200,128]{1,0:T(8,128)S(1)} %get-tuple-element.71), channel_id=1, source_target_pairs={{0,15},{1,2},{2,1},{3,4},{4,3},{5,6},{6,5},{7,8},{8,7},{9,10},{10,... | collective-permute-start | bytes 307208 | tf_op jit(solution)/shard_map/ppermute | solution.py:661
  23.7 4.7 %collective-permute-start.2 = (f32[200,128]{1,0:T(8,128)S(1)}, f32[200,128]{1,0:T(8,128)S(1)}, u32[]{:S(2)}, u32[]{:S(2)}) collective-permute-start(f32[200,128]{1,0:T(8,128)S(1)} %get-tuple-element.58.after.refs_9_), channel_id=1, source_target_pairs={{0,1},{1,0},{2,3},{3,2},{4,5},{5,4},{6,7},{7,6},{8,9},{9,8},{10,11... | collective-permute-start | bytes 307208 | tf_op jit(solution)/shard_map/ppermute | solution.py:661
  28.3 34.8 %copy-start.1 = (f32[32,256]{1,0:T(8,128)S(1)}, f32[32,256]{1,0:T(8,128)}, u32[]{:S(2)}) copy-start(f32[32,256]{1,0:T(8,128)} %kappa_ref.5) | copy-start | bytes 98308
  62.0 9.9 %collective-permute-start.5 = (f32[1024,128]{1,0:T(8,128)S(1)}, f32[1024,128]{1,0:T(8,128)S(1)}, u32[]{:S(2)}, u32[]{:S(2)}) collective-permute-start(f32[1024,128]{1,0:T(8,128)S(1)} %get-tuple-element.83), channel_id=1, source_target_pairs={{0,112},{16,32},{32,16},{48,64},{64,48},{80,96},{96,80},{112,0},{1... | collective-permute-start | bytes 1572872 | tf_op jit(solution)/shard_map/ppermute | solution.py:661
  62.1 9.8 %collective-permute-start.4 = (f32[1024,128]{1,0:T(8,128)S(1)}, f32[1024,128]{1,0:T(8,128)S(1)}, u32[]{:S(2)}, u32[]{:S(2)}) collective-permute-start(f32[1024,128]{1,0:T(8,128)S(1)} %get-tuple-element.74.after), channel_id=1, source_target_pairs={{0,16},{16,0},{32,48},{48,32},{64,80},{80,64},{96,112},{112,96},{1... | collective-permute-start | bytes 1572872 | tf_op jit(solution)/shard_map/ppermute | solution.py:661
  72.4 7.8 %collective-permute-start.7 = (f32[160,128]{1,0:T(8,128)S(1)}, f32[160,128]{1,0:T(8,128)S(1)}, u32[]{:S(2)}, u32[]{:S(2)}) collective-permute-start(f32[160,128]{1,0:T(8,128)S(1)} %get-tuple-element.95), channel_id=1, source_target_pairs={{0,15},{1,2},{2,1},{3,4},{4,3},{5,6},{6,5},{7,8},{8,7},{9,10},{10,... | collective-permute-start | bytes 245768 | tf_op jit(solution)/shard_map/ppermute | solution.py:661
  74.1 6.2 %collective-permute-start.6 = (f32[160,128]{1,0:T(8,128)S(1)}, f32[160,128]{1,0:T(8,128)S(1)}, u32[]{:S(2)}, u32[]{:S(2)}) collective-permute-start(f32[160,128]{1,0:T(8,128)S(1)} %get-tuple-element.86.refs_9_), channel_id=1, source_target_pairs={{0,1},{1,0},{2,3},{3,2},{4,5},{5,4},{6,7},{7,6},{8,9},{9,8},{10,11... | collective-permute-start | bytes 245768 | tf_op jit(solution)/shard_map/ppermute | solution.py:661
  83.7 1.3 %collective-permute-start.8 = (f32[72,128]{1,0:T(8,128)S(1)}, f32[72,128]{1,0:T(8,128)S(1)}, u32[]{:S(2)}, u32[]{:S(2)}) collective-permute-start(f32[72,128]{1,0:T(8,128)S(1)} %get-tuple-element.97), channel_id=1, source_target_pairs={{0,16},{16,0},{32,48},{48,32},{64,80},{80,64},{96,112},{112,96},{1... | collective-permute-start | bytes 110600 | tf_op jit(solution)/shard_map/ppermute | solution.py:725
  85.0 5.5 %collective-permute-start.11 = (f32[72,128]{1,0:T(8,128)S(1)}, f32[72,128]{1,0:T(8,128)S(1)}, u32[]{:S(2)}, u32[]{:S(2)}) collective-permute-start(f32[72,128]{1,0:T(8,128)S(1)} %add.30.after), channel_id=1, source_target_pairs={{0,96},{16,112},{32,64},{48,80},{64,32},{80,48},{96,0},{112,16},{1... | collective-permute-start | bytes 110600 | tf_op jit(solution)/shard_map/ppermute | solution.py:725
  85.8 5.8 %collective-permute-start.10 = (f32[72,128]{1,0:T(8,128)S(1)}, f32[72,128]{1,0:T(8,128)S(1)}, u32[]{:S(2)}, u32[]{:S(2)}) collective-permute-start(f32[72,128]{1,0:T(8,128)S(1)} %add.30.after), channel_id=1, source_target_pairs={{0,64},{16,80},{32,96},{48,112},{64,0},{80,16},{96,32},{112,48},{1... | collective-permute-start | bytes 110600 | tf_op jit(solution)/shard_map/ppermute | solution.py:725
  87.2 4.3 %collective-permute-start.9 = (f32[72,128]{1,0:T(8,128)S(1)}, f32[72,128]{1,0:T(8,128)S(1)}, u32[]{:S(2)}, u32[]{:S(2)}) collective-permute-start(f32[72,128]{1,0:T(8,128)S(1)} %add.30.after), channel_id=1, source_target_pairs={{0,32},{16,48},{32,0},{48,16},{64,96},{80,112},{96,64},{112,80},{1... | collective-permute-start | bytes 110600 | tf_op jit(solution)/shard_map/ppermute | solution.py:725
  91.6 5.3 %collective-permute-start.14 = (f32[72,128]{1,0:T(8,128)S(1)}, f32[72,128]{1,0:T(8,128)S(1)}, u32[]{:S(2)}, u32[]{:S(2)}) collective-permute-start(f32[72,128]{1,0:T(8,128)S(1)} %add_add_fusion.1), channel_id=1, source_target_pairs={{0,3},{1,2},{2,1},{3,0},{4,7},{5,6},{6,5},{7,4},{8,11},{9,10},{10,... | collective-permute-start | bytes 110600 | tf_op jit(solution)/shard_map/ppermute | solution.py:725
  91.7 5.5 %collective-permute-start.13 = (f32[72,128]{1,0:T(8,128)S(1)}, f32[72,128]{1,0:T(8,128)S(1)}, u32[]{:S(2)}, u32[]{:S(2)}) collective-permute-start(f32[72,128]{1,0:T(8,128)S(1)} %add_add_fusion.1), channel_id=1, source_target_pairs={{0,2},{1,3},{2,0},{3,1},{4,6},{5,7},{6,4},{7,5},{8,10},{9,11},{10,... | collective-permute-start | bytes 110600 | tf_op jit(solution)/shard_map/ppermute | solution.py:725
  94.3 4.0 %collective-permute-start.12 = (f32[72,128]{1,0:T(8,128)S(1)}, f32[72,128]{1,0:T(8,128)S(1)}, u32[]{:S(2)}, u32[]{:S(2)}) collective-permute-start(f32[72,128]{1,0:T(8,128)S(1)} %add_add_fusion.1), channel_id=1, source_target_pairs={{0,1},{1,0},{2,3},{3,2},{4,5},{5,4},{6,7},{7,6},{8,9},{9,8},{10,11... | collective-permute-start | bytes 110600 | tf_op jit(solution)/shard_map/ppermute | solution.py:725
  98.3 6.3 %collective-permute-start.17 = (f32[72,128]{1,0:T(8,128)S(1)}, f32[72,128]{1,0:T(8,128)S(1)}, u32[]{:S(2)}, u32[]{:S(2)}) collective-permute-start(f32[72,128]{1,0:T(8,128)S(1)} %add_add_fusion.x_ref), channel_id=1, source_target_pairs={{0,12},{1,13},{2,14},{3,15},{4,8},{5,9},{6,10},{7,11},{8,4},{9,5},... | collective-permute-start | bytes 110600 | tf_op jit(solution)/shard_map/ppermute | solution.py:725
  100.1 5.5 %collective-permute-start.16 = (f32[72,128]{1,0:T(8,128)S(1)}, f32[72,128]{1,0:T(8,128)S(1)}, u32[]{:S(2)}, u32[]{:S(2)}) collective-permute-start(f32[72,128]{1,0:T(8,128)S(1)} %add_add_fusion.x_ref), channel_id=1, source_target_pairs={{0,8},{1,9},{2,10},{3,11},{4,12},{5,13},{6,14},{7,15},{8,0},{9,1},... | collective-permute-start | bytes 110600 | tf_op jit(solution)/shard_map/ppermute | solution.py:725
  101.5 4.1 %collective-permute-start.15 = (f32[72,128]{1,0:T(8,128)S(1)}, f32[72,128]{1,0:T(8,128)S(1)}, u32[]{:S(2)}, u32[]{:S(2)}) collective-permute-start(f32[72,128]{1,0:T(8,128)S(1)} %add_add_fusion.x_ref), channel_id=1, source_target_pairs={{0,4},{1,5},{2,6},{3,7},{4,0},{5,1},{6,2},{7,3},{8,12},{9,13},{10,... | collective-permute-start | bytes 110600 | tf_op jit(solution)/shard_map/ppermute | solution.py:725

commit v7 on v6

--- a/solution.py
+++ b/solution.py
@@ -115,7 +115,7 @@
     )(in_hbm(counts), in_hbm(kappa), in_hbm(probes))
 
 
-def turn_kernel(flags, kappa_ref, p_hbm, ext, own_a, own_b, chunk, sems):
+def turn_kernel(flags, p_hbm, ext, own_a, own_b, chunk, sems):
     def copy(n):
         half, block = n // 4, n % 4
         return pltpu.make_async_copy(
@@ -133,53 +133,54 @@
     odd = flags[2]
     for own, low in ((own_a, odd), (own_b, 1 - odd)):
         col = jnp.where(low == 1, 0, C - H)
-        lane = pl.multiple_of(jnp.where(low == 1, 0, LANES), LANES)
         for r in range(R):
             own[r * H:(r + 1) * H, :] = ext[pl.ds(at(r + H, 8) + col, H), :]
-        own[R * H:, :] = kappa_ref[:, pl.ds(lane, LANES)]
-
-
-def turn(flags, kappa, probes):
+
+
+def turn(flags, probes):
     return pl.pallas_call(
         turn_kernel,
-        in_specs=[smem_spec(), vmem_spec(), hbm_spec()],
+        in_specs=[smem_spec(), hbm_spec()],
         out_specs=[vmem_spec()] * 3,
-        out_shape=[held(NROW + 16, K), held(OWN_ROWS, K), held(OWN_ROWS, K)],
+        out_shape=[held(NROW + 16, K), held(R * H, K), held(R * H, K)],
         scratch_shapes=[pltpu.VMEM((8, K, 8, LANES), jnp.float32), pltpu.SemaphoreType.DMA((8,))],
         compiler_params=pltpu.CompilerParams(vmem_limit_bytes=6 * 1024 * 1024),
         cost_estimate=pl.CostEstimate(flops=0, bytes_accessed=12 * 1024 * 1024, transcendentals=0),
         name="turn",
-    )(flags, kappa, in_hbm(probes))
-
-
-def corner_kernel(flags, own_a, own_b, lat_a, lat_b, after, pay_a, pay_b):
+    )(flags, in_hbm(probes))
+
+
+def corner_kernel(flags, own_a, own_b, lat_a, lat_b, after, *rest):
+    *kappa, pay_a, pay_b = rest
     odd = flags[2]
-    own_rows = own_a.shape[0]
     for own, pay, low in ((own_a, pay_a, odd), (own_b, pay_b, 1 - odd)):
         col = jnp.where(low == 1, 0, C - H)
-        pay[:own_rows, :] = own[...]
-        base = own_rows
+        pay[:R * H, :] = own[...]
+        base = R * H
+        if kappa:
+            pay[base:base + R, :] = jnp.where(low == 1, kappa[0][:, :LANES], kappa[0][:, LANES:])
+            base += R
         for lat in (lat_a, lat_b):
             for r in range(H):
                 pay[base:base + H, :] = lat[pl.ds(r * C + col, H), :]
                 base += H
-        if own_rows > R * H:
+        if kappa:
             for lat in (lat_a, lat_b):
                 for r in range(H):
                     pay[base:base + 1, :] = lat[pl.ds(H * C + 2 * r + 1 - low, 1), :]
                     base += 1
 
 
-def corner(flags, own_a, own_b, lat_a, lat_b, after):
-    rows = own_a.shape[0] + 2 * H * H + (2 * H if own_a.shape[0] > R * H else 0)
+def corner(flags, own_a, own_b, lat_a, lat_b, after, *kappa):
+    rows = R * H + 2 * H * H + (R + 2 * H if kappa else 0)
     return pl.pallas_call(
         corner_kernel,
-        in_specs=[smem_spec()] + [vmem_spec()] * 4 + [pl.BlockSpec(memory_space=pl.ANY)],
+        in_specs=[smem_spec()] + [vmem_spec()] * 4 + [pl.BlockSpec(memory_space=pl.ANY)] + [vmem_spec()] * len(kappa),
         out_specs=[vmem_spec()] * 2,
         out_shape=[f32(rows, K)] * 2,
         compiler_params=pltpu.CompilerParams(vmem_limit_bytes=2 * 1024 * 1024),
         name="corner",
-    )(flags, *in_vmem(own_a, own_b), lat_a, lat_b, after)
+    )(flags, *in_vmem(own_a, own_b), lat_a, lat_b, after, *kappa)
 
 
 def keep(ok, x):
@@ -674,14 +675,17 @@
     col = lax.broadcasted_iota(jnp.int32, (8, K), 1)
     wide = lambda x: jnp.broadcast_to(x, (8, K))
     panels, last = [], None
+    following = a_ref[0:8, :]
     for q in range(K // 8):
         c = 8 * q
-        panel = a_ref[c:c + 8, :]
-        if q > 1:
-            done = jnp.concatenate(panels[:q - 1], axis=0)
-            panel = panel - lax.dot_general(
-                done[:, c:c + 8], done, (((0,), (0,)), ((), ())),
-                precision=lax.Precision.HIGHEST, preferred_element_type=jnp.float32)
+        panel = following
+        if q + 1 < K // 8:
+            following = a_ref[c + 8:c + 16, :]
+            if q > 0:
+                done = jnp.concatenate(panels, axis=0)
+                following = following - lax.dot_general(
+                    done[:, c + 8:c + 16], done, (((0,), (0,)), ((), ())),
+                    precision=lax.Precision.HIGHEST, preferred_element_type=jnp.float32)
         b = {(i, m): wide(panel[i:i + 1, c + m:c + m + 1]) for i in range(8) for m in range(i, 8)}
         rows = [wide(panel[i:i + 1, :]) for i in range(8)]
         if q > 0:
@@ -743,11 +747,11 @@
         lon % 2, ((lon > 0) & (lon < n_lon - 1)).astype(jnp.int32),
     ]).astype(jnp.int32)
     lat_a, lat_b = swap(*edge_pack(sweep_counts, kappa, probes), "lat")
-    ext, own_a, own_b = turn(flags, kappa, probes)
+    ext, own_a, own_b = turn(flags, probes)
     kap, act = coeffs(flags, sweep_counts, kappa, own_a)
     levels = inner(ext, kap, act)
     count = obs_count.reshape(1)
-    lon_pay = corner(flags, own_a, own_b, lat_a, lat_b, levels[-1])
+    lon_pay = corner(flags, own_a, own_b, lat_a, lat_b, levels[-1], kappa)
     cell, place = places(count, obs_cell.reshape(1, SLOTS), obs_owner.reshape(1, SLOTS), lon_pay[0])
     tail_a, tail_b, ext, levels, kap, act = ends(flags, ext, levels, kap, act, (lat_a, lat_b), lon_pay[0])
     lon_a, lon_b = swap(*lon_pay, "lon")

time: 112 us -> 111 us (level)
  transfers between devices with their start and end apart: 18 -> 18, of which waited for: 10 -> 11; matrix products, arithmetic and copies ran while one was open for 0% -> 0% of each run, Pallas kernels for 24% -> 24%
where the time goes in v7:
time: 111 us; the launch traced here: 110 us
  Pallas kernels  46.2 us (42%)
  blocking collectives  26.3 us (24%)
  starting transfers between devices  24.4 us (22%)
  waiting for transfers between devices  11.9 us (11%)
  between operations  1.54 us (1%)
    all_to_all x1, blocking collectives, shards(): lax.all_to_all(outgoing, 'lon', split_axis=0, concat_axis=0, tiled=True)  13.6 us
    all_to_all x1, blocking collectives, shards(): lax.all_to_all(mixed, 'lon', split_axis=0, concat_axis=0, tiled=True)  12.6 us
    ppermute x10, starting transfers between devices, stage(): lax.ppermute(x, axis, [(i, i ^ d) for i in range(size)])  12.5 us
    ppermute x4, starting transfers between devices, swap(): lax.ppermute(b, axis, pairs(size, 1))  10.8 us
    pallas_call x2, Pallas kernels, inner(): pl.pallas_call(inner_kernel, in_specs=[vmem_spec()] * 3, out_specs=[vmem_...  9.85 us
    ppermute x10, waiting for transfers between devices, stage(): lax.ppermute(x, axis, [(i, i ^ d) for i in range(size)])  7.09 us
    pallas_call x1, Pallas kernels, factor(): pl.pallas_call(functools.partial(factor_kernel, scale), in_specs=[vmem_sp...  5.43 us
    pallas_call x1, Pallas kernels, bulk(): pl.pallas_call(bulk_kernel, in_specs=[smem_spec()] + [vmem_spec()] * 9 +...  4.67 us
  transfers between devices with their start and end apart: 18, of which 11 were waited for; matrix products, arithmetic and copies ran while one was open for 0% of the time, Pallas kernels for 24%

profile of v7, /device:TPU:0, one launch (start us, length us, event | category | flops | bytes accessed | tf_op | source)
XLA Modules:
  0.0 110.5 jit_solution(16427727974955283007)
XLA Ops:
  0.6 1.8 %edge_pack.1 = (f32[1040,128]{1,0:T(8,128)S(1)}, f32[1040,128]{1,0:T(8,128)S(1)}) custom-call(s32[32]{0:T(128)} %counts.3, f32[32,256]{1,0:T(8,128)} %kappa_ref.3, f32[128,32,256]{2,1,0:T(8,128)} %refs_10_.1), custom_call_target="tpu_custom_call" | custom-call | tf_op jit(solution)/shard_map/edge_pack/pallas_call | solution.py:102
  2.5 3.2 %collective-permute-start.1 = (f32[1040,128]{1,0:T(8,128)S(1)}, f32[1040,128]{1,0:T(8,128)S(1)}, u32[]{:S(2)}, u32[]{:S(2)}) collective-permute-start(f32[1040,128]{1,0:T(8,128)S(1)} %get-tuple-element.53), channel_id=1, source_target_pairs={{0,112},{16,32},{32,16},{48,64},{64,48},{80,96},{96,80},{112,0},{1... | collective-permute-start | bytes 1597448 | tf_op jit(solution)/shard_map/ppermute | solution.py:662
  5.8 3.3 %turn.1 = (f32[10896,128]{1,0:T(8,128)S(1)}, f32[128,128]{1,0:T(8,128)S(1)}, f32[128,128]{1,0:T(8,128)S(1)}) custom-call(s32[4]{0:T(128)S(1)} %pad_add_fusion.flags, f32[128,32,256]{2,1,0:T(8,128)} %refs_10_.1), custom_call_target="tpu_custom_call" | custom-call | bytes 12582912 | tf_op jit(solution)/shard_map/turn/pallas_call | solution.py:141
  9.1 1.8 %coeffs.2 = (f32[10896,128]{1,0:T(8,128)S(1)}, f32[4,40,8,128]{3,2,1,0:T(8,128)S(1)}) custom-call(s32[4]{0:T(128)S(1)} %pad_add_fusion.flags, s32[32]{0:T(128)S(1)} %copy-done.1, f32[32,256]{1,0:T(8,128)S(1)} %copy-done, f32[128,128]{1,0:T(8,128)S(1)} %get-tuple-element.50.after.own_a), custom_call_target="tpu_custom_call" | custom-call | bytes 4194304 | tf_op jit(solution)/shard_map/coeffs/pallas_call | solution.py:375
  10.9 5.1 %inner.2 = (f32[10896,128]{1,0:T(8,128)S(1)}, f32[10896,128]{1,0:T(8,128)S(1)}, f32[10896,128]{1,0:T(8,128)S(1)}, f32[10896,128]{1,0:T(8,128)S(1)}) custom-call(f32[10896,128]{1,0:T(8,128)S(1)} %get-tuple-element.54.ext.refs_0_, f32[10896,128]{1,0:T(8,128)S(1)} %get-tuple-element.55.kap.refs_5_, f32[4,40,8,128]{3,2,1,0:T(8,128)S(1)} %get-tuple-element.56.act.refs_6_), custom_call_target="tpu_custom_call" | custom-call | bytes 16777216 | tf_op jit(solution)/shard_map/inner/pallas_call | solution.py:308
  16.6 6.3 %collective-permute-start.3 = (f32[200,128]{1,0:T(8,128)S(1)}, f32[200,128]{1,0:T(8,128)S(1)}, u32[]{:S(2)}, u32[]{:S(2)}) collective-permute-start(f32[200,128]{1,0:T(8,128)S(1)} %get-tuple-element.71), channel_id=1, source_target_pairs={{0,15},{1,2},{2,1},{3,4},{4,3},{5,6},{6,5},{7,8},{8,7},{9,10},{10,... | collective-permute-start | bytes 307208 | tf_op jit(solution)/shard_map/ppermute | solution.py:662
  23.9 2.4 %ends.1 = (f32[16,128]{1,0:T(8,128)S(1)}, f32[16,128]{1,0:T(8,128)S(1)}, f32[10896,128]{1,0:T(8,128)S(1)}, f32[10896,128]{1,0:T(8,128)S(1)}, f32[10896,128]{1,0:...) custom-call(s32[4]{0:T(128)S(1)} %pad_add_fusion.flags, ...), custom_call_target="tpu_custom_call", output_to_operand_aliasing={{2}: (1, {}), {3}: (2, {}), {4}: (3, {}), {5}: (4, {}), {6}... | custom-call | bytes 8388608 | tf_op jit(solution)/shard_map/ends/pallas_call | solution.py:353
  27.6 2.5 %smooth.1 = (f32[768,128]{1,0:T(8,128)S(1)}, f32[10896,128]{1,0:T(8,128)S(1)}, f32[10896,128]{1,0:T(8,128)S(1)}, f32[10896,128]{1,0:T(8,128)S(1)}, f32[10896,128...) custom-call(s32[4]{0:T(128)S(1)} %pad_add_fusion.flags, ...), custom_call_target="tpu_custom_call", output_to_operand_aliasing={{1}: (3, {}), {2}: (4, {}), {3}: (5, {}), {4}: (6, {}), {5}... | custom-call | tf_op jit(solution)/shard_map/smooth/pallas_call | solution.py:432
  30.1 13.6 %all_to_all.22 = f32[16,48,128]{2,1,0:T(8,128)S(1)} all-to-all(f32[16,48,128]{2,1,0:T(8,128)S(1)} %bitcast.16), channel_id=1, replica_groups=mesh['lat'=8,'lon'=16] {'lon'}, dimensions={0} | all-to-all | bytes 786432 | tf_op jit(solution)/shard_map/all_to_all | solution.py:759
  43.7 2.7 %weigh.1 = f32[768,128]{1,0:T(8,128)S(1)} custom-call(f32[768,128]{1,0:T(8,128)S(1)} %bitcast.14, f32[768,768]{1,0:T(8,128)} %bitcast.18), custom_call_target="tpu_custom_call" | custom-call | tf_op jit(solution)/shard_map/weigh/pallas_call | solution.py:467
  46.5 12.6 %all_to_all.23 = f32[16,48,128]{2,1,0:T(8,128)S(1)} all-to-all(f32[16,48,128]{2,1,0:T(8,128)S(1)} %bitcast.15), channel_id=1, replica_groups=mesh['lat'=8,'lon'=16] {'lon'}, dimensions={0} | all-to-all | bytes 786432 | tf_op jit(solution)/shard_map/all_to_all | solution.py:761
  59.1 2.4 %spread.1 = (f32[10896,128]{1,0:T(8,128)S(1)}, f32[1024,128]{1,0:T(8,128)S(1)}, f32[1024,128]{1,0:T(8,128)S(1)}, f32[128,128]{1,0:T(8,128)S(1)}, f32[128,128]{1,0:T(8,128)S(1)}) custom-call(s32[4]{0:T(128)S(1)} %pad_add_fusion.flags, s32[1,384]{1,0:T(1,128)S(1)} %get-tuple-element.59.cell_ref, s32[1,384]{1,0:T(1,128)S(1)} %get-tuple-element.60.place_ref, ...), custom_call_target="tpu_custom_call" | custom-call | tf_op jit(solution)/shard_map/spread/pallas_call | solution.py:512
  62.5 2.4 %coeffs.3 = (f32[10896,128]{1,0:T(8,128)S(1)}, f32[4,40,8,128]{3,2,1,0:T(8,128)S(1)}) custom-call(s32[4]{0:T(128)S(1)} %pad_add_fusion.flags, s32[32]{0:T(128)S(1)} %copy-done.1, f32[32,256]{1,0:T(8,128)S(1)} %copy-done, f32[1024,128]{1,0:T(8,128)S(1)} %get-tuple-element.74.after, f32[16,128]{1,0:T(8,128)S(1)} %get-tuple-element.75.rest_0_, ...), custom_call_target="tpu_custom_call" | custom-call | bytes 4194304 | tf_op jit(solution)/shard_map/coeffs/pallas_call | solution.py:375
  65.0 4.8 %inner.3 = (f32[10896,128]{1,0:T(8,128)S(1)}, f32[10896,128]{1,0:T(8,128)S(1)}, f32[10896,128]{1,0:T(8,128)S(1)}, f32[10896,128]{1,0:T(8,128)S(1)}) custom-call(f32[10896,128]{1,0:T(8,128)S(1)} %get-tuple-element.73.ext.refs_0_, f32[10896,128]{1,0:T(8,128)S(1)} %get-tuple-element.77.kap.refs_5_, f32[4,40,8,128]{3,2,1,0:T(8,128)S(1)} %get-tuple-element.78.act.refs_6_), custom_call_target="tpu_custom_call" | custom-call | bytes 16777216 | tf_op jit(solution)/shard_map/inner/pallas_call | solution.py:308
  69.7 1.7 %collective-permute-done.5.lat_b.refs_8_ = f32[1024,128]{1,0:T(8,128)S(1)} collective-permute-done((f32[1024,128]{1,0:T(8,128)S(1)}, f32[1024,128]{1,0:T(8,128)S(1)}, u32[]{:S(2)}, u32[]{:S(2)}) %collective-permute-start.5) | collective-permute-done | bytes 524320 | tf_op jit(solution)/shard_map/ppermute | solution.py:662
  73.3 4.7 %bulk.1 = (f32[10896,128]{1,0:T(8,128)S(1)}, f32[10896,128]{1,0:T(8,128)S(1)}, f32[10896,128]{1,0:T(8,128)S(1)}, f32[10896,128]{1,0:T(8,128)S(1)}, f32[10896,128...) custom-call(s32[4]{0:T(128)S(1)} %pad_add_fusion.flags, ...), custom_call_target="tpu_custom_call", output_to_operand_aliasing={{0}: (1, {}), {1}: (2, {}), {2}: (3, {}), {3}: (4, {}), {4}... | custom-call | bytes 16777216 | tf_op jit(solution)/shard_map/bulk/pallas_call | solution.py:570
  77.9 1.9 %collective-permute-done.7.refs_11_ = f32[160,128]{1,0:T(8,128)S(1)} collective-permute-done((f32[160,128]{1,0:T(8,128)S(1)}, f32[160,128]{1,0:T(8,128)S(1)}, u32[]{:S(2)}, u32[]{:S(2)}) %collective-permute-start.7) | collective-permute-done | bytes 81952 | tf_op jit(solution)/shard_map/ppermute | solution.py:662
  79.8 3.5 %finish.1 = (f32[72,128]{1,0:T(8,128)S(1)}, f32[10896,128]{1,0:T(8,128)S(1)}, f32[10896,128]{1,0:T(8,128)S(1)}, f32[10896,128]{1,0:T(8,128)S(1)}, f32[10896,128]...) custom-call(s32[4]{0:T(128)S(1)} %pad_add_fusion.flags, ...), custom_call_target="tpu_custom_call", output_to_operand_aliasing={{1}: (1, {}), {2}: (2, {}), {3}: (3, {}), {4}: (4, {}), {5}... | custom-call | tf_op jit(solution)/shard_map/finish/pallas_call | solution.py:623
  86.6 2.1 %collective-permute-start.9 = (f32[72,128]{1,0:T(8,128)S(1)}, f32[72,128]{1,0:T(8,128)S(1)}, u32[]{:S(2)}, u32[]{:S(2)}) collective-permute-start(f32[72,128]{1,0:T(8,128)S(1)} %add.30.after), channel_id=1, source_target_pairs={{0,32},{16,48},{32,0},{48,16},{64,96},{80,112},{96,64},{112,80},{1... | collective-permute-start | bytes 110600 | tf_op jit(solution)/shard_map/ppermute | solution.py:729
  91.1 2.2 %collective-permute-start.13 = (f32[72,128]{1,0:T(8,128)S(1)}, f32[72,128]{1,0:T(8,128)S(1)}, u32[]{:S(2)}, u32[]{:S(2)}) collective-permute-start(f32[72,128]{1,0:T(8,128)S(1)} %add_add_fusion.1), channel_id=1, source_target_pairs={{0,2},{1,3},{2,0},{3,1},{4,6},{5,7},{6,4},{7,5},{8,10},{9,11},{10,... | collective-permute-start | bytes 110600 | tf_op jit(solution)/shard_map/ppermute | solution.py:729
  93.3 1.9 %collective-permute-start.12 = (f32[72,128]{1,0:T(8,128)S(1)}, f32[72,128]{1,0:T(8,128)S(1)}, u32[]{:S(2)}, u32[]{:S(2)}) collective-permute-start(f32[72,128]{1,0:T(8,128)S(1)} %add_add_fusion.1), channel_id=1, source_target_pairs={{0,1},{1,0},{2,3},{3,2},{4,5},{5,4},{6,7},{7,6},{8,9},{9,8},{10,11... | collective-permute-start | bytes 110600 | tf_op jit(solution)/shard_map/ppermute | solution.py:729
  97.5 2.0 %collective-permute-start.17 = (f32[72,128]{1,0:T(8,128)S(1)}, f32[72,128]{1,0:T(8,128)S(1)}, u32[]{:S(2)}, u32[]{:S(2)}) collective-permute-start(f32[72,128]{1,0:T(8,128)S(1)} %add_add_fusion.x_ref), channel_id=1, source_target_pairs={{0,12},{1,13},{2,14},{3,15},{4,8},{5,9},{6,10},{7,11},{8,4},{9,5},... | collective-permute-start | bytes 110600 | tf_op jit(solution)/shard_map/ppermute | solution.py:729
  101.7 2.1 %store.1 = f32[128,32,256]{2,1,0:T(8,128)} custom-call(f32[8,128,8,128]{3,2,1,0:T(8,128)S(1)} %get-tuple-element.96.chunk, f32[72,128]{1,0:T(8,128)S(1)} %add.30.after), custom_call_target="tpu_custom_call" | custom-call | bytes 8388608 | tf_op jit(solution)/shard_map/store/pallas_call | solution.py:644
  105.0 5.4 %factor.1 = f32[128,128]{1,0:T(8,128)} custom-call(f32[72,128]{1,0:T(8,128)S(1)} %add_add_fusion.x_ref, f32[72,128]{1,0:T(8,128)S(1)} %collective-permute-done.15.g1_ref, f32[72,128]{1,0:T(8,128)S(1)} %collective-permute-done.16.g2_ref, f32[72,128]{1,0:T(8,128)S(1)} %collective-permute-done.17.g3_ref), custom_call_target="tpu_custom_call" | custom-call | tf_op jit(solution)/shard_map/factor/pallas_call | solution.py:715
  (44 shorter events, 16.6 us)
Async XLA Ops:
  0.6 8.5 %copy-start = (f32[32,256]{1,0:T(8,128)S(1)}, f32[32,256]{1,0:T(8,128)}, u32[]{:S(2)}) copy-start(f32[32,256]{1,0:T(8,128)} %kappa_ref.3) | copy-start | bytes 98308
  0.6 8.5 %copy-start.1 = (s32[32]{0:T(128)S(1)}, s32[32]{0:T(128)}, u32[]{:S(2)}) copy-start(s32[32]{0:T(128)} %counts.3) | copy-start | bytes 388
  2.4 13.6 %collective-permute-start = (f32[1040,128]{1,0:T(8,128)S(1)}, f32[1040,128]{1,0:T(8,128)S(1)}, u32[]{:S(2)}, u32[]{:S(2)}) collective-permute-start(f32[1040,128]{1,0:T(8,128)S(1)} %get-tuple-element.52), channel_id=1, source_target_pairs={{0,16},{16,0},{32,48},{48,32},{64,80},{80,64},{96,112},{112,96},{1... | collective-permute-start | bytes 1597448 | tf_op jit(solution)/shard_map/ppermute | solution.py:662
  2.5 13.5 %collective-permute-start.1 = (f32[1040,128]{1,0:T(8,128)S(1)}, f32[1040,128]{1,0:T(8,128)S(1)}, u32[]{:S(2)}, u32[]{:S(2)}) collective-permute-start(f32[1040,128]{1,0:T(8,128)S(1)} %get-tuple-element.53), channel_id=1, source_target_pairs={{0,112},{16,32},{32,16},{48,64},{64,48},{80,96},{96,80},{112,0},{1... | collective-permute-start | bytes 1597448 | tf_op jit(solution)/shard_map/ppermute | solution.py:662
  16.0 7.6 %copy-start.3 = (s32[384]{0:T(512)S(1)}, s32[384]{0:T(512)}, u32[]{:S(2)}) copy-start(s32[384]{0:T(512)} %param.10) | copy-start | bytes 4612
  16.0 7.6 %copy-start.2 = (s32[384,1]{0,1:T(1,128)S(1)}, s32[384,1]{0,1:T(1,128)}, u32[]{:S(2)}) copy-start(s32[384,1]{0,1:T(1,128)} %param.11) | copy-start | bytes 4612
  16.6 9.7 %collective-permute-start.3 = (f32[200,128]{1,0:T(8,128)S(1)}, f32[200,128]{1,0:T(8,128)S(1)}, u32[]{:S(2)}, u32[]{:S(2)}) collective-permute-start(f32[200,128]{1,0:T(8,128)S(1)} %get-tuple-element.71), channel_id=1, source_target_pairs={{0,15},{1,2},{2,1},{3,4},{4,3},{5,6},{6,5},{7,8},{8,7},{9,10},{10,... | collective-permute-start | bytes 307208 | tf_op jit(solution)/shard_map/ppermute | solution.py:662
  23.0 4.7 %collective-permute-start.2 = (f32[200,128]{1,0:T(8,128)S(1)}, f32[200,128]{1,0:T(8,128)S(1)}, u32[]{:S(2)}, u32[]{:S(2)}) collective-permute-start(f32[200,128]{1,0:T(8,128)S(1)} %get-tuple-element.58.after.refs_9_), channel_id=1, source_target_pairs={{0,1},{1,0},{2,3},{3,2},{4,5},{5,4},{6,7},{7,6},{8,9},{9,8},{10,11... | collective-permute-start | bytes 307208 | tf_op jit(solution)/shard_map/ppermute | solution.py:662
  61.5 9.9 %collective-permute-start.5 = (f32[1024,128]{1,0:T(8,128)S(1)}, f32[1024,128]{1,0:T(8,128)S(1)}, u32[]{:S(2)}, u32[]{:S(2)}) collective-permute-start(f32[1024,128]{1,0:T(8,128)S(1)} %get-tuple-element.83), channel_id=1, source_target_pairs={{0,112},{16,32},{32,16},{48,64},{64,48},{80,96},{96,80},{112,0},{1... | collective-permute-start | bytes 1572872 | tf_op jit(solution)/shard_map/ppermute | solution.py:662
  61.6 9.8 %collective-permute-start.4 = (f32[1024,128]{1,0:T(8,128)S(1)}, f32[1024,128]{1,0:T(8,128)S(1)}, u32[]{:S(2)}, u32[]{:S(2)}) collective-permute-start(f32[1024,128]{1,0:T(8,128)S(1)} %get-tuple-element.74.after), channel_id=1, source_target_pairs={{0,16},{16,0},{32,48},{48,32},{64,80},{80,64},{96,112},{112,96},{1... | collective-permute-start | bytes 1572872 | tf_op jit(solution)/shard_map/ppermute | solution.py:662
  72.0 7.8 %collective-permute-start.7 = (f32[160,128]{1,0:T(8,128)S(1)}, f32[160,128]{1,0:T(8,128)S(1)}, u32[]{:S(2)}, u32[]{:S(2)}) collective-permute-start(f32[160,128]{1,0:T(8,128)S(1)} %get-tuple-element.95), channel_id=1, source_target_pairs={{0,15},{1,2},{2,1},{3,4},{4,3},{5,6},{6,5},{7,8},{8,7},{9,10},{10,... | collective-permute-start | bytes 245768 | tf_op jit(solution)/shard_map/ppermute | solution.py:662
  73.1 6.7 %collective-permute-start.6 = (f32[160,128]{1,0:T(8,128)S(1)}, f32[160,128]{1,0:T(8,128)S(1)}, u32[]{:S(2)}, u32[]{:S(2)}) collective-permute-start(f32[160,128]{1,0:T(8,128)S(1)} %get-tuple-element.86.refs_9_), channel_id=1, source_target_pairs={{0,1},{1,0},{2,3},{3,2},{4,5},{5,4},{6,7},{7,6},{8,9},{9,8},{10,11... | collective-permute-start | bytes 245768 | tf_op jit(solution)/shard_map/ppermute | solution.py:662
  83.3 1.3 %collective-permute-start.8 = (f32[72,128]{1,0:T(8,128)S(1)}, f32[72,128]{1,0:T(8,128)S(1)}, u32[]{:S(2)}, u32[]{:S(2)}) collective-permute-start(f32[72,128]{1,0:T(8,128)S(1)} %get-tuple-element.97), channel_id=1, source_target_pairs={{0,16},{16,0},{32,48},{48,32},{64,80},{80,64},{96,112},{112,96},{1... | collective-permute-start | bytes 110600 | tf_op jit(solution)/shard_map/ppermute | solution.py:729
  84.6 5.5 %collective-permute-start.11 = (f32[72,128]{1,0:T(8,128)S(1)}, f32[72,128]{1,0:T(8,128)S(1)}, u32[]{:S(2)}, u32[]{:S(2)}) collective-permute-start(f32[72,128]{1,0:T(8,128)S(1)} %add.30.after), channel_id=1, source_target_pairs={{0,96},{16,112},{32,64},{48,80},{64,32},{80,48},{96,0},{112,16},{1... | collective-permute-start | bytes 110600 | tf_op jit(solution)/shard_map/ppermute | solution.py:729
  85.3 5.6 %collective-permute-start.10 = (f32[72,128]{1,0:T(8,128)S(1)}, f32[72,128]{1,0:T(8,128)S(1)}, u32[]{:S(2)}, u32[]{:S(2)}) collective-permute-start(f32[72,128]{1,0:T(8,128)S(1)} %add.30.after), channel_id=1, source_target_pairs={{0,64},{16,80},{32,96},{48,112},{64,0},{80,16},{96,32},{112,48},{1... | collective-permute-start | bytes 110600 | tf_op jit(solution)/shard_map/ppermute | solution.py:729
  86.6 4.4 %collective-permute-start.9 = (f32[72,128]{1,0:T(8,128)S(1)}, f32[72,128]{1,0:T(8,128)S(1)}, u32[]{:S(2)}, u32[]{:S(2)}) collective-permute-start(f32[72,128]{1,0:T(8,128)S(1)} %add.30.after), channel_id=1, source_target_pairs={{0,32},{16,48},{32,0},{48,16},{64,96},{80,112},{96,64},{112,80},{1... | collective-permute-start | bytes 110600 | tf_op jit(solution)/shard_map/ppermute | solution.py:729
  91.0 5.3 %collective-permute-start.14 = (f32[72,128]{1,0:T(8,128)S(1)}, f32[72,128]{1,0:T(8,128)S(1)}, u32[]{:S(2)}, u32[]{:S(2)}) collective-permute-start(f32[72,128]{1,0:T(8,128)S(1)} %add_add_fusion.1), channel_id=1, source_target_pairs={{0,3},{1,2},{2,1},{3,0},{4,7},{5,6},{6,5},{7,4},{8,11},{9,10},{10,... | collective-permute-start | bytes 110600 | tf_op jit(solution)/shard_map/ppermute | solution.py:729
  91.1 5.5 %collective-permute-start.13 = (f32[72,128]{1,0:T(8,128)S(1)}, f32[72,128]{1,0:T(8,128)S(1)}, u32[]{:S(2)}, u32[]{:S(2)}) collective-permute-start(f32[72,128]{1,0:T(8,128)S(1)} %add_add_fusion.1), channel_id=1, source_target_pairs={{0,2},{1,3},{2,0},{3,1},{4,6},{5,7},{6,4},{7,5},{8,10},{9,11},{10,... | collective-permute-start | bytes 110600 | tf_op jit(solution)/shard_map/ppermute | solution.py:729
  93.3 4.2 %collective-permute-start.12 = (f32[72,128]{1,0:T(8,128)S(1)}, f32[72,128]{1,0:T(8,128)S(1)}, u32[]{:S(2)}, u32[]{:S(2)}) collective-permute-start(f32[72,128]{1,0:T(8,128)S(1)} %add_add_fusion.1), channel_id=1, source_target_pairs={{0,1},{1,0},{2,3},{3,2},{4,5},{5,4},{6,7},{7,6},{8,9},{9,8},{10,11... | collective-permute-start | bytes 110600 | tf_op jit(solution)/shard_map/ppermute | solution.py:729
  97.5 6.3 %collective-permute-start.17 = (f32[72,128]{1,0:T(8,128)S(1)}, f32[72,128]{1,0:T(8,128)S(1)}, u32[]{:S(2)}, u32[]{:S(2)}) collective-permute-start(f32[72,128]{1,0:T(8,128)S(1)} %add_add_fusion.x_ref), channel_id=1, source_target_pairs={{0,12},{1,13},{2,14},{3,15},{4,8},{5,9},{6,10},{7,11},{8,4},{9,5},... | collective-permute-start | bytes 110600 | tf_op jit(solution)/shard_map/ppermute | solution.py:729
  99.6 5.5 %collective-permute-start.16 = (f32[72,128]{1,0:T(8,128)S(1)}, f32[72,128]{1,0:T(8,128)S(1)}, u32[]{:S(2)}, u32[]{:S(2)}) collective-permute-start(f32[72,128]{1,0:T(8,128)S(1)} %add_add_fusion.x_ref), channel_id=1, source_target_pairs={{0,8},{1,9},{2,10},{3,11},{4,12},{5,13},{6,14},{7,15},{8,0},{9,1},... | collective-permute-start | bytes 110600 | tf_op jit(solution)/shard_map/ppermute | solution.py:729
  100.7 4.3 %collective-permute-start.15 = (f32[72,128]{1,0:T(8,128)S(1)}, f32[72,128]{1,0:T(8,128)S(1)}, u32[]{:S(2)}, u32[]{:S(2)}) collective-permute-start(f32[72,128]{1,0:T(8,128)S(1)} %add_add_fusion.x_ref), channel_id=1, source_target_pairs={{0,4},{1,5},{2,6},{3,7},{4,0},{5,1},{6,2},{7,3},{8,12},{9,13},{10,... | collective-permute-start | bytes 110600 | tf_op jit(solution)/shard_map/ppermute | solution.py:729
